TPU v7x, 32 devices: a whole 2x2x4 slice. The times are simulated.
32 devices in a mesh: lat: 4 (over z), lon: 8 (over y, x, core).
Axes of the slice: x: 2, y: 2, z: 4, core: 2. Of those that a mesh axis runs over, the one named last changes fastest.
Arguments:
- wind_u: float32 [8, 256, 12000], P(None, 'lat', 'lon'), may hold values from -6 to 6
- wind_v: float32 [8, 256, 12000], P(None, 'lat', 'lon'), may hold values from -6 to 6
- tracer: float32 [8, 256, 12000], P(None, 'lat', 'lon'), may hold values from -6 to 6
- cutoff: int32 [256], P('lat'), may hold values from 1 to 1024, as said below
- row_scale: float32 [256], P('lat'), may hold values from 1 to 10
Outputs:
- tracer_next: float32 [8, 256, 12000], P(None, 'lat', 'lon')
- divergence: float32 [8, 256, 12000], P(None, 'lat', 'lon')
- vorticity: float32 [8, 256, 12000], P(None, 'lat', 'lon')
Inputs may be any that keep to these rules, and one draw needn't show every extreme that they name: cutoff of row r is min(1024, 1024 * (r + 1) // 256 + j) with a whole j from 0 to 63 drawn per row, and at least 1; the last row's is 1024.
All inputs are finite; a program needn't handle non-finite values.
Results may differ from a plain program's by a relative error of at most 0.00014.
Values sent between devices are 32-bit elements; how exact they have to be, the bound alone decides.
No kernel may reach another device: no remote copies, remote signals or barrier semaphores. Data moves between devices by JAX's collectives and lax.ppermute only.
A program may use at most 128 MiB of HBM per device.

v0:
```python
import math

import jax
import jax.numpy as jnp
from jax import lax
from jax.sharding import PartitionSpec as P

NLON = 12000
KMAX = 1024
BLOCK = 128


courant = 0.5


def padded(cells, sides, width, closed):
    for axis, dim in sides:
        count = lax.axis_size(axis)
        ends = count if closed else count - 1
        head = lax.slice_in_dim(cells, 0, width, axis=dim)
        tail = lax.slice_in_dim(cells, cells.shape[dim] - width, cells.shape[dim], axis=dim)
        cells = jnp.concatenate(
            [
                lax.ppermute(tail, axis, [(i, (i + 1) % count) for i in range(ends)]),
                cells,
                lax.ppermute(head, axis, [((i + 1) % count, i) for i in range(ends)]),
            ],
            axis=dim,
        )
    return cells


def phase_tables(offset, count, first):
    positions = offset + jnp.arange(count, dtype=jnp.int32)
    numbers = first + jnp.arange(BLOCK, dtype=jnp.int32)
    turns = positions[:, None] * numbers[None, :] % NLON
    angles = turns.astype(jnp.float32) * (2.0 * math.pi / NLON)
    return (jnp.cos(angles), jnp.sin(angles))


def block_weights(limits, first):
    numbers = first + jnp.arange(BLOCK, dtype=jnp.int32)
    factor = jnp.where(numbers == 0, 1.0, 2.0).astype(jnp.float32) / NLON
    return jnp.where(numbers[None, :] < limits[:, None], factor[None, :], jnp.float32(0.0))


def contract_rows(coeffs, table):
    return lax.dot_general(
        coeffs,
        table,
        (((1,), (1,)), ((), ())),
        precision=lax.Precision.HIGHEST,
        preferred_element_type=jnp.float32,
    )


def analyse(lines, offset, blocks):
    count = lines.shape[1]
    empty = jnp.zeros((lines.shape[0], KMAX), jnp.float32)

    def analyse_step(index, carry):
        cosine, sine_part = carry
        first = index * BLOCK
        table_c, table_s = phase_tables(offset, count, first)
        part_c = jnp.dot(
            lines, table_c, precision=lax.Precision.HIGHEST, preferred_element_type=jnp.float32
        )
        part_s = jnp.dot(
            lines, table_s, precision=lax.Precision.HIGHEST, preferred_element_type=jnp.float32
        )
        return (
            lax.dynamic_update_slice_in_dim(cosine, part_c, first, 1),
            lax.dynamic_update_slice_in_dim(sine_part, part_s, first, 1),
        )

    return lax.fori_loop(0, blocks, analyse_step, (empty, empty))


def synthesise(cosine, sine_part, limits, offset, count, blocks):
    empty = jnp.zeros((cosine.shape[0], count), jnp.float32)

    def synthesise_step(index, carry):
        first = index * BLOCK
        table_c, table_s = phase_tables(offset, count, first)
        weights = block_weights(limits, first)
        coef_c = lax.dynamic_slice_in_dim(cosine, first, BLOCK, 1) * weights
        coef_s = lax.dynamic_slice_in_dim(sine_part, first, BLOCK, 1) * weights
        values = carry[0] + contract_rows(coef_c, table_c) + contract_rows(coef_s, table_s)
        return (values,)

    start = (empty,)
    return lax.fori_loop(0, blocks, synthesise_step, start)


def on_device(wind_u, wind_v, tracer, cutoff, row_scale):
    levels, rows, width = wind_u.shape
    lines = jnp.stack([wind_u, wind_v, tracer]).reshape(3 * levels * rows, width)
    blocks = (jnp.max(cutoff) + BLOCK - 1) // BLOCK
    limits = jnp.tile(cutoff, 3 * levels)
    offset = lax.axis_index("lon") * width
    cosine, sine_part = analyse(lines, offset, blocks)
    cosine, sine_part = lax.psum((cosine, sine_part), "lon")
    result = synthesise(cosine, sine_part, limits, offset, width, blocks)
    filtered = result[0].reshape(3, levels, rows, width)
    padded_lon = padded(filtered, (("lon", 3),), 1, True)
    lon_change = padded_lon[..., 2:] - padded_lon[..., :-2]
    metric = row_scale[None, :, None]
    weighted = jnp.stack([filtered[0] / metric, filtered[1] / metric, filtered[2]])
    padded_lat = padded(weighted, (("lat", 2),), 1, False)
    lat_change = padded_lat[:, :, 2:] - padded_lat[:, :, :-2]
    divergence = metric * (lon_change[0] + lat_change[1])
    vorticity = metric * (lon_change[1] - lat_change[0])
    tracer_next = tracer - courant * (
        filtered[0] * metric * lon_change[2] + filtered[1] * lat_change[2]
    )
    return (tracer_next, divergence, vorticity)


def solution(mesh):
    in_specs = (
        P(None, "lat", "lon"),
        P(None, "lat", "lon"),
        P(None, "lat", "lon"),
        P("lat"),
        P("lat"),
    )
    out_specs = (P(None, "lat", "lon"), P(None, "lat", "lon"), P(None, "lat", "lon"))
    return jax.shard_map(
        on_device, mesh=mesh, in_specs=in_specs, out_specs=out_specs, check_vma=False
    )
```

profile of v0, /device:TPU:19, one launch (start us, length us, event | category | flops | bytes accessed | tf_op | source)
XLA Modules:
  0.0 778.4 jit_solution(4910263654455271403)
XLA Ops:
  24.7 229.7 %while.27 = (s32[]{:T(128)}, f32[1536,1024]{1,0:T(8,128)}, f32[1536,1024]{1,0:T(8,128)}, s32[]{:T(128)}, s32[]{:T(128)}, /*index=5*/f32[1536,1500]{1,0:T(8,128)}, s32[]{:T(128)}, s32[]{:T(128)}, s32[]{:T(128)}, s32[]{:T(128)}) while((s32[]{:T(128)}, f32[1536,1024]{1,0:T(8,128)}, f32[1536,1024]{1,0:T(8,128)}, s32[]{:T(128)}, s32[]{:T(128)}, ...), condition=%wide.region_2.3_spmd, body=%wide.region_1.2_spmd.sunk | while | flops 7081345536 | bytes 26316016 | solution.py:76
  24.7 15.5 %convolution_bitcast_fusion.4 = f32[1536,128]{0,1:T(8,128)S(1)} fusion(f32[1536,1500]{1,0:T(8,128)} %get-tuple-element.355, s32[128]{0:T(128)S(1)} %iota_add_fusion.8, s32[1500]{0:T(1024)S(1)} %iota_add_fusion.9), kind=kOutput, calls=%fused_computation.1.clone.1 | convolution fusion | flops 3540672000 | bytes 10008944 | tf_op jit(solution)/shard_map/while/body/dot_general | solution.py:68
  40.4 15.5 %convolution_bitcast_fusion.5 = f32[1536,128]{0,1:T(8,128)S(1)} fusion(f32[1536,1500]{1,0:T(8,128)} %get-tuple-element.355, s32[128]{0:T(128)S(1)} %iota_add_fusion.8, s32[1500]{0:T(1024)S(1)} %iota_add_fusion.9), kind=kOutput, calls=%fused_computation.2.clone.1 | convolution fusion | flops 3540672000 | bytes 10008944 | tf_op jit(solution)/shard_map/while/body/dot_general | solution.py:65
  57.5 15.5 %convolution_bitcast_fusion.4 = f32[1536,128]{0,1:T(8,128)S(1)} fusion(f32[1536,1500]{1,0:T(8,128)} %get-tuple-element.355, s32[128]{0:T(128)S(1)} %iota_add_fusion.8, s32[1500]{0:T(1024)S(1)} %iota_add_fusion.9), kind=kOutput, calls=%fused_computation.1.clone.1 | convolution fusion | flops 3540672000 | bytes 10008944 | tf_op jit(solution)/shard_map/while/body/dot_general | solution.py:68
  73.3 15.5 %convolution_bitcast_fusion.5 = f32[1536,128]{0,1:T(8,128)S(1)} fusion(f32[1536,1500]{1,0:T(8,128)} %get-tuple-element.355, s32[128]{0:T(128)S(1)} %iota_add_fusion.8, s32[1500]{0:T(1024)S(1)} %iota_add_fusion.9), kind=kOutput, calls=%fused_computation.2.clone.1 | convolution fusion | flops 3540672000 | bytes 10008944 | tf_op jit(solution)/shard_map/while/body/dot_general | solution.py:65
  90.3 15.5 %convolution_bitcast_fusion.4 = f32[1536,128]{0,1:T(8,128)S(1)} fusion(f32[1536,1500]{1,0:T(8,128)} %get-tuple-element.355, s32[128]{0:T(128)S(1)} %iota_add_fusion.8, s32[1500]{0:T(1024)S(1)} %iota_add_fusion.9), kind=kOutput, calls=%fused_computation.1.clone.1 | convolution fusion | flops 3540672000 | bytes 10008944 | tf_op jit(solution)/shard_map/while/body/dot_general | solution.py:68
  106.1 15.5 %convolution_bitcast_fusion.5 = f32[1536,128]{0,1:T(8,128)S(1)} fusion(f32[1536,1500]{1,0:T(8,128)} %get-tuple-element.355, s32[128]{0:T(128)S(1)} %iota_add_fusion.8, s32[1500]{0:T(1024)S(1)} %iota_add_fusion.9), kind=kOutput, calls=%fused_computation.2.clone.1 | convolution fusion | flops 3540672000 | bytes 10008944 | tf_op jit(solution)/shard_map/while/body/dot_general | solution.py:65
  123.1 15.5 %convolution_bitcast_fusion.4 = f32[1536,128]{0,1:T(8,128)S(1)} fusion(f32[1536,1500]{1,0:T(8,128)} %get-tuple-element.355, s32[128]{0:T(128)S(1)} %iota_add_fusion.8, s32[1500]{0:T(1024)S(1)} %iota_add_fusion.9), kind=kOutput, calls=%fused_computation.1.clone.1 | convolution fusion | flops 3540672000 | bytes 10008944 | tf_op jit(solution)/shard_map/while/body/dot_general | solution.py:68
  138.9 15.5 %convolution_bitcast_fusion.5 = f32[1536,128]{0,1:T(8,128)S(1)} fusion(f32[1536,1500]{1,0:T(8,128)} %get-tuple-element.355, s32[128]{0:T(128)S(1)} %iota_add_fusion.8, s32[1500]{0:T(1024)S(1)} %iota_add_fusion.9), kind=kOutput, calls=%fused_computation.2.clone.1 | convolution fusion | flops 3540672000 | bytes 10008944 | tf_op jit(solution)/shard_map/while/body/dot_general | solution.py:65
  155.9 15.5 %convolution_bitcast_fusion.4 = f32[1536,128]{0,1:T(8,128)S(1)} fusion(f32[1536,1500]{1,0:T(8,128)} %get-tuple-element.355, s32[128]{0:T(128)S(1)} %iota_add_fusion.8, s32[1500]{0:T(1024)S(1)} %iota_add_fusion.9), kind=kOutput, calls=%fused_computation.1.clone.1 | convolution fusion | flops 3540672000 | bytes 10008944 | tf_op jit(solution)/shard_map/while/body/dot_general | solution.py:68
  171.6 15.5 %convolution_bitcast_fusion.5 = f32[1536,128]{0,1:T(8,128)S(1)} fusion(f32[1536,1500]{1,0:T(8,128)} %get-tuple-element.355, s32[128]{0:T(128)S(1)} %iota_add_fusion.8, s32[1500]{0:T(1024)S(1)} %iota_add_fusion.9), kind=kOutput, calls=%fused_computation.2.clone.1 | convolution fusion | flops 3540672000 | bytes 10008944 | tf_op jit(solution)/shard_map/while/body/dot_general | solution.py:65
  188.7 15.5 %convolution_bitcast_fusion.4 = f32[1536,128]{0,1:T(8,128)S(1)} fusion(f32[1536,1500]{1,0:T(8,128)} %get-tuple-element.355, s32[128]{0:T(128)S(1)} %iota_add_fusion.8, s32[1500]{0:T(1024)S(1)} %iota_add_fusion.9), kind=kOutput, calls=%fused_computation.1.clone.1 | convolution fusion | flops 3540672000 | bytes 10008944 | tf_op jit(solution)/shard_map/while/body/dot_general | solution.py:68
  204.4 15.5 %convolution_bitcast_fusion.5 = f32[1536,128]{0,1:T(8,128)S(1)} fusion(f32[1536,1500]{1,0:T(8,128)} %get-tuple-element.355, s32[128]{0:T(128)S(1)} %iota_add_fusion.8, s32[1500]{0:T(1024)S(1)} %iota_add_fusion.9), kind=kOutput, calls=%fused_computation.2.clone.1 | convolution fusion | flops 3540672000 | bytes 10008944 | tf_op jit(solution)/shard_map/while/body/dot_general | solution.py:65
  221.5 15.5 %convolution_bitcast_fusion.4 = f32[1536,128]{0,1:T(8,128)S(1)} fusion(f32[1536,1500]{1,0:T(8,128)} %get-tuple-element.355, s32[128]{0:T(128)S(1)} %iota_add_fusion.8, s32[1500]{0:T(1024)S(1)} %iota_add_fusion.9), kind=kOutput, calls=%fused_computation.1.clone.1 | convolution fusion | flops 3540672000 | bytes 10008944 | tf_op jit(solution)/shard_map/while/body/dot_general | solution.py:68
  237.3 15.5 %convolution_bitcast_fusion.5 = f32[1536,128]{0,1:T(8,128)S(1)} fusion(f32[1536,1500]{1,0:T(8,128)} %get-tuple-element.355, s32[128]{0:T(128)S(1)} %iota_add_fusion.8, s32[1500]{0:T(1024)S(1)} %iota_add_fusion.9), kind=kOutput, calls=%fused_computation.2.clone.1 | convolution fusion | flops 3540672000 | bytes 10008944 | tf_op jit(solution)/shard_map/while/body/dot_general | solution.py:65
  254.4 206.6 %all-reduce.3.cloned.1.call-done = (f32[1536,1024]{1,0:T(8,128)}, f32[1536,1024]{1,0:T(8,128)}) async-done(((f32[1536,1024]{1,0:T(8,128)}, f32[1536,1024]{1,0:T(8,128)}), (f32[1536,1024]{1,0:T(8,128)}, f32[1536,1024]{1,0:T(8,128)})) %all-reduce.3.cloned.1.call-update) | async-done | bytes 12582928 | tf_op jit(solution)/shard_map/psum | solution.py:102
  465.8 216.3 %while.28 = (s32[]{:T(128)}, f32[1536,1500]{0,1:T(8,128)}, s32[]{:T(128)}, f32[1536,1024]{1,0:T(8,128)}, s32[]{:T(128)}, /*index=5*/f32[1536,1024]{1,0:T(8,128)}...) while((s32[]{:T(128)}, f32[1536,1500]{0,1:T(8,128)}, s32[]{:T(128)}, ...), condition=%wide.region_6.7_spmd.clone, body=%wide.region_5.6_spmd.clone.sunk | while | flops 7087133696 | bytes 38547744 | solution.py:92
  480.6 15.4 %convolution_add_fusion.5 = f32[1536,1500]{0,1:T(8,128)} fusion(f32[1536,1500]{0,1:T(8,128)S(1)} %convolution_add_fusion.4, f32[1536,1024]{1,0:T(8,128)} %get-tuple-element.387, s32[]{:T(128)S(6)} %select_n.109, f32[128]{0:T(128)S(1)} %fusion.93, s32[128]{0:T(128)S(1)} %iota_add_fusion.10, s32[1536]{0:T(1024)S(1)} %lt.134, s32[1500]{0:T(1024)S(1)} %iota_add_fusion.11), kind=kOutput, calls=%fused_computation.30.clone.1 | convolution fusion | flops 3543565824 | bytes 19260932 | tf_op jit(solution)/shard_map/while/body/dot_general | solution.py:48
  510.6 15.4 %convolution_add_fusion.5 = f32[1536,1500]{0,1:T(8,128)} fusion(f32[1536,1500]{0,1:T(8,128)S(1)} %convolution_add_fusion.4, f32[1536,1024]{1,0:T(8,128)} %get-tuple-element.387, s32[]{:T(128)S(6)} %select_n.109, f32[128]{0:T(128)S(1)} %fusion.93, s32[128]{0:T(128)S(1)} %iota_add_fusion.10, s32[1536]{0:T(1024)S(1)} %lt.134, s32[1500]{0:T(1024)S(1)} %iota_add_fusion.11), kind=kOutput, calls=%fused_computation.30.clone.1 | convolution fusion | flops 3543565824 | bytes 19260932 | tf_op jit(solution)/shard_map/while/body/dot_general | solution.py:48
  540.6 15.4 %convolution_add_fusion.5 = f32[1536,1500]{0,1:T(8,128)} fusion(f32[1536,1500]{0,1:T(8,128)S(1)} %convolution_add_fusion.4, f32[1536,1024]{1,0:T(8,128)} %get-tuple-element.387, s32[]{:T(128)S(6)} %select_n.109, f32[128]{0:T(128)S(1)} %fusion.93, s32[128]{0:T(128)S(1)} %iota_add_fusion.10, s32[1536]{0:T(1024)S(1)} %lt.134, s32[1500]{0:T(1024)S(1)} %iota_add_fusion.11), kind=kOutput, calls=%fused_computation.30.clone.1 | convolution fusion | flops 3543565824 | bytes 19260932 | tf_op jit(solution)/shard_map/while/body/dot_general | solution.py:48
  570.6 15.4 %convolution_add_fusion.5 = f32[1536,1500]{0,1:T(8,128)} fusion(f32[1536,1500]{0,1:T(8,128)S(1)} %convolution_add_fusion.4, f32[1536,1024]{1,0:T(8,128)} %get-tuple-element.387, s32[]{:T(128)S(6)} %select_n.109, f32[128]{0:T(128)S(1)} %fusion.93, s32[128]{0:T(128)S(1)} %iota_add_fusion.10, s32[1536]{0:T(1024)S(1)} %lt.134, s32[1500]{0:T(1024)S(1)} %iota_add_fusion.11), kind=kOutput, calls=%fused_computation.30.clone.1 | convolution fusion | flops 3543565824 | bytes 19260932 | tf_op jit(solution)/shard_map/while/body/dot_general | solution.py:48
  600.6 15.4 %convolution_add_fusion.5 = f32[1536,1500]{0,1:T(8,128)} fusion(f32[1536,1500]{0,1:T(8,128)S(1)} %convolution_add_fusion.4, f32[1536,1024]{1,0:T(8,128)} %get-tuple-element.387, s32[]{:T(128)S(6)} %select_n.109, f32[128]{0:T(128)S(1)} %fusion.93, s32[128]{0:T(128)S(1)} %iota_add_fusion.10, s32[1536]{0:T(1024)S(1)} %lt.134, s32[1500]{0:T(1024)S(1)} %iota_add_fusion.11), kind=kOutput, calls=%fused_computation.30.clone.1 | convolution fusion | flops 3543565824 | bytes 19260932 | tf_op jit(solution)/shard_map/while/body/dot_general | solution.py:48
  630.6 15.4 %convolution_add_fusion.5 = f32[1536,1500]{0,1:T(8,128)} fusion(f32[1536,1500]{0,1:T(8,128)S(1)} %convolution_add_fusion.4, f32[1536,1024]{1,0:T(8,128)} %get-tuple-element.387, s32[]{:T(128)S(6)} %select_n.109, f32[128]{0:T(128)S(1)} %fusion.93, s32[128]{0:T(128)S(1)} %iota_add_fusion.10, s32[1536]{0:T(1024)S(1)} %lt.134, s32[1500]{0:T(1024)S(1)} %iota_add_fusion.11), kind=kOutput, calls=%fused_computation.30.clone.1 | convolution fusion | flops 3543565824 | bytes 19260932 | tf_op jit(solution)/shard_map/while/body/dot_general | solution.py:48
  715.8 32.5 %collective-permute-start.3 = (f32[3,8,1,1500]{3,2,1,0:T(1,128)S(1)}, f32[3,8,1,1500]{3,2,1,0:T(1,128)S(1)}, u32[]{:S(2)}, u32[]{:S(2)}) collective-permute-start(f32[3,8,1,1500]{3,2,1,0:T(1,128)S(1)} %get-tuple-element.238), channel_id=1, source_target_pairs={{0,8},{8,16},{16,24},{1,9},{9,17},{17,25},{2,10},{10,18},{18,26},{... | collective-permute-start | bytes 432008 | tf_op jit(solution)/shard_map/ppermute | solution.py:24
  (122 shorter events, 208.7 us)
Async XLA Ops:
  7.2 453.8 %all-reduce.3.cloned.1.call-start = ((), (), s32[]{:S(2)}) async-start(), calls=%async_computation | async-start | bytes 25165824 | tf_op jit(solution)/shard_map/psum | solution.py:102
  254.4 211.4 %copy-start.7 = (s32[64]{0:T(128)S(1)}, s32[64]{0:T(128)}, u32[]{:S(2)}) copy-start(s32[64]{0:T(128)} %param.12) | copy-start | bytes 772
  691.6 16.8 %copy-start.8 = (f32[64]{0:T(128)S(1)}, f32[64]{0:T(128)}, u32[]{:S(2)}) copy-start(f32[64]{0:T(128)} %param.13) | copy-start | bytes 772
  698.9 12.3 %copy-start = (f32[512,1500]{1,0:T(8,128)}, f32[512,1500]{1,0:T(8,128)S(1)}, u32[]{:S(2)}) copy-start(f32[512,1500]{1,0:T(8,128)S(1)} %get-tuple-element.239) | copy-start | bytes 9216004
  704.3 44.0 %collective-permute-start = (f32[3,8,64,1]{2,1,3,0:T(8,128)S(1)}, f32[3,8,64,1]{2,1,3,0:T(8,128)S(1)}, u32[]{:S(2)}, u32[]{:S(2)}) collective-permute-start(f32[3,8,64,1]{2,1,3,0:T(8,128)S(1)} %copy.26), channel_id=1, source_target_pairs={{1,0},{2,1},{3,2},{4,3},{5,4},{6,5},{7,6},{0,7},{9,8},{10,9},{11,1... | collective-permute-start | bytes 18440 | tf_op jit(solution)/shard_map/ppermute | solution.py:26
  706.5 42.1 %collective-permute-start.1 = (f32[3,8,64,1]{2,1,3,0:T(8,128)S(1)}, f32[3,8,64,1]{2,1,3,0:T(8,128)S(1)}, u32[]{:S(2)}, u32[]{:S(2)}) collective-permute-start(f32[3,8,64,1]{2,1,3,0:T(8,128)S(1)} %copy.28), channel_id=1, source_target_pairs={{0,1},{1,2},{2,3},{3,4},{4,5},{5,6},{6,7},{7,0},{8,9},{9,10},{10,1... | collective-permute-start | bytes 18440 | tf_op jit(solution)/shard_map/ppermute | solution.py:24
  708.4 2.8 copy-start.1
  711.2 1.7 copy-start.3
  711.2 2.7 copy-start.5
  713.9 46.6 %collective-permute-start.2 = (f32[3,8,1,1500]{3,2,1,0:T(1,128)S(1)}, f32[3,8,1,1500]{3,2,1,0:T(1,128)S(1)}, u32[]{:S(2)}, u32[]{:S(2)}) collective-permute-start(f32[3,8,1,1500]{3,2,1,0:T(1,128)S(1)} %get-tuple-element.237), channel_id=1, source_target_pairs={{8,0},{16,8},{24,16},{9,1},{17,9},{25,17},{10,2},{18,10},{26,18},{... | collective-permute-start | bytes 432008 | tf_op jit(solution)/shard_map/ppermute | solution.py:26
  715.8 44.7 %collective-permute-start.3 = (f32[3,8,1,1500]{3,2,1,0:T(1,128)S(1)}, f32[3,8,1,1500]{3,2,1,0:T(1,128)S(1)}, u32[]{:S(2)}, u32[]{:S(2)}) collective-permute-start(f32[3,8,1,1500]{3,2,1,0:T(1,128)S(1)} %get-tuple-element.238), channel_id=1, source_target_pairs={{0,8},{8,16},{16,24},{1,9},{9,17},{17,25},{2,10},{10,18},{18,26},{... | collective-permute-start | bytes 432008 | tf_op jit(solution)/shard_map/ppermute | solution.py:24
  749.0 11.5 %copy-start.2 = (f32[512,1500]{1,0:T(8,128)S(1)}, f32[512,1500]{1,0:T(8,128)}, u32[]{:S(2)}) copy-start(f32[512,1500]{1,0:T(8,128)} %get-tuple-element.240) | copy-start | bytes 9216004
  749.0 11.5 %copy-start.4 = (f32[1,8,64,1500]{3,2,1,0:T(8,128)S(1)}, f32[1,8,64,1500]{3,2,1,0:T(8,128)}, u32[]{:S(2)}) copy-start(f32[1,8,64,1500]{3,2,1,0:T(8,128)} %copy-done.3) | copy-start | bytes 9216004
  749.0 11.5 %copy-start.6 = (f32[1,8,64,1500]{3,2,1,0:T(8,128)S(1)}, f32[1,8,64,1500]{3,2,1,0:T(8,128)}, u32[]{:S(2)}) copy-start(f32[1,8,64,1500]{3,2,1,0:T(8,128)} %copy-done.5) | copy-start | bytes 9216004
Sparse Core Ops, SparseCore 0:
  254.5 206.4 all-reduce.2
where the time goes:
time: 789 us; the launch traced here: 778 us
  matrix products  426 us (54%)
  waiting for transfers between devices  207 us (26%)
  local copies, waits for them, and re-layouts  51.9 us (7%)
  starting transfers between devices  37.1 us (5%)
  other arithmetic  35.4 us (4%)
  between operations  15.1 us (2%)
    dot_general x14, matrix products, contract_rows(): lax.dot_general(coeffs, table, (((1,), (1,)), ((), ())), precision=lax.Pr...  209 us
    psum x1, waiting for transfers between devices, on_device(): cosine, sine_part = lax.psum((cosine, sine_part), 'lon')  207 us
    dot_general x7, matrix products, analyse_step(): jnp.dot(lines, table_c, precision=lax.Precision.HIGHEST, preferred_elemen...  108 us
    dot_general x7, matrix products, analyse_step(): jnp.dot(lines, table_s, precision=lax.Precision.HIGHEST, preferred_elemen...  108 us
    ppermute x2, starting transfers between devices, padded(): lax.ppermute(tail, axis, [(i, (i + 1) % count) for i in range(ends)])  34.4 us
  transfers between devices with their start and end apart: 5, of which 1 were waited for; matrix products, arithmetic and copies ran while one was open for 2% of the time, Pallas kernels for 0%

commit v1 on v0

v1 whole, which is shorter than its diff:
```python
import functools
import math

import jax
import jax.numpy as jnp
import ml_dtypes
import numpy as np
from jax import lax
from jax.experimental import pallas as pl
from jax.experimental.pallas import tpu as pltpu
from jax.sharding import PartitionSpec as P

NLON = 12000
KMAX = 1024
MOMENTS = 32
EXTRA = 32
LANES = 128
CHUNKS = 1
courant = 0.5
BF = jnp.bfloat16
F32 = jnp.float32
VMEM_LIMIT = 56 * 1024 * 1024


def prolate(points, band, count):
    i = np.arange(points)
    diag = ((points - 1 - 2 * i) / 2.0) ** 2 * np.cos(2 * np.pi * band)
    off = i[1:] * (points - i[1:]) / 2.0
    mid = points // 2
    half = (count + 1) // 2
    out = np.zeros((points, 2 * half))
    dd, ee = diag[mid:], off[mid:].copy()
    scaled = ee.copy()
    scaled[0] *= math.sqrt(2.0)
    even = np.linalg.eigh(np.diag(dd) + np.diag(scaled, 1) + np.diag(scaled, -1))[1]
    even = even[:, ::-1][:, :half]
    wing = even[1:] / math.sqrt(2.0)
    out[mid, 0::2] = even[0]
    out[mid + 1 :, 0::2] = wing
    out[:mid, 0::2] = wing[::-1]
    odd = np.linalg.eigh(np.diag(dd[1:]) + np.diag(ee[1:], 1) + np.diag(ee[1:], -1))[1]
    wing = odd[:, ::-1][:, :half] / math.sqrt(2.0)
    out[mid + 1 :, 1::2] = wing
    out[:mid, 1::2] = -wing[::-1]
    return out


def interpolation(low, high, nodes, snap):
    fine = prolate(2 * (high - low) + 1, (KMAX - 0.5) / NLON / 2, nodes + 2)
    wave = fine[:, nodes]
    at = np.nonzero(wave[:-1] * wave[1:] < 0)[0]
    roots = (at + wave[at] / (wave[at] - wave[at + 1]))[: nodes // 2] / 2 + low
    left = snap(roots)
    for i in range(1, len(left)):
        left[i] = max(left[i], left[i - 1] + 1)
    places = np.concatenate([left, (low + high) - left[::-1]])
    kept = nodes - 4
    index = np.round((places - low) * 2).astype(int)
    return places, fine[::2, :kept] @ np.linalg.pinv(fine[index, :kept])


def near_kernel(distance):
    return 1.0 / (NLON * np.sin(np.pi * distance / NLON))


def two_parts(table):
    high = table.astype(np.float32).astype(ml_dtypes.bfloat16)
    low = (table - high.astype(np.float64)).astype(np.float32).astype(ml_dtypes.bfloat16)
    return high, low


@functools.lru_cache(maxsize=4)
def make_tables(width, segments):
    nodes = -(-2 * KMAX * width // NLON // 32) * 32 + EXTRA
    source, gather = interpolation(0, width - 1, nodes, np.round)
    target, spread = interpolation(-1, width, nodes, lambda r: np.floor(r) + 0.5)
    local = near_kernel(target[:, None] - source[None])
    offsets = [d for d in range(-(segments - 1), segments) if d]
    far = {d: near_kernel(target[:, None] + width * d - source[None]) for d in offsets}
    every = np.concatenate([far[d] for d in offsets])
    half, pairs = nodes // 2, MOMENTS // 2
    mirrored = every[:, ::-1][:, :half]
    even = np.linalg.svd(every[:, :half] + mirrored, full_matrices=False)[2][:pairs]
    odd = np.linalg.svd(every[:, :half] - mirrored, full_matrices=False)[2][:pairs]
    moments = np.concatenate(
        [
            np.concatenate([even, even[:, ::-1]], 1),
            np.concatenate([odd, -odd[:, ::-1]], 1),
        ]
    ) / math.sqrt(2.0)
    moments *= np.sign(moments[:, :1])

    high, low = two_parts(gather.T)
    gather_table = np.concatenate([high, low], 0)
    high, low = two_parts(np.concatenate([local, moments], 0))
    local_table = np.concatenate([high, low, high], 1)
    blocks = []
    for d in range(segments):
        zero = np.zeros((nodes, MOMENTS))
        row = [zero if e == d else far[d - e] @ moments.T for e in range(segments)]
        high, low = two_parts(np.concatenate(row, 1))
        blocks.append(np.concatenate([high, low, high], 1))
    far_table = np.stack(blocks)
    lanes = -(-(width + 2) // LANES) * LANES
    wide = np.zeros((nodes, lanes))
    wide[:, : width + 1] = spread.T[:, 1:]
    wide[:, lanes - 1] = spread.T[:, 0]
    high, low = two_parts(wide)
    spread_table = np.concatenate([high, low, high], 0)
    places = np.stack([2 * source - width, 2 * target - width]).astype(np.float32)
    return gather_table, local_table, far_table, spread_table, places[:, :, None]


def phases(cut, places, device, segments, width):
    full = 4.0 * NLON
    odd = 2.0 * cut - 1.0
    inner = odd * places
    inner = inner - full * jnp.floor(inner * (1.0 / full) + 0.5)
    base = odd * (2.0 * device + 1.0)
    cycle = 4.0 * segments
    base = (base - cycle * jnp.floor(base * (1.0 / cycle))) * float(width)
    total = inner + base
    total = total - full * jnp.floor(total * (1.0 / full) + 0.5)
    angle = total * (2.0 * math.pi / full)
    return jnp.cos(angle), jnp.sin(angle)


def parts(values):
    high = values.astype(BF)
    return high, (values - high.astype(F32)).astype(BF)


def stacked(values):
    high, low = parts(values)
    return jnp.concatenate([high, high, low], axis=0)


def product(a, b, dims):
    return lax.dot_general(a, b, (dims, ((), ())), preferred_element_type=F32)


def fill_phases(cut_ref, places_ref, device, segments, width, table_ref):
    for side in range(2):
        cosine, sine = phases(cut_ref[...], places_ref[side], device, segments, width)
        table_ref[2 * side] = cosine
        table_ref[2 * side + 1] = sine


def analyse_lines(lines, gather_ref, local_ref, table_ref, near_ref, moment_ref):
    nodes = gather_ref.shape[0] // 2
    tiles = lines.shape[0] // LANES
    high, low = parts(lines)
    both = product(gather_ref[...], high, ((1,), (1,)))
    rest = product(gather_ref[:nodes], low, ((1,), (1,)))
    held = both[:nodes] + both[nodes:] + rest
    for tile in range(tiles):
        mine = held[:, tile * LANES : (tile + 1) * LANES]
        turned = jnp.concatenate([mine * table_ref[0], mine * table_ref[1]], axis=1)
        out = product(local_ref[...], stacked(turned), ((1,), (0,)))
        near_ref[tile] = (
            table_ref[3] * out[:nodes, :LANES] - table_ref[2] * out[:nodes, LANES:]
        )
        moment_ref[tile, 0] = out[nodes:, :LANES]
        moment_ref[tile, 1] = out[nodes:, LANES:]


def analyse_kernel(
    segments, first, groups, device_ref, cut_ref, places_ref, gather_ref, local_ref,
    u_ref, v_ref, q_ref, near_ref, moment_ref, lines_ref, table_ref, sems,
):
    step = pl.program_id(0)
    width = u_ref.shape[2]
    levels = lines_ref.shape[1]

    def transfer(at, start):
        field, group = at // groups, at % groups
        slot = at % 2
        for number, ref in enumerate((u_ref, v_ref, q_ref)):

            @pl.when(field == number)
            def _():
                copy = pltpu.make_async_copy(
                    ref.at[pl.ds(first + group * levels, levels)], lines_ref.at[slot], sems.at[slot]
                )
                if start:
                    copy.start()
                else:
                    copy.wait()

    @pl.when(step == 0)
    def _():
        transfer(step, True)
        fill_phases(cut_ref, places_ref, device_ref[0].astype(F32), segments, width, table_ref)

    @pl.when(step + 1 < pl.num_programs(0))
    def _():
        transfer(step + 1, True)

    transfer(step, False)
    lines = lines_ref[step % 2]
    lines = lines.reshape(levels * lines.shape[1], width)
    analyse_lines(lines, gather_ref, local_ref, table_ref, near_ref, moment_ref)


def edge_kernel(
    segments, device_ref, cut_ref, places_ref, gather_ref, local_ref, up_ref, down_ref,
    near_in, moment_in, near_ref, moment_ref, table_ref,
):
    width = up_ref.shape[1]
    fill_phases(cut_ref, places_ref, device_ref[0].astype(F32), segments, width, table_ref)
    count = up_ref.shape[0]
    pad = jnp.zeros((LANES - 2 * count, width), F32)
    lines = jnp.concatenate([up_ref[...], down_ref[...], pad], axis=0)
    analyse_lines(lines, gather_ref, local_ref, table_ref, near_ref, moment_ref)


def finish_kernel(
    segments, first, levels_total, device_ref, cut_ref, edge_cut_ref, places_ref, far_ref, spread_ref,
    scale_ref, edge_scale_ref,
    near_u, near_v, near_q, near_e, far_u, far_v, far_q, far_e, tracer_ref,
    next_ref, div_ref, vort_ref, table_ref, edge_ref,
):
    step = pl.program_id(0)
    pair, rows, width = tracer_ref.shape
    moments = far_u.shape[3]
    nodes = near_u.shape[1]
    lanes = spread_ref.shape[1]
    device = device_ref[0].astype(F32)

    def whole(near_parts, far_parts, table):
        count = len(near_parts)
        sides = []
        for side in range(2):
            for part in far_parts:
                sides.append(part[:, 0, side].reshape(segments * moments, LANES))
        got = product(far_ref[0], stacked(jnp.concatenate(sides, axis=1)), ((1,), (0,)))
        values = []
        for i, near in enumerate(near_parts):
            cosine = got[:, i * LANES : (i + 1) * LANES]
            sine = got[:, (count + i) * LANES : (count + i + 1) * LANES]
            values.append(near[0] + table[1] * cosine - table[0] * sine)
        held = stacked(jnp.concatenate(values, axis=1))
        return product(held, spread_ref[...], ((0,), (0,)))

    @pl.when(step == 0)
    def _():
        cosine, sine = phases(edge_cut_ref[...], places_ref[1], device, segments, width)
        table_ref[0] = cosine
        table_ref[1] = sine
        edges = whole([near_e], [far_e], table_ref)
        edge_ref[...] = edges[: edge_ref.shape[0]] * edge_scale_ref[...]
        cosine, sine = phases(cut_ref[...], places_ref[1], device, segments, width)
        table_ref[0] = cosine
        table_ref[1] = sine

    filtered = whole([near_u, near_v, near_q], [far_u, far_v, far_q], table_ref)
    scale = scale_ref[...]
    inverse = 1.0 / scale
    row_number = lax.broadcasted_iota(jnp.int32, (rows, 1), 0)
    for part in range(pair):
        level = first + step * pair + part

        def field(number):
            at = number * pair * rows + part * rows
            return filtered[at : at + rows]

        def east_west(values):
            return pltpu.roll(values, lanes - 1, 1) - pltpu.roll(values, 1, 1)

        def north_south(values, number):
            above = edge_ref[pl.ds(number * levels_total + level, 1), :]
            below = edge_ref[pl.ds((3 + number) * levels_total + level, 1), :]
            later = jnp.where(row_number == rows - 1, below, pltpu.roll(values, rows - 1, 0))
            earlier = jnp.where(row_number == 0, above, pltpu.roll(values, 1, 0))
            return later - earlier

        u, v, q = field(0), field(1), field(2)
        div = scale * (east_west(u) + north_south(v * inverse, 1))
        vort = scale * (east_west(v) - north_south(u * inverse, 0))
        change = courant * (u * scale * east_west(q) + v * north_south(q, 2))
        div_ref[part] = div[:, :width]
        vort_ref[part] = vort[:, :width]
        next_ref[part] = tracer_ref[part] - change[:, :width]


def whole_spec():
    return pl.BlockSpec(memory_space=pltpu.VMEM)


def on_device(segments, lats, tables, wind_u, wind_v, tracer, cutoff, row_scale):
    levels, rows, width = wind_u.shape
    gather_table, local_table, far_table, spread_table, places = tables
    nodes = gather_table.shape[0] // 2
    lanes = spread_table.shape[1]
    nl = levels // CHUNKS
    pair = LANES // rows
    group = 2 * pair
    groups = nl // group
    tiles = 3 * nl // pair
    device = lax.axis_index("lon").astype(jnp.int32)[None]

    def edge(row):
        pack = jnp.stack([cutoff[row].astype(F32), row_scale[row]])
        pack = jnp.pad(pack, (0, width - 2))[None]
        return jnp.concatenate([wind_u[:, row], wind_v[:, row], tracer[:, row], pack], axis=0)

    up = lax.ppermute(edge(rows - 1), "lat", [(i, i + 1) for i in range(lats - 1)])
    down = lax.ppermute(edge(0), "lat", [(i + 1, i) for i in range(lats - 1)])
    count = 3 * levels
    edge_cut = jnp.concatenate(
        [
            jnp.broadcast_to(up[count, 0], (count,)),
            jnp.broadcast_to(down[count, 0], (count,)),
            jnp.ones((LANES - 2 * count,), F32),
        ]
    )[None]
    weighted = jnp.arange(count) < 2 * levels

    def edge_weight(got):
        held = got[count, 1]
        held = jnp.where(held > 0.0, held, 1.0)
        return jnp.where(weighted, 1.0 / held, 1.0)

    edge_scale = jnp.concatenate([edge_weight(up), edge_weight(down)])[:, None]
    cut = jnp.tile(cutoff.astype(F32), pair)[None]
    scale = row_scale[:, None]

    smem = pl.BlockSpec(memory_space=pltpu.SMEM)
    anywhere = pl.BlockSpec(memory_space=pl.ANY)
    params = pltpu.CompilerParams(
        dimension_semantics=("arbitrary",), vmem_limit_bytes=VMEM_LIMIT
    )
    table_scratch = pltpu.VMEM((4, nodes, LANES), F32)

    def analyse(chunk, extra):
        shapes = (
            jax.ShapeDtypeStruct((tiles + extra, nodes, LANES), F32),
            jax.ShapeDtypeStruct((tiles + extra, 2, MOMENTS, LANES), F32),
        )
        return pl.pallas_call(
            functools.partial(analyse_kernel, segments, chunk * nl, groups),
            out_shape=shapes,
            grid=(3 * groups,),
            in_specs=[smem] + [whole_spec()] * 4 + [anywhere] * 3,
            out_specs=(
                pl.BlockSpec((2, nodes, LANES), lambda s: (s, 0, 0)),
                pl.BlockSpec((2, 2, MOMENTS, LANES), lambda s: (s, 0, 0, 0)),
            ),
            scratch_shapes=[
                pltpu.VMEM((2, group, rows, width), F32),
                table_scratch,
                pltpu.SemaphoreType.DMA((2,)),
            ],
            compiler_params=params,
            name="analyse",
        )(device, cut, places, gather_table, local_table, wind_u, wind_v, tracer)

    def analyse_edges(near, moment):
        last = tiles
        return pl.pallas_call(
            functools.partial(edge_kernel, segments),
            out_shape=(
                jax.ShapeDtypeStruct(near.shape, F32),
                jax.ShapeDtypeStruct(moment.shape, F32),
            ),
            grid=(1,),
            in_specs=[smem] + [whole_spec()] * 6 + [anywhere] * 2,
            out_specs=(
                pl.BlockSpec((1, nodes, LANES), lambda s: (last, 0, 0)),
                pl.BlockSpec((1, 2, MOMENTS, LANES), lambda s: (last, 0, 0, 0)),
            ),
            scratch_shapes=[table_scratch],
            input_output_aliases={7: 0, 8: 1},
            compiler_params=params,
            name="edges",
        )(device, edge_cut, places, gather_table, local_table, up[:count], down[:count], near, moment)

    def finish(chunk, near, far, edge_near, edge_far):
        per_field = nl // pair

        def near_spec(at, moving):
            return pl.BlockSpec((1, nodes, LANES), lambda s, d: (at + s * moving, 0, 0))

        def far_spec(at, moving):
            return pl.BlockSpec(
                (segments, 1, 2, MOMENTS, LANES), lambda s, d: (0, at + s * moving, 0, 0, 0)
            )

        start = chunk * nl // pair
        block = pl.BlockSpec((pair, rows, width), lambda s, d: (start + s, 0, 0))
        out_block = pl.BlockSpec((pair, rows, width), lambda s, d: (s, 0, 0))
        return pl.pallas_call(
            functools.partial(finish_kernel, segments, chunk * nl, levels),
            out_shape=(jax.ShapeDtypeStruct((nl, rows, width), F32),) * 3,
            grid_spec=pltpu.PrefetchScalarGridSpec(
                num_scalar_prefetch=1,
                grid=(per_field,),
                in_specs=[whole_spec()] * 3
                + [pl.BlockSpec((1,) + far_table.shape[1:], lambda s, d: (d[0], 0, 0))]
                + [whole_spec()] * 3
                + [near_spec(0, 1), near_spec(per_field, 1), near_spec(2 * per_field, 1)]
                + [near_spec(tiles, 0)]
                + [far_spec(0, 1), far_spec(per_field, 1), far_spec(2 * per_field, 1)]
                + [far_spec(tiles, 0), block],
                out_specs=(out_block,) * 3,
                scratch_shapes=[
                    pltpu.VMEM((2, nodes, LANES), F32),
                    pltpu.VMEM((2 * count, lanes), F32),
                ],
            ),
            compiler_params=params,
            name="finish",
        )(
            device, cut, edge_cut, places, far_table, spread_table, scale, edge_scale,
            near, near, near, edge_near, far, far, far, edge_far, tracer,
        )

    near, moment = analyse(0, 1)
    near, moment = analyse_edges(near, moment)
    far = lax.all_gather(moment, "lon")
    return finish(0, near, far, near, far)


def solution(mesh):
    segments, lats = mesh.shape["lon"], mesh.shape["lat"]
    tables = tuple(make_tables(NLON // segments, segments))
    line = P(None, "lat", "lon")
    return jax.shard_map(
        functools.partial(on_device, segments, lats, tables),
        mesh=mesh,
        in_specs=(line, line, line, P("lat"), P("lat")),
        out_specs=(line, line, line),
        check_vma=False,
    )
```

time: 789 us -> 108 us (0.14)
  the two profiles are of different devices: /device:TPU:19 before, /device:TPU:8 now
where the time goes in v1:
time: 108 us; the launch traced here: 106 us
  Pallas kernels  37.4 us (35%)
  waiting for transfers between devices  29.6 us (27%)
  between operations  18.1 us (17%)
  local copies, waits for them, and re-layouts  12.2 us (11%)
  starting transfers between devices  5.88 us (5%)
  other arithmetic  2.8 us (3%)
    all_gather x1, waiting for transfers between devices, on_device(): far = lax.all_gather(moment, 'lon')  29.6 us
    pallas_call x1, Pallas kernels, finish(): pl.pallas_call(functools.partial(finish_kernel, segments, chunk * nl, lev...  16.8 us
    pallas_call x1, Pallas kernels, analyse(): pl.pallas_call(functools.partial(analyse_kernel, segments, chunk * nl, gr...  16.2 us
    pallas_call x1, Pallas kernels, analyse_edges(): pl.pallas_call(functools.partial(edge_kernel, segments), out_shape=(jax.S...  4.4 us
    ppermute x1, starting transfers between devices, on_device(): lax.ppermute(edge(rows - 1), 'lat', [(i, i + 1) for i in range(lats - 1)])  3.92 us
    slice x2, local copies, waits for them, and re-layouts, edge(): pack = jnp.stack([cutoff[row].astype(F32), row_scale[row]])  2.63 us
  transfers between devices with their start and end apart: 3, of which 1 were waited for; matrix products, arithmetic and copies ran while one was open for 3% of the time, Pallas kernels for 15%

profile of v1, /device:TPU:8, one launch (start us, length us, event | category | flops | bytes accessed | tf_op | source)
XLA Modules:
  0.0 106.0 jit_solution(1749005775966929617)
XLA Ops:
  7.2 1.3 %fusion.5 = (s32[1]{0:T(128)}, s32[1]{0:T(128)}) fusion(s32[64]{0:T(128)} %param.13), kind=kLoop, calls=%fused_computation.20 | loop fusion | bytes 16 | tf_op jit(solution)/shard_map/slice | solution.py:303
  9.8 1.3 %fusion.6 = (f32[1]{0:T(128)}, f32[1]{0:T(128)}) fusion(f32[64]{0:T(128)} %param.14), kind=kLoop, calls=%fused_computation.21 | loop fusion | bytes 16 | tf_op jit(solution)/shard_map/slice | solution.py:303
  11.1 1.4 %select_maximum_fusion = (f32[1500]{0:T(1024)S(1)}, f32[1500]{0:T(1024)S(1)}) fusion(f32[1]{0:T(128)} %get-tuple-element.24, f32[1]{0:T(128)S(6)} %convert_element_type.16, f32[1]{0:T(128)} %get-tuple-element.23, f32[1]{0:T(128)S(6)} %convert_element_type.15), kind=kLoop, calls=%fused_computation.8 | loop fusion | flops 10500 | bytes 12016 | tf_op jit(solution)/shard_map/stack | solution.py:303
  12.5 1.2 %fusion = (f32[8,1,1500]{2,1,0:T(1,128)S(1)}, f32[8,1,1500]{2,1,0:T(1,128)S(1)}) fusion(f32[8,64,1500]{2,1,0:T(8,128)} %u_ref.1), kind=kLoop, calls=%fused_computation.15 | loop fusion | bytes 192000 | tf_op jit(solution)/shard_map/slice | solution.py:305
  13.7 1.2 %fusion.1 = (f32[8,1,1500]{2,1,0:T(1,128)S(1)}, f32[8,1,1500]{2,1,0:T(1,128)S(1)}) fusion(f32[8,64,1500]{2,1,0:T(8,128)} %v_ref.1), kind=kLoop, calls=%fused_computation.16 | loop fusion | bytes 192000 | tf_op jit(solution)/shard_map/slice | solution.py:305
  14.9 1.2 %fusion.2 = (f32[8,1,1500]{2,1,0:T(1,128)S(1)}, f32[8,1,1500]{2,1,0:T(1,128)S(1)}) fusion(f32[8,64,1500]{2,1,0:T(8,128)} %tracer_ref.1), kind=kLoop, calls=%fused_computation.17 | loop fusion | bytes 192000 | tf_op jit(solution)/shard_map/slice | solution.py:305
  16.1 1.9 %collective-permute-start.1 = (f32[25,1500]{1,0:T(8,128)S(1)}, f32[25,1500]{1,0:T(8,128)S(1)}, u32[]{:S(2)}, u32[]{:S(2)}) collective-permute-start(f32[25,1500]{1,0:T(8,128)S(1)} %pad_maximum_fusion.1), channel_id=1, source_target_pairs={{8,0},{16,8},{24,16},{9,1},{17,9},{25,17},{10,2},{18,10},{26,18},{... | collective-permute-start | bytes 450008 | tf_op jit(solution)/shard_map/ppermute | solution.py:308
  18.1 3.9 %collective-permute-start = (f32[25,1500]{1,0:T(8,128)S(1)}, f32[25,1500]{1,0:T(8,128)S(1)}, u32[]{:S(2)}, u32[]{:S(2)}) collective-permute-start(f32[25,1500]{1,0:T(8,128)S(1)} %pad_maximum_fusion), channel_id=1, source_target_pairs={{0,8},{8,16},{16,24},{1,9},{9,17},{17,25},{2,10},{10,18},{18,26},{... | collective-permute-start | bytes 450008 | tf_op jit(solution)/shard_map/ppermute | solution.py:307
  22.1 0.7 convert_element_type.14
  22.7 0.6 broadcast_in_dim_tile.3.cut_ref
  23.3 16.2 %analyse.1 = (f32[13,288,128]{2,1,0:T(8,128)}, f32[13,2,32,128]{3,2,1,0:T(8,128)}) custom-call(s32[1]{0:T(128)} %bitcast.device_ref, f32[1,128]{1,0:T(1,128)} %broadcast_in_dim_tile.3.cut_ref, f32[2,288,1]{2,1,0:T(8,128)} %constant.8.clone.places_ref, bf16[576,1500]{1,0:T(8,128)(2,1)} %constant.24.clone.gather_ref, ...), custom_call_target="tpu_custom_call" | custom-call | tf_op jit(solution)/shard_map/analyse/pallas_call | solution.py:340
  39.6 0.6 fusion.4
  40.2 0.7 fusion.3
  40.8 0.6 broadcast_in_dim.43
  41.5 0.6 broadcast_in_dim.41
  42.1 0.7 maximum_bitcast_fusion.cut_ref.edge_cut_ref
  42.8 0.7 slice.69.down_ref
  43.5 0.7 slice.68.up_ref
  44.1 4.4 %edges.1 = (f32[13,288,128]{2,1,0:T(8,128)}, f32[13,2,32,128]{3,2,1,0:T(8,128)}) custom-call(s32[1]{0:T(128)} %bitcast.device_ref, f32[1,128]{1,0:T(1,128)} %maximum_bitcast_fusion.cut_ref.edge_cut_ref, f32[2,288,1]{2,1,0:T(8,128)} %constant.8.clone.places_ref, ...), custom_call_target="tpu_custom_call", output_to_operand_aliasing={{0}: (7, {}), {1}: (8, {})} | custom-call | tf_op jit(solution)/shard_map/edges/pallas_call | solution.py:360
  48.6 0.7 copy.29.scale_ref
  51.9 0.1 maximum_bitcast_fusion.1
  52.0 0.7 copy.30.edge_scale_ref
  52.7 29.6 %all-gather.3.cloned.1.call-done = f32[104,2,32,128]{3,2,1,0:T(8,128)} async-done(((f32[13,2,32,128]{3,2,1,0:T(8,128)}), f32[104,2,32,128]{3,2,1,0:T(8,128)}) %all-gather.3.cloned.1.call-update) | async-done | bytes 3407888 | tf_op jit(solution)/shard_map/all_gather | solution.py:420
  82.3 16.8 %finish.1 = (f32[8,64,1500]{2,1,0:T(8,128)}, f32[8,64,1500]{2,1,0:T(8,128)}, f32[8,64,1500]{2,1,0:T(8,128)}) custom-call(s32[1]{0:T(128)} %bitcast.device_ref, f32[1,128]{1,0:T(1,128)} %broadcast_in_dim_tile.3.cut_ref, f32[1,128]{1,0:T(1,128)} %maximum_bitcast_fusion.cut_ref.edge_cut_ref, f32[2,288,1]{2,1,0:T(8,128)} %constant.8.clone.places_ref, ...), custom_call_target="tpu_custom_call" | custom-call | tf_op jit(solution)/shard_map/finish/pallas_call | solution.py:392
  (18 shorter events, 0.2 us)
Async XLA Ops:
  7.2 75.1 %all-gather.3.cloned.1.call-start = ((), (), s32[]{:S(2)}) async-start(), calls=%async_computation | async-start | bytes 3833856 | tf_op jit(solution)/shard_map/all_gather | solution.py:420
  16.1 23.4 %collective-permute-start.1 = (f32[25,1500]{1,0:T(8,128)S(1)}, f32[25,1500]{1,0:T(8,128)S(1)}, u32[]{:S(2)}, u32[]{:S(2)}) collective-permute-start(f32[25,1500]{1,0:T(8,128)S(1)} %pad_maximum_fusion.1), channel_id=1, source_target_pairs={{8,0},{16,8},{24,16},{9,1},{17,9},{25,17},{10,2},{18,10},{26,18},{... | collective-permute-start | bytes 450008 | tf_op jit(solution)/shard_map/ppermute | solution.py:308
  18.1 22.0 %collective-permute-start = (f32[25,1500]{1,0:T(8,128)S(1)}, f32[25,1500]{1,0:T(8,128)S(1)}, u32[]{:S(2)}, u32[]{:S(2)}) collective-permute-start(f32[25,1500]{1,0:T(8,128)S(1)} %pad_maximum_fusion), channel_id=1, source_target_pairs={{0,8},{8,16},{16,24},{1,9},{9,17},{17,25},{2,10},{10,18},{18,26},{... | collective-permute-start | bytes 450008 | tf_op jit(solution)/shard_map/ppermute | solution.py:307
  42.8 5.8 %copy-start = (f32[64]{0:T(128)S(1)}, f32[64]{0:T(128)}, u32[]{:S(2)}) copy-start(f32[64]{0:T(128)} %param.14) | copy-start | bytes 772
Sparse Core Ops, SparseCore 0:
  48.7 33.5 all-gather.2

commit v2 on v1

v2 whole, which is shorter than its diff:
```python
import functools
import math

import jax
import jax.numpy as jnp
import ml_dtypes
import numpy as np
from jax import lax
from jax.experimental import pallas as pl
from jax.experimental.pallas import tpu as pltpu
from jax.sharding import PartitionSpec as P

NLON = 12000
KMAX = 1024
NEAR = 16
FAR = 8
EXTRA = 32
LANES = 128
CHUNKS = 1
courant = 0.5
BF = jnp.bfloat16
F32 = jnp.float32
VMEM_LIMIT = 56 * 1024 * 1024


def prolate(points, band, count):
    i = np.arange(points)
    diag = ((points - 1 - 2 * i) / 2.0) ** 2 * np.cos(2 * np.pi * band)
    off = i[1:] * (points - i[1:]) / 2.0
    mid = points // 2
    half = (count + 1) // 2
    out = np.zeros((points, 2 * half))
    dd, ee = diag[mid:], off[mid:].copy()
    scaled = ee.copy()
    scaled[0] *= math.sqrt(2.0)
    even = np.linalg.eigh(np.diag(dd) + np.diag(scaled, 1) + np.diag(scaled, -1))[1]
    even = even[:, ::-1][:, :half]
    wing = even[1:] / math.sqrt(2.0)
    out[mid, 0::2] = even[0]
    out[mid + 1 :, 0::2] = wing
    out[:mid, 0::2] = wing[::-1]
    odd = np.linalg.eigh(np.diag(dd[1:]) + np.diag(ee[1:], 1) + np.diag(ee[1:], -1))[1]
    wing = odd[:, ::-1][:, :half] / math.sqrt(2.0)
    out[mid + 1 :, 1::2] = wing
    out[:mid, 1::2] = -wing[::-1]
    return out


def interpolation(low, high, nodes, snap):
    fine = prolate(2 * (high - low) + 1, (KMAX - 0.5) / NLON / 2, nodes + 2)
    wave = fine[:, nodes]
    at = np.nonzero(wave[:-1] * wave[1:] < 0)[0]
    roots = (at + wave[at] / (wave[at] - wave[at + 1]))[: nodes // 2] / 2 + low
    left = snap(roots)
    for i in range(1, len(left)):
        left[i] = max(left[i], left[i - 1] + 1)
    places = np.concatenate([left, (low + high) - left[::-1]])
    kept = nodes - 4
    index = np.round((places - low) * 2).astype(int)
    return places, fine[::2, :kept] @ np.linalg.pinv(fine[index, :kept])


def near_kernel(distance):
    return 1.0 / (NLON * np.sin(np.pi * distance / NLON))


def two_parts(table):
    high = table.astype(np.float32).astype(ml_dtypes.bfloat16)
    low = (table - high.astype(np.float64)).astype(np.float32).astype(ml_dtypes.bfloat16)
    return high, low


@functools.lru_cache(maxsize=4)
def make_tables(width, segments):
    main = -(-2 * KMAX * width // NLON // LANES) * LANES
    nodes = main + EXTRA
    source, gather = interpolation(0, width - 1, nodes, np.round)
    target, spread = interpolation(-1, width, nodes, lambda r: np.floor(r) + 0.5)
    local = near_kernel(target[:, None] - source[None])
    offsets = [d for d in range(-(segments - 1), segments) if d]
    far = {d: near_kernel(target[:, None] + width * d - source[None]) for d in offsets}

    def leading(kernel, count):
        found = np.linalg.svd(kernel, full_matrices=False)[2][:count]
        peak = np.take_along_axis(found, np.abs(found).argmax(1)[:, None], 1)
        return found * np.sign(peak)

    right, left = leading(far[1], NEAR), leading(far[-1], NEAR)
    every = np.concatenate([far[d] for d in range(2, segments - 1)])
    half = nodes // 2
    mirrored = every[:, ::-1][:, :half]
    even = leading(every[:, :half] + mirrored, FAR // 2)
    odd = leading(every[:, :half] - mirrored, FAR // 2)
    rest = np.concatenate(
        [np.concatenate([even, even[:, ::-1]], 1), np.concatenate([odd, -odd[:, ::-1]], 1)]
    ) / math.sqrt(2.0)

    high, low = two_parts(gather.T)
    gather_table = np.concatenate([high, low], 0)
    high, low = two_parts(np.concatenate([local, right, left, rest], 0))
    local_table = np.concatenate([high, low, high], 1)
    blocks = []
    for d in range(segments):
        row = [far[d - (d - 1) % segments] @ right.T, far[d - (d + 1) % segments] @ left.T]
        row += [far[d - (d - s) % segments] @ rest.T for s in range(2, segments - 1)]
        high, low = two_parts(np.concatenate(row, 1))
        blocks.append(np.concatenate([high, low, high], 1))
    far_table = np.stack(blocks)
    lanes = -(-(width + 2) // LANES) * LANES
    wide = np.zeros((nodes, lanes))
    wide[:, : width + 1] = spread.T[:, 1:]
    wide[:, lanes - 1] = spread.T[:, 0]
    high, low = two_parts(wide)
    none = np.zeros((LANES - 3 * EXTRA, lanes), high.dtype)
    spread_table = np.concatenate(
        [high[:main], low[:main], high[:main], high[main:], low[main:], high[main:], none], 0
    )
    places = np.stack([2 * source - width, 2 * target - width]).astype(np.float32)
    return gather_table, local_table, far_table, spread_table, places[:, :, None]


def phases(cut, places, device, segments, width):
    full = 4.0 * NLON
    odd = 2.0 * cut - 1.0
    inner = odd * places
    inner = inner - full * jnp.floor(inner * (1.0 / full) + 0.5)
    base = odd * (2.0 * device + 1.0)
    cycle = 4.0 * segments
    base = (base - cycle * jnp.floor(base * (1.0 / cycle))) * float(width)
    total = inner + base
    total = total - full * jnp.floor(total * (1.0 / full) + 0.5)
    quarter = jnp.floor(total * (4.0 / full) + 0.5)
    x = (total - (full / 4.0) * quarter) * (2.0 * math.pi / full)
    y = x * x
    sine = x + x * y * (
        -1.0 / 6 + y * (1.0 / 120 + y * (-1.0 / 5040 + y * (1.0 / 362880)))
    )
    cosine = 1.0 + y * (
        -0.5 + y * (1.0 / 24 + y * (-1.0 / 720 + y * (1.0 / 40320 + y * (-1.0 / 3628800))))
    )
    odd_quarter = jnp.abs(quarter) == 1.0
    turned_c = jnp.where(odd_quarter, -quarter * sine, cosine)
    turned_s = jnp.where(odd_quarter, quarter * cosine, sine)
    flip = jnp.where(jnp.abs(quarter) == 2.0, -1.0, 1.0)
    return turned_c * flip, turned_s * flip


def parts(values):
    high = values.astype(BF)
    return high, (values - high.astype(F32)).astype(BF)


def stacked(values):
    high, low = parts(values)
    return jnp.concatenate([high, high, low], axis=0)


def product(a, b, dims):
    return lax.dot_general(a, b, (dims, ((), ())), preferred_element_type=F32)


def lane_cut(cut_ref):
    cut = cut_ref[...].astype(F32)
    return jnp.concatenate([cut] * (LANES // cut.shape[1]), axis=1)


def packed(values):
    main = values.shape[1] - LANES
    high, low = parts(values)
    last, last_low = high[:, main:].astype(F32), low[:, main:].astype(F32)
    last = last + pltpu.roll(last, EXTRA, 1) + pltpu.roll(last_low, 2 * EXTRA, 1)
    return jnp.concatenate([high[:, :main], low[:, :main], last.astype(BF)], axis=1)


def spread_lines(pack, spread_ref):
    main = (pack.shape[1] - LANES) // 2
    held = jnp.concatenate([pack[:, :main], pack], axis=1)
    return product(held, spread_ref[...], ((1,), (0,)))


def analyse_kernel(
    segments, first, groups, device_ref, cut_ref, places_ref, gather_ref, local_ref,
    u_ref, v_ref, q_ref, near_ref, right_ref, left_ref, far_ref, lines_ref, table_ref, sems,
):
    step = pl.program_id(0)
    width = u_ref.shape[2]
    levels = lines_ref.shape[1]
    nodes = gather_ref.shape[0] // 2

    def transfer(at, start):
        field, group = at // groups, at % groups
        slot = at % 2
        for number, ref in enumerate((u_ref, v_ref, q_ref)):

            @pl.when(field == number)
            def _():
                copy = pltpu.make_async_copy(
                    ref.at[pl.ds(first + group * levels, levels)], lines_ref.at[slot], sems.at[slot]
                )
                if start:
                    copy.start()
                else:
                    copy.wait()

    @pl.when(step == 0)
    def _():
        transfer(step, True)
        device = device_ref[0].astype(F32)
        for side in range(2):
            cosine, sine = phases(lane_cut(cut_ref), places_ref[side], device, segments, width)
            table_ref[2 * side] = cosine
            table_ref[2 * side + 1] = sine

    @pl.when(step + 1 < pl.num_programs(0))
    def _():
        transfer(step + 1, True)

    transfer(step, False)
    lines = lines_ref[step % 2]
    lines = lines.reshape(levels * lines.shape[1], width)
    high, low = parts(lines)
    both = product(gather_ref[...], high, ((1,), (1,)))
    rest = product(gather_ref[:nodes], low, ((1,), (1,)))
    held = both[:nodes] + both[nodes:] + rest
    for tile in range(lines.shape[0] // LANES):
        mine = held[:, tile * LANES : (tile + 1) * LANES]
        turned = jnp.concatenate([mine * table_ref[0], mine * table_ref[1]], axis=1)
        out = product(local_ref[...], stacked(turned), ((1,), (0,)))
        near_ref[tile] = (
            table_ref[3] * out[:nodes, :LANES] - table_ref[2] * out[:nodes, LANES:]
        )
        at = nodes
        for ref in (right_ref, left_ref, far_ref):
            count = ref.shape[2]
            ref[tile, 0] = out[at : at + count, :LANES]
            ref[tile, 1] = out[at : at + count, LANES:]
            at += count


def combine_kernel(segments, width, per_field, device_ref, cut_ref, scale_ref, places_ref, table_in, near_ref, *refs):
    moment_refs, (pack_ref, top_ref, bottom_ref, table_ref) = refs[:-4], refs[-4:]
    step = pl.program_id(0)
    tiles, nodes, _ = near_ref.shape
    rows = cut_ref.shape[1]

    @pl.when(step == 0)
    def _():
        device = device_ref[0].astype(F32)
        cosine, sine = phases(lane_cut(cut_ref), places_ref[1], device, segments, width)
        table_ref[0] = cosine
        table_ref[1] = sine

    sides = []
    for tile in range(tiles):
        for side in range(2):
            sides.append(jnp.concatenate([ref[tile, side] for ref in moment_refs], axis=0))
    got = product(table_in[0], stacked(jnp.concatenate(sides, axis=1)), ((1,), (0,)))
    inverse = 1.0 / scale_ref[...]
    none = jnp.zeros((LANES - EXTRA, LANES), F32)
    for tile in range(tiles):
        at = 2 * tile * LANES
        cosine, sine = got[:, at : at + LANES], got[:, at + LANES : at + 2 * LANES]
        values = near_ref[tile] + table_ref[1] * cosine - table_ref[0] * sine
        values = jnp.transpose(jnp.concatenate([values, none], axis=0))
        pack_ref[tile] = packed(values)
        number = step * tiles + tile
        wind = number < 2 * per_field
        top_weight = jnp.where(wind, inverse[:, :1], 1.0)
        bottom_weight = jnp.where(wind, inverse[:, rows - 1 :], 1.0)
        pair = LANES // rows
        for part in range(pair):
            line = number * pair + part
            top_ref[pl.ds(line, 1), :] = values[part * rows : part * rows + 1] * top_weight
            last = part * rows + rows - 1
            bottom_ref[pl.ds(line, 1), :] = values[last : last + 1] * bottom_weight


def finish_kernel(
    scale_ref, spread_ref, above_ref, below_ref, pack_u, pack_v, pack_q, tracer_ref, *refs
):
    next_ref, div_ref, vort_ref, edge_ref, column_ref = refs[-5:]
    step = pl.program_id(0)
    pair, rows, width = tracer_ref.shape
    lanes = spread_ref.shape[1]
    count = above_ref.shape[0]
    levels = count // 3

    @pl.when(step == 0)
    def _():
        edges = jnp.concatenate([above_ref[...], below_ref[...]], axis=0)
        edge_ref[...] = spread_lines(packed(edges), spread_ref)
        here = lax.broadcasted_iota(jnp.int32, (rows, rows), 0)
        there = lax.broadcasted_iota(jnp.int32, (rows, rows), 1)
        column = jnp.where(here == there, jnp.broadcast_to(scale_ref[...], (rows, rows)), 0.0)
        column = jnp.sum(column, axis=1, keepdims=True)
        column_ref[0] = jnp.broadcast_to(column, (rows, LANES))
        column_ref[1] = 1.0 / column_ref[0]

    pack = jnp.concatenate([pack_u[0], pack_v[0], pack_q[0]], axis=0)
    filtered = spread_lines(pack, spread_ref)
    scale = column_ref[0][:, :1]
    inverse = column_ref[1][:, :1]
    row_number = lax.broadcasted_iota(jnp.int32, (rows, 1), 0)
    for part in range(pair):
        level = step * pair + part

        def field(number):
            at = number * pair * rows + part * rows
            return filtered[at : at + rows]

        def east_west(values):
            return pltpu.roll(values, lanes - 1, 1) - pltpu.roll(values, 1, 1)

        def north_south(values, number):
            above = edge_ref[pl.ds(number * levels + level, 1), :]
            below = edge_ref[pl.ds(count + number * levels + level, 1), :]
            later = jnp.where(row_number == rows - 1, below, pltpu.roll(values, rows - 1, 0))
            earlier = jnp.where(row_number == 0, above, pltpu.roll(values, 1, 0))
            return later - earlier

        u, v, q = field(0), field(1), field(2)
        div = scale * (east_west(u) + north_south(v * inverse, 1))
        vort = scale * (east_west(v) - north_south(u * inverse, 0))
        change = courant * (u * scale * east_west(q) + v * north_south(q, 2))
        div_ref[part] = div[:, :width]
        vort_ref[part] = vort[:, :width]
        next_ref[part] = tracer_ref[part] - change[:, :width]


def whole_spec():
    return pl.BlockSpec(memory_space=pltpu.VMEM)


def on_device(segments, lats, tables, wind_u, wind_v, tracer, cutoff, row_scale):
    levels, rows, width = wind_u.shape
    gather_table, local_table, far_table, spread_table, places = tables
    nodes = gather_table.shape[0] // 2
    lanes = spread_table.shape[1]
    wide = nodes - EXTRA + LANES
    nl = levels // CHUNKS
    pair = LANES // rows
    group = 2 * pair
    groups = nl // group
    tiles = 3 * nl // pair
    per_field = nl // pair
    count = 3 * nl
    device = lax.axis_index("lon").astype(jnp.int32)[None]
    cut = cutoff.reshape(1, rows)
    scale = row_scale.reshape(1, rows)

    smem = pl.BlockSpec(memory_space=pltpu.SMEM)
    anywhere = pl.BlockSpec(memory_space=pl.ANY)
    params = pltpu.CompilerParams(
        dimension_semantics=("arbitrary",), vmem_limit_bytes=VMEM_LIMIT
    )

    def analyse(chunk):
        moments = (NEAR, NEAR, FAR)
        return pl.pallas_call(
            functools.partial(analyse_kernel, segments, chunk * nl, groups),
            out_shape=(jax.ShapeDtypeStruct((tiles, nodes, LANES), F32),)
            + tuple(jax.ShapeDtypeStruct((tiles, 2, n, LANES), F32) for n in moments),
            grid=(3 * groups,),
            in_specs=[smem] + [whole_spec()] * 4 + [anywhere] * 3,
            out_specs=(pl.BlockSpec((2, nodes, LANES), lambda s: (s, 0, 0)),)
            + tuple(pl.BlockSpec((2, 2, n, LANES), lambda s: (s, 0, 0, 0)) for n in moments),
            scratch_shapes=[
                pltpu.VMEM((2, group, rows, width), F32),
                pltpu.VMEM((4, nodes, LANES), F32),
                pltpu.SemaphoreType.DMA((2,)),
            ],
            compiler_params=params,
            name="analyse",
        )(device, cut, places, gather_table, local_table, wind_u, wind_v, tracer)

    def exchange(right, left, far):
        def shifted(array, by):
            return lax.ppermute(
                array, "lon", [(i, (i + by) % segments) for i in range(segments)]
            )

        got = [shifted(right, 1), shifted(left, -1)]
        return got + [shifted(far, s) for s in range(2, segments - 1)]

    def combine(near, moments):
        step_tiles = 2
        moment_specs = [
            pl.BlockSpec((step_tiles,) + m.shape[1:], lambda s, d: (s, 0, 0, 0)) for m in moments
        ]
        edge = jax.ShapeDtypeStruct((count, wide), F32)
        return pl.pallas_call(
            functools.partial(combine_kernel, segments, width, per_field),
            out_shape=(
                jax.ShapeDtypeStruct((tiles, LANES, 2 * wide - LANES), BF), edge, edge,
            ),
            grid_spec=pltpu.PrefetchScalarGridSpec(
                num_scalar_prefetch=1,
                grid=(tiles // step_tiles,),
                in_specs=[whole_spec()] * 3
                + [pl.BlockSpec((1,) + far_table.shape[1:], lambda s, d: (d[0], 0, 0))]
                + [pl.BlockSpec((step_tiles, nodes, LANES), lambda s, d: (s, 0, 0))]
                + moment_specs,
                out_specs=(
                    pl.BlockSpec((step_tiles, LANES, 2 * wide - LANES), lambda s, d: (s, 0, 0)),
                    pl.BlockSpec((count, wide), lambda s, d: (0, 0)),
                    pl.BlockSpec((count, wide), lambda s, d: (0, 0)),
                ),
                scratch_shapes=[pltpu.VMEM((2, nodes, LANES), F32)],
            ),
            compiler_params=params,
            name="combine",
        )(device, cut, scale, places, far_table, near, *moments)

    def finish(chunk, pack, above, below, before):
        def pack_spec(field):
            return pl.BlockSpec(
                (1, LANES, 2 * wide - LANES), lambda s: (field * per_field + s, 0, 0)
            )

        start = chunk * nl // pair
        block = pl.BlockSpec((pair, rows, width), lambda s: (start + s, 0, 0))
        return pl.pallas_call(
            finish_kernel,
            out_shape=(jax.ShapeDtypeStruct((levels, rows, width), F32),) * 3,
            grid=(per_field,),
            in_specs=[whole_spec()] * 4
            + [pack_spec(0), pack_spec(1), pack_spec(2), block]
            + [anywhere] * len(before),
            out_specs=(block,) * 3,
            scratch_shapes=[
                pltpu.VMEM((2 * count, lanes), F32),
                pltpu.VMEM((2, rows, LANES), F32),
            ],
            input_output_aliases={8 + i: i for i in range(len(before))},
            compiler_params=params,
            name="finish",
        )(scale, spread_table, above, below, pack, pack, pack, tracer, *before)

    analysed = [analyse(chunk) for chunk in range(CHUNKS)]
    moments = [exchange(*got[1:]) for got in analysed]
    edges, packs = [], []
    for got, moment in zip(analysed, moments):
        pack, top, bottom = combine(got[0], moment)
        above = lax.ppermute(bottom, "lat", [(i, i + 1) for i in range(lats - 1)])
        below = lax.ppermute(top, "lat", [(i + 1, i) for i in range(lats - 1)])
        packs.append(pack)
        edges.append((above, below))
    out = ()
    for chunk in range(CHUNKS):
        out = finish(chunk, packs[chunk], *edges[chunk], out)
    return out


def solution(mesh):
    segments, lats = mesh.shape["lon"], mesh.shape["lat"]
    tables = tuple(make_tables(NLON // segments, segments))
    line = P(None, "lat", "lon")
    return jax.shard_map(
        functools.partial(on_device, segments, lats, tables),
        mesh=mesh,
        in_specs=(line, line, line, P("lat"), P("lat")),
        out_specs=(line, line, line),
        check_vma=False,
    )
```

time: 108 us -> 65.2 us (0.60)
  the two profiles are of different devices: /device:TPU:8 before, /device:TPU:0 now
where the time goes in v2:
time: 65.2 us; the launch traced here: 64.9 us
  Pallas kernels  36.3 us (56%)
  starting transfers between devices  15.5 us (24%)
  waiting for transfers between devices  11 us (17%)
  local copies, waits for them, and re-layouts  1.37 us (2%)
  between operations  0.72 us (1%)
    pallas_call x1, Pallas kernels, analyse(): pl.pallas_call(functools.partial(analyse_kernel, segments, chunk * nl, gr...  16.6 us
    pallas_call x1, Pallas kernels, finish(): pl.pallas_call(finish_kernel, out_shape=(jax.ShapeDtypeStruct((levels, ro...  12.9 us
    ppermute x7, starting transfers between devices, shifted(): lax.ppermute(array, 'lon', [(i, (i + by) % segments) for i in range(segme...  10.7 us
    pallas_call x1, Pallas kernels, combine(): pl.pallas_call(functools.partial(combine_kernel, segments, width, per_fie...  6.81 us
    ppermute x7, waiting for transfers between devices, shifted(): lax.ppermute(array, 'lon', [(i, (i + by) % segments) for i in range(segme...  6.2 us
    ppermute x1, waiting for transfers between devices, on_device(): below = lax.ppermute(top, 'lat', [(i + 1, i) for i in range(lats - 1)])  4.13 us
    ppermute x1, starting transfers between devices, on_device(): above = lax.ppermute(bottom, 'lat', [(i, i + 1) for i in range(lats - 1)])  3.48 us
    unnamed x18, local copies, waits for them, and re-layouts  1.37 us
  transfers between devices with their start and end apart: 9, of which 5 were waited for; matrix products, arithmetic and copies ran while one was open for 0% of the time, Pallas kernels for 0%

profile of v2, /device:TPU:0, one launch (start us, length us, event | category | flops | bytes accessed | tf_op | source)
XLA Modules:
  0.0 64.9 jit_solution(4786252564655636562)
XLA Ops:
  0.6 16.6 %analyse.1 = (f32[12,288,128]{2,1,0:T(8,128)}, f32[12,2,16,128]{3,2,1,0:T(8,128)}, f32[12,2,16,128]{3,2,1,0:T(8,128)}, f32[12,2,8,128]{3,2,1,0:T(8,128)}) custom-call(s32[1]{0:T(128)} %bitcast.1.device_ref, s32[1,64]{1,0:T(1,128)} %bitcast.3, f32[2,288,1]{2,1,0:T(8,128)} %constant.14.clone.places_ref, bf16[576,1500]{1,0:T(8,128)(2,1)} %constant.15.clone.gather_ref, ...), custom_call_target="tpu_custom_call" | custom-call | tf_op jit(solution)/shard_map/analyse/pallas_call | solution.py:359
  17.2 3.9 %collective-permute-start.6 = (f32[12,2,8,128]{3,2,1,0:T(8,128)}, f32[12,2,8,128]{3,2,1,0:T(8,128)S(1)}, u32[]{:S(2)}, u32[]{:S(2)}) collective-permute-start(f32[12,2,8,128]{3,2,1,0:T(8,128)} %get-tuple-element.13), channel_id=1, source_target_pairs={{0,6},{1,7},{2,0},{3,1},{4,2},{5,3},{6,4},{7,5},{8,14},{9,15},{10,... | collective-permute-start | bytes 294920 | tf_op jit(solution)/shard_map/ppermute | solution.py:378
  21.2 0.0 collective-permute-start.5
  21.2 0.6 collective-permute-start
  21.8 2.0 %collective-permute-start.1 = (f32[12,2,16,128]{3,2,1,0:T(8,128)}, f32[12,2,16,128]{3,2,1,0:T(8,128)S(1)}, u32[]{:S(2)}, u32[]{:S(2)}) collective-permute-start(f32[12,2,16,128]{3,2,1,0:T(8,128)} %get-tuple-element.12), channel_id=1, source_target_pairs={{0,7},{1,0},{2,1},{3,2},{4,3},{5,4},{6,5},{7,6},{8,15},{9,8},{10,9... | collective-permute-start | bytes 589832 | tf_op jit(solution)/shard_map/ppermute | solution.py:378
  23.8 1.2 %collective-permute-start.4 = (f32[12,2,8,128]{3,2,1,0:T(8,128)}, f32[12,2,8,128]{3,2,1,0:T(8,128)S(1)}, u32[]{:S(2)}, u32[]{:S(2)}) collective-permute-start(f32[12,2,8,128]{3,2,1,0:T(8,128)} %get-tuple-element.13), channel_id=1, source_target_pairs={{0,4},{1,5},{2,6},{3,7},{4,0},{5,1},{6,2},{7,3},{8,12},{9,13},{10,... | collective-permute-start | bytes 294920 | tf_op jit(solution)/shard_map/ppermute | solution.py:378
  25.0 0.7 %collective-permute-done.5.refs_5_ = f32[12,2,8,128]{3,2,1,0:T(8,128)S(1)} collective-permute-done((f32[12,2,8,128]{3,2,1,0:T(8,128)}, f32[12,2,8,128]{3,2,1,0:T(8,128)S(1)}, u32[]{:S(2)}, u32[]{:S(2)}) %collective-permute-start.5) | collective-permute-done | bytes 98336 | tf_op jit(solution)/shard_map/ppermute | solution.py:378
  25.7 2.9 %collective-permute-start.2 = (f32[12,2,8,128]{3,2,1,0:T(8,128)}, f32[12,2,8,128]{3,2,1,0:T(8,128)S(1)}, u32[]{:S(2)}, u32[]{:S(2)}) collective-permute-start(f32[12,2,8,128]{3,2,1,0:T(8,128)} %get-tuple-element.13), channel_id=1, source_target_pairs={{0,2},{1,3},{2,4},{3,5},{4,6},{5,7},{6,0},{7,1},{8,10},{9,11},{10,... | collective-permute-start | bytes 294920 | tf_op jit(solution)/shard_map/ppermute | solution.py:378
  28.6 5.2 %collective-permute-done.4.refs_4_ = f32[12,2,8,128]{3,2,1,0:T(8,128)S(1)} collective-permute-done((f32[12,2,8,128]{3,2,1,0:T(8,128)}, f32[12,2,8,128]{3,2,1,0:T(8,128)S(1)}, u32[]{:S(2)}, u32[]{:S(2)}) %collective-permute-start.4) | collective-permute-done | bytes 98336 | tf_op jit(solution)/shard_map/ppermute | solution.py:378
  33.9 0.3 collective-permute-done.3.refs_3_
  34.2 0.0 copy-start
  34.2 0.0 copy-start.1
  34.2 0.3 copy-done.4
  34.5 0.3 copy-done.5
  34.8 0.0 copy-done.6
  34.8 0.1 copy-done
  34.9 0.1 copy-done.1
  35.0 6.8 %combine.1 = (bf16[12,128,640]{2,1,0:T(8,128)(2,1)}, f32[24,384]{1,0:T(8,128)}, f32[24,384]{1,0:T(8,128)}) custom-call(s32[1]{0:T(128)} %bitcast.1.device_ref, s32[1,64]{1,0:T(1,128)} %bitcast.4, f32[1,64]{1,0:T(1,128)} %bitcast.5, f32[2,288,1]{2,1,0:T(8,128)} %constant.14.clone.places_ref, bf16[8,288,216]{2,1,0:T(8,128)(2,1)} %constant.17.clone.table_in, ...), custom_call_target="tpu_custom_call" | custom-call | tf_op jit(solution)/shard_map/combine/pallas_call | solution.py:391
  41.8 3.5 %collective-permute-start.7 = (f32[24,384]{1,0:T(8,128)}, f32[24,384]{1,0:T(8,128)S(1)}, u32[]{:S(2)}, u32[]{:S(2)}) collective-permute-start(f32[24,384]{1,0:T(8,128)} %get-tuple-element.14), channel_id=1, source_target_pairs={{0,8},{8,16},{16,24},{1,9},{9,17},{17,25},{2,10},{10,18},{18,26},{... | collective-permute-start | bytes 110600 | tf_op jit(solution)/shard_map/ppermute | solution.py:444
  45.3 1.3 %collective-permute-start.8 = (f32[24,384]{1,0:T(8,128)}, f32[24,384]{1,0:T(8,128)S(1)}, u32[]{:S(2)}, u32[]{:S(2)}) collective-permute-start(f32[24,384]{1,0:T(8,128)} %get-tuple-element.15), channel_id=1, source_target_pairs={{8,0},{16,8},{24,16},{9,1},{17,9},{25,17},{10,2},{18,10},{26,18},{... | collective-permute-start | bytes 110600 | tf_op jit(solution)/shard_map/ppermute | solution.py:445
  46.6 0.6 collective-permute-done.7.above_ref
  47.2 4.1 %collective-permute-done.8.below_ref = f32[24,384]{1,0:T(8,128)S(1)} collective-permute-done((f32[24,384]{1,0:T(8,128)}, f32[24,384]{1,0:T(8,128)S(1)}, u32[]{:S(2)}, u32[]{:S(2)}) %collective-permute-start.8) | collective-permute-done | bytes 36896 | tf_op jit(solution)/shard_map/ppermute | solution.py:445
  51.3 0.6 copy-done.8
  51.9 12.9 %finish.1 = (f32[8,64,1500]{2,1,0:T(8,128)}, f32[8,64,1500]{2,1,0:T(8,128)}, f32[8,64,1500]{2,1,0:T(8,128)}) custom-call(f32[1,64]{1,0:T(1,128)} %bitcast.6, bf16[896,1536]{1,0:T(8,128)(2,1)} %constant.18.clone.spread_ref, f32[24,384]{1,0:T(8,128)} %copy-done.7, f32[24,384]{1,0:T(8,128)} %copy-done.8, ...), custom_call_target="tpu_custom_call" | custom-call | tf_op jit(solution)/shard_map/finish/pallas_call | solution.py:422
  (15 shorter events, 0.0 us)
Async XLA Ops:
  17.2 7.8 %collective-permute-start.6 = (f32[12,2,8,128]{3,2,1,0:T(8,128)}, f32[12,2,8,128]{3,2,1,0:T(8,128)S(1)}, u32[]{:S(2)}, u32[]{:S(2)}) collective-permute-start(f32[12,2,8,128]{3,2,1,0:T(8,128)} %get-tuple-element.13), channel_id=1, source_target_pairs={{0,6},{1,7},{2,0},{3,1},{4,2},{5,3},{6,4},{7,5},{8,14},{9,15},{10,... | collective-permute-start | bytes 294920 | tf_op jit(solution)/shard_map/ppermute | solution.py:378
  21.2 4.5 %collective-permute-start.5 = (f32[12,2,8,128]{3,2,1,0:T(8,128)}, f32[12,2,8,128]{3,2,1,0:T(8,128)S(1)}, u32[]{:S(2)}, u32[]{:S(2)}) collective-permute-start(f32[12,2,8,128]{3,2,1,0:T(8,128)} %get-tuple-element.13), channel_id=1, source_target_pairs={{0,5},{1,6},{2,7},{3,0},{4,1},{5,2},{6,3},{7,4},{8,13},{9,14},{10,... | collective-permute-start | bytes 294920 | tf_op jit(solution)/shard_map/ppermute | solution.py:378
  21.2 13.0 %collective-permute-start = (f32[12,2,16,128]{3,2,1,0:T(8,128)}, f32[12,2,16,128]{3,2,1,0:T(8,128)S(1)}, u32[]{:S(2)}, u32[]{:S(2)}) collective-permute-start(f32[12,2,16,128]{3,2,1,0:T(8,128)} %get-tuple-element.11), channel_id=1, source_target_pairs={{0,1},{1,2},{2,3},{3,4},{4,5},{5,6},{6,7},{7,0},{8,9},{9,10},{10,1... | collective-permute-start | bytes 589832 | tf_op jit(solution)/shard_map/ppermute | solution.py:378
  21.8 12.3 %collective-permute-start.1 = (f32[12,2,16,128]{3,2,1,0:T(8,128)}, f32[12,2,16,128]{3,2,1,0:T(8,128)S(1)}, u32[]{:S(2)}, u32[]{:S(2)}) collective-permute-start(f32[12,2,16,128]{3,2,1,0:T(8,128)} %get-tuple-element.12), channel_id=1, source_target_pairs={{0,7},{1,0},{2,1},{3,2},{4,3},{5,4},{6,5},{7,6},{8,15},{9,8},{10,9... | collective-permute-start | bytes 589832 | tf_op jit(solution)/shard_map/ppermute | solution.py:378
  23.8 10.0 %collective-permute-start.4 = (f32[12,2,8,128]{3,2,1,0:T(8,128)}, f32[12,2,8,128]{3,2,1,0:T(8,128)S(1)}, u32[]{:S(2)}, u32[]{:S(2)}) collective-permute-start(f32[12,2,8,128]{3,2,1,0:T(8,128)} %get-tuple-element.13), channel_id=1, source_target_pairs={{0,4},{1,5},{2,6},{3,7},{4,0},{5,1},{6,2},{7,3},{8,12},{9,13},{10,... | collective-permute-start | bytes 294920 | tf_op jit(solution)/shard_map/ppermute | solution.py:378
  25.0 9.2 %copy-start.2 = (f32[12,2,8,128]{3,2,1,0:T(8,128)}, f32[12,2,8,128]{3,2,1,0:T(8,128)S(1)}, u32[]{:S(2)}) copy-start(f32[12,2,8,128]{3,2,1,0:T(8,128)S(1)} %collective-permute-done.6.refs_6_) | copy-start | bytes 294916
  25.0 9.1 %collective-permute-start.3 = (f32[12,2,8,128]{3,2,1,0:T(8,128)}, f32[12,2,8,128]{3,2,1,0:T(8,128)S(1)}, u32[]{:S(2)}, u32[]{:S(2)}) collective-permute-start(f32[12,2,8,128]{3,2,1,0:T(8,128)} %get-tuple-element.13), channel_id=1, source_target_pairs={{0,3},{1,4},{2,5},{3,6},{4,7},{5,0},{6,1},{7,2},{8,11},{9,12},{10,... | collective-permute-start | bytes 294920 | tf_op jit(solution)/shard_map/ppermute | solution.py:378
  25.7 8.5 %copy-start.3 = (f32[12,2,8,128]{3,2,1,0:T(8,128)}, f32[12,2,8,128]{3,2,1,0:T(8,128)S(1)}, u32[]{:S(2)}) copy-start(f32[12,2,8,128]{3,2,1,0:T(8,128)S(1)} %collective-permute-done.5.refs_5_) | copy-start | bytes 294916
  25.7 8.5 %collective-permute-start.2 = (f32[12,2,8,128]{3,2,1,0:T(8,128)}, f32[12,2,8,128]{3,2,1,0:T(8,128)S(1)}, u32[]{:S(2)}, u32[]{:S(2)}) collective-permute-start(f32[12,2,8,128]{3,2,1,0:T(8,128)} %get-tuple-element.13), channel_id=1, source_target_pairs={{0,2},{1,3},{2,4},{3,5},{4,6},{5,7},{6,0},{7,1},{8,10},{9,11},{10,... | collective-permute-start | bytes 294920 | tf_op jit(solution)/shard_map/ppermute | solution.py:378
  33.9 0.6 copy-start.4
  34.2 0.6 copy-start.5
  34.2 0.7 %copy-start.6 = (f32[12,2,8,128]{3,2,1,0:T(8,128)}, f32[12,2,8,128]{3,2,1,0:T(8,128)S(1)}, u32[]{:S(2)}) copy-start(f32[12,2,8,128]{3,2,1,0:T(8,128)S(1)} %collective-permute-done.2.refs_2_) | copy-start | bytes 294916
  34.2 0.7 %copy-start = (f32[12,2,16,128]{3,2,1,0:T(8,128)}, f32[12,2,16,128]{3,2,1,0:T(8,128)S(1)}, u32[]{:S(2)}) copy-start(f32[12,2,16,128]{3,2,1,0:T(8,128)S(1)} %collective-permute-done.refs_0_) | copy-start | bytes 589828
  34.2 0.8 %copy-start.1 = (f32[12,2,16,128]{3,2,1,0:T(8,128)}, f32[12,2,16,128]{3,2,1,0:T(8,128)S(1)}, u32[]{:S(2)}) copy-start(f32[12,2,16,128]{3,2,1,0:T(8,128)S(1)} %collective-permute-done.1.refs_1_) | copy-start | bytes 589828
  41.8 5.4 %collective-permute-start.7 = (f32[24,384]{1,0:T(8,128)}, f32[24,384]{1,0:T(8,128)S(1)}, u32[]{:S(2)}, u32[]{:S(2)}) collective-permute-start(f32[24,384]{1,0:T(8,128)} %get-tuple-element.14), channel_id=1, source_target_pairs={{0,8},{8,16},{16,24},{1,9},{9,17},{17,25},{2,10},{10,18},{18,26},{... | collective-permute-start | bytes 110600 | tf_op jit(solution)/shard_map/ppermute | solution.py:444
  45.3 6.1 %collective-permute-start.8 = (f32[24,384]{1,0:T(8,128)}, f32[24,384]{1,0:T(8,128)S(1)}, u32[]{:S(2)}, u32[]{:S(2)}) collective-permute-start(f32[24,384]{1,0:T(8,128)} %get-tuple-element.15), channel_id=1, source_target_pairs={{8,0},{16,8},{24,16},{9,1},{17,9},{25,17},{10,2},{18,10},{26,18},{... | collective-permute-start | bytes 110600 | tf_op jit(solution)/shard_map/ppermute | solution.py:445
  47.2 4.1 %copy-start.7 = (f32[24,384]{1,0:T(8,128)}, f32[24,384]{1,0:T(8,128)S(1)}, u32[]{:S(2)}) copy-start(f32[24,384]{1,0:T(8,128)S(1)} %collective-permute-done.7.above_ref) | copy-start | bytes 110596
  51.3 0.6 copy-start.8

commit v3 on v2

v3 whole, which is shorter than its diff:
```python
import functools
import math

import jax
import jax.numpy as jnp
import ml_dtypes
import numpy as np
from jax import lax
from jax.experimental import pallas as pl
from jax.experimental.pallas import tpu as pltpu
from jax.sharding import PartitionSpec as P

NLON = 12000
KMAX = 1024
NEAR = 12
FAR = 4
EXTRA = 32
LANES = 128
CHUNKS = 1
courant = 0.5
BF = jnp.bfloat16
F32 = jnp.float32
VMEM_LIMIT = 56 * 1024 * 1024


def prolate(points, band, count):
    i = np.arange(points)
    diag = ((points - 1 - 2 * i) / 2.0) ** 2 * np.cos(2 * np.pi * band)
    off = i[1:] * (points - i[1:]) / 2.0
    mid = points // 2
    half = (count + 1) // 2
    out = np.zeros((points, 2 * half))
    dd, ee = diag[mid:], off[mid:].copy()
    scaled = ee.copy()
    scaled[0] *= math.sqrt(2.0)
    even = np.linalg.eigh(np.diag(dd) + np.diag(scaled, 1) + np.diag(scaled, -1))[1]
    even = even[:, ::-1][:, :half]
    wing = even[1:] / math.sqrt(2.0)
    out[mid, 0::2] = even[0]
    out[mid + 1 :, 0::2] = wing
    out[:mid, 0::2] = wing[::-1]
    odd = np.linalg.eigh(np.diag(dd[1:]) + np.diag(ee[1:], 1) + np.diag(ee[1:], -1))[1]
    wing = odd[:, ::-1][:, :half] / math.sqrt(2.0)
    out[mid + 1 :, 1::2] = wing
    out[:mid, 1::2] = -wing[::-1]
    return out


def interpolation(low, high, nodes, snap):
    fine = prolate(2 * (high - low) + 1, (KMAX - 0.5) / NLON / 2, nodes + 2)
    wave = fine[:, nodes]
    at = np.nonzero(wave[:-1] * wave[1:] < 0)[0]
    roots = (at + wave[at] / (wave[at] - wave[at + 1]))[: nodes // 2] / 2 + low
    left = snap(roots)
    for i in range(1, len(left)):
        left[i] = max(left[i], left[i - 1] + 1)
    places = np.concatenate([left, (low + high) - left[::-1]])
    kept = nodes - 4
    index = np.round((places - low) * 2).astype(int)
    return places, fine[::2, :kept] @ np.linalg.pinv(fine[index, :kept])


def near_kernel(distance):
    return 1.0 / (NLON * np.sin(np.pi * distance / NLON))


def two_parts(table):
    high = table.astype(np.float32).astype(ml_dtypes.bfloat16)
    low = (table - high.astype(np.float64)).astype(np.float32).astype(ml_dtypes.bfloat16)
    return high, low


@functools.lru_cache(maxsize=4)
def make_tables(width, segments):
    main = -(-2 * KMAX * width // NLON // LANES) * LANES
    nodes = main + EXTRA
    source, gather = interpolation(0, width - 1, nodes, np.round)
    target, spread = interpolation(-1, width, nodes, lambda r: np.floor(r) + 0.5)
    local = near_kernel(target[:, None] - source[None])
    offsets = [d for d in range(-(segments - 1), segments) if d]
    far = {d: near_kernel(target[:, None] + width * d - source[None]) for d in offsets}

    def leading(kernel, count):
        found = np.linalg.svd(kernel, full_matrices=False)[2][:count]
        peak = np.take_along_axis(found, np.abs(found).argmax(1)[:, None], 1)
        return found * np.sign(peak)

    ahead = range(1, segments)
    basis = {s: leading(far[s], FAR) for s in ahead}
    for s in (1, segments - 1):
        both = leading(far[s], FAR + NEAR)
        basis[s], basis[-s] = both[:FAR], both[FAR:]

    high, low = two_parts(gather.T)
    gather_table = np.concatenate([high, low], 0)
    more = [basis[-1], basis[1 - segments]] + [basis[s] for s in ahead]
    rows = np.concatenate([local] + more, 0)
    rows = np.pad(rows, ((0, -len(rows) % 8), (0, 0)))
    high, low = two_parts(rows)
    local_table = np.concatenate([high, low, high], 1)
    blocks = []
    for d in range(segments):
        pieces = [far[d - (d - s) % segments] @ basis[-s].T for s in (1, segments - 1)]
        for e in range(segments):
            if e == d:
                pieces.append(np.zeros((nodes, FAR)))
            else:
                pieces.append(far[d - e] @ basis[(d - e) % segments].T)
        top = [p for piece in pieces for p in (piece, 0 * piece)]
        low_part = [p for piece in pieces for p in (0 * piece, piece)]
        both = np.concatenate([np.concatenate(top, 1), np.concatenate(low_part, 1)], 0)
        high, low = two_parts(both)
        blocks.append(np.concatenate([high, low, high], 1))
    far_table = np.stack(blocks)
    lanes = -(-(width + 2) // LANES) * LANES
    wide = np.zeros((nodes, lanes))
    wide[:, : width + 1] = spread.T[:, 1:]
    wide[:, lanes - 1] = spread.T[:, 0]
    high, low = two_parts(wide)
    none = np.zeros((LANES - 3 * EXTRA, lanes), high.dtype)
    spread_table = np.concatenate(
        [high[:main], low[:main], high[:main], high[main:], low[main:], high[main:], none], 0
    )
    places = np.stack([2 * source - width, 2 * target - width]).astype(np.float32)
    return gather_table, local_table, far_table, spread_table, places[:, :, None]


def phases(cut, places, device, segments, width):
    full = 4.0 * NLON
    odd = 2.0 * cut - 1.0
    inner = odd * places
    inner = inner - full * jnp.floor(inner * (1.0 / full) + 0.5)
    base = odd * (2.0 * device + 1.0)
    cycle = 4.0 * segments
    base = (base - cycle * jnp.floor(base * (1.0 / cycle))) * float(width)
    total = inner + base
    total = total - full * jnp.floor(total * (1.0 / full) + 0.5)
    quarter = jnp.floor(total * (4.0 / full) + 0.5)
    x = (total - (full / 4.0) * quarter) * (2.0 * math.pi / full)
    y = x * x
    sine = x + x * y * (
        -1.0 / 6 + y * (1.0 / 120 + y * (-1.0 / 5040 + y * (1.0 / 362880)))
    )
    cosine = 1.0 + y * (
        -0.5 + y * (1.0 / 24 + y * (-1.0 / 720 + y * (1.0 / 40320 + y * (-1.0 / 3628800))))
    )
    odd_quarter = jnp.abs(quarter) == 1.0
    turned_c = jnp.where(odd_quarter, -quarter * sine, cosine)
    turned_s = jnp.where(odd_quarter, quarter * cosine, sine)
    flip = jnp.where(jnp.abs(quarter) == 2.0, -1.0, 1.0)
    return turned_c * flip, turned_s * flip


def parts(values):
    high = values.astype(BF)
    return high, (values - high.astype(F32)).astype(BF)


def stacked(values):
    high, low = parts(values)
    return jnp.concatenate([high, high, low], axis=0)


def product(a, b, dims):
    return lax.dot_general(a, b, (dims, ((), ())), preferred_element_type=F32)


def lane_cut(cut_ref):
    cut = cut_ref[...].astype(F32)
    return jnp.concatenate([cut] * (LANES // cut.shape[1]), axis=1)


def packed(values):
    main = values.shape[1] - LANES
    high, low = parts(values)
    last, last_low = high[:, main:].astype(F32), low[:, main:].astype(F32)
    last = last + pltpu.roll(last, EXTRA, 1) + pltpu.roll(last_low, 2 * EXTRA, 1)
    return jnp.concatenate([high[:, :main], low[:, :main], last.astype(BF)], axis=1)


def spread_lines(pack, spread_ref):
    main = (pack.shape[1] - LANES) // 2
    held = jnp.concatenate([pack[:, :main], pack], axis=1)
    return product(held, spread_ref[...], ((1,), (0,)))


def analyse_kernel(
    segments, first, groups, device_ref, cut_ref, places_ref, gather_ref, local_ref,
    u_ref, v_ref, q_ref, near_ref, ahead_ref, behind_ref, every_ref, turn_ref,
    lines_ref, high_ref, low_ref, held_ref, table_ref, sems,
):
    width = u_ref.shape[2]
    steps, levels, rows, _ = lines_ref.shape
    lines = levels * rows
    nodes = gather_ref.shape[0] // 2
    me = device_ref[0]

    copies = []
    for step in range(steps):
        ref = (u_ref, v_ref, q_ref)[step // groups]
        levels_at = pl.ds(first + (step % groups) * levels, levels)
        copies.append(pltpu.make_async_copy(ref.at[levels_at], lines_ref.at[step], sems.at[step]))
        copies[-1].start()
    for side in range(2):
        cosine, sine = phases(
            lane_cut(cut_ref), places_ref[side], me.astype(F32), segments, width
        )
        if side == 0:
            table_ref[0], table_ref[1] = cosine, sine
        else:
            turn_ref[0], turn_ref[1] = cosine, sine
    every_ref[me] = jnp.zeros(every_ref.shape[1:], F32)

    def cast(step):
        values = lines_ref[step].reshape(lines, width)
        high, low = parts(values)
        high_ref[step % 2] = high
        low_ref[step % 2] = low

    def gather(step):
        both = product(gather_ref[...], high_ref[step % 2], ((1,), (1,)))
        rest = product(gather_ref[:nodes], low_ref[step % 2], ((1,), (1,)))
        held_ref[step % 2] = both[:nodes] + both[nodes:] + rest

    def local(step):
        for part in range(lines // LANES):
            tile = step * (lines // LANES) + part
            mine = held_ref[step % 2, :, part * LANES : (part + 1) * LANES]
            turned = jnp.concatenate([mine * table_ref[0], mine * table_ref[1]], axis=1)
            out = product(local_ref[...], stacked(turned), ((1,), (0,)))
            near_ref[tile] = (
                turn_ref[1] * out[:nodes, :LANES] - turn_ref[0] * out[:nodes, LANES:]
            )
            at = nodes
            for ref in (ahead_ref, behind_ref):
                ref[tile, :NEAR] = out[at : at + NEAR, :LANES]
                ref[tile, NEAR:] = out[at : at + NEAR, LANES:]
                at += NEAR
            for s in range(1, segments):
                to = lax.rem(me + s, segments)
                every_ref[to, tile, :FAR] = out[at : at + FAR, :LANES]
                every_ref[to, tile, FAR:] = out[at : at + FAR, LANES:]
                at += FAR

    copies[0].wait()
    cast(0)
    for step in range(steps):
        if step + 1 < steps:
            copies[step + 1].wait()
        gather(step)
        if step + 1 < steps:
            cast(step + 1)
        if step > 0:
            local(step - 1)
    local(steps - 1)


def combine_kernel(
    per_field, rows, device_ref, scale_ref, turn_ref, table_in, near_ref, behind_ref, ahead_ref,
    every_ref, pack_ref, top_ref, bottom_ref,
):
    step = pl.program_id(0)
    tiles, nodes, _ = near_ref.shape
    segments = every_ref.shape[0]
    columns = []
    for tile in range(tiles):
        pieces = [behind_ref[tile], ahead_ref[tile]]
        pieces += [every_ref[e, tile] for e in range(segments)]
        columns.append(jnp.concatenate(pieces, axis=0))
    got = product(table_in[0], stacked(jnp.concatenate(columns, axis=1)), ((1,), (0,)))
    inverse = 1.0 / scale_ref[...]
    none = jnp.zeros((LANES - EXTRA, LANES), F32)
    for tile in range(tiles):
        at = tile * LANES
        cosine, sine = got[:nodes, at : at + LANES], got[nodes:, at : at + LANES]
        values = near_ref[tile] + turn_ref[1] * cosine - turn_ref[0] * sine
        values = jnp.transpose(jnp.concatenate([values, none], axis=0))
        pack_ref[tile] = packed(values)
        number = step * tiles + tile
        wind = number < 2 * per_field
        top_weight = jnp.where(wind, inverse[:, :1], 1.0)
        bottom_weight = jnp.where(wind, inverse[:, rows - 1 :], 1.0)
        pair = LANES // rows
        for part in range(pair):
            line = number * pair + part
            top_ref[pl.ds(line, 1), :] = values[part * rows : part * rows + 1] * top_weight
            last = part * rows + rows - 1
            bottom_ref[pl.ds(line, 1), :] = values[last : last + 1] * bottom_weight


def finish_kernel(
    first, scale_ref, spread_ref, above_ref, below_ref, pack_ref, tracer_ref, *refs
):
    outs = refs[-9:-6]
    filtered_ref, edge_ref, column_ref, held_ref, load_sems, sems = refs[-6:]
    _, rows, width = tracer_ref.shape
    lanes = spread_ref.shape[1]
    count = above_ref.shape[0]
    levels = count // 3
    pair = LANES // rows
    steps = levels // pair
    tracer_slot = 6 * pair

    def load(step):
        return pltpu.make_async_copy(
            tracer_ref.at[pl.ds(first + step * pair, pair)],
            held_ref.at[pl.ds(tracer_slot + step % 2 * pair, pair)],
            load_sems.at[step % 2],
        )

    def store(step, number):
        return pltpu.make_async_copy(
            held_ref.at[pl.ds((3 * (step % 2) + number) * pair, pair)],
            outs[number].at[pl.ds(first + step * pair, pair)],
            sems.at[step % 2, number],
        )

    load(0).start()
    edges = jnp.concatenate([above_ref[...], below_ref[...]], axis=0)
    edge_ref[...] = spread_lines(packed(edges), spread_ref)
    here = lax.broadcasted_iota(jnp.int32, (rows, rows), 0)
    there = lax.broadcasted_iota(jnp.int32, (rows, rows), 1)
    column = jnp.where(here == there, jnp.broadcast_to(scale_ref[...], (rows, rows)), 0.0)
    column = jnp.sum(column, axis=1, keepdims=True)
    column_ref[0] = jnp.broadcast_to(column, (rows, LANES))
    column_ref[1] = 1.0 / column_ref[0]
    row_number = lax.broadcasted_iota(jnp.int32, (rows, 1), 0)

    def fill(step):
        pack = jnp.concatenate([pack_ref[f * steps + step] for f in range(3)], axis=0)
        filtered_ref[step % 2] = spread_lines(pack, spread_ref)

    def east_west(values):
        return pltpu.roll(values, lanes - 1, 1) - pltpu.roll(values, 1, 1)

    def stencil(step):
        scale = column_ref[0][:, :1]
        inverse = column_ref[1][:, :1]
        for part in range(pair):
            level = step * pair + part

            def field(number):
                at = number * pair * rows + part * rows
                return filtered_ref[step % 2, at : at + rows]

            def north_south(values, number):
                at = number * levels + level
                above = edge_ref[at : at + 1]
                below = edge_ref[count + at : count + at + 1]
                later = jnp.where(row_number == rows - 1, below, pltpu.roll(values, rows - 1, 0))
                earlier = jnp.where(row_number == 0, above, pltpu.roll(values, 1, 0))
                return later - earlier

            u, v, q = field(0), field(1), field(2)
            div = scale * (east_west(u) + north_south(v * inverse, 1))
            vort = scale * (east_west(v) - north_south(u * inverse, 0))
            change = courant * (u * scale * east_west(q) + v * north_south(q, 2))
            base = 3 * (step % 2) * pair + part
            held_ref[base] = held_ref[tracer_slot + step % 2 * pair + part] - change[:, :width]
            held_ref[base + pair] = div[:, :width]
            held_ref[base + 2 * pair] = vort[:, :width]

    fill(0)
    for step in range(steps):
        if step + 1 < steps:
            load(step + 1).start()
        load(step).wait()
        if step >= 2:
            for number in range(3):
                store(step - 2, number).wait()
        stencil(step)
        if step + 1 < steps:
            fill(step + 1)
        for number in range(3):
            store(step, number).start()
    for step in range(max(steps - 2, 0), steps):
        for number in range(3):
            store(step, number).wait()


def whole_spec():
    return pl.BlockSpec(memory_space=pltpu.VMEM)


def on_device(segments, lats, tables, wind_u, wind_v, tracer, cutoff, row_scale):
    levels, rows, width = wind_u.shape
    gather_table, local_table, far_table, spread_table, places = tables
    nodes = gather_table.shape[0] // 2
    lanes = spread_table.shape[1]
    wide = nodes - EXTRA + LANES
    nl = levels // CHUNKS
    pair = LANES // rows
    group = 2 * pair
    groups = nl // group
    tiles = 3 * nl // pair
    per_field = nl // pair
    count = 3 * nl
    device = lax.axis_index("lon").astype(jnp.int32)[None]
    cut = cutoff.reshape(1, rows)
    scale = row_scale.reshape(1, rows)

    smem = pl.BlockSpec(memory_space=pltpu.SMEM)
    anywhere = pl.BlockSpec(memory_space=pl.ANY)
    params = pltpu.CompilerParams(
        dimension_semantics=("arbitrary",), vmem_limit_bytes=VMEM_LIMIT
    )
    flat = pltpu.CompilerParams(vmem_limit_bytes=VMEM_LIMIT)

    def analyse(chunk):
        steps = 3 * groups
        extra = jax.ShapeDtypeStruct((tiles, 2 * NEAR, LANES), F32)
        return pl.pallas_call(
            functools.partial(analyse_kernel, segments, chunk * nl, groups),
            out_shape=(
                jax.ShapeDtypeStruct((tiles, nodes, LANES), F32),
                extra,
                extra,
                jax.ShapeDtypeStruct((segments, tiles, 2 * FAR, LANES), F32),
                jax.ShapeDtypeStruct((2, nodes, LANES), F32),
            ),
            in_specs=[smem] + [whole_spec()] * 4 + [anywhere] * 3,
            out_specs=(whole_spec(),) * 5,
            scratch_shapes=[
                pltpu.VMEM((steps, group, rows, width), F32),
                pltpu.VMEM((2, group * rows, width), BF),
                pltpu.VMEM((2, group * rows, width), BF),
                pltpu.VMEM((2, nodes, group * rows), F32),
                pltpu.VMEM((2, nodes, LANES), F32),
                pltpu.SemaphoreType.DMA((steps,)),
            ],
            compiler_params=flat,
            name="analyse",
        )(device, cut, places, gather_table, local_table, wind_u, wind_v, tracer)

    def exchange(ahead, behind, every):
        def shifted(array, by):
            return lax.ppermute(
                array, "lon", [(i, (i + by) % segments) for i in range(segments)]
            )

        got = lax.all_to_all(every, "lon", 0, 0)
        return shifted(ahead, 1), shifted(behind, -1), got

    def combine(near, turn, moments):
        step_tiles = 4
        edge = jax.ShapeDtypeStruct((count, wide), F32)
        extra_spec = pl.BlockSpec((step_tiles, 2 * NEAR, LANES), lambda s, d: (s, 0, 0))
        return pl.pallas_call(
            functools.partial(combine_kernel, per_field, rows),
            out_shape=(
                jax.ShapeDtypeStruct((tiles, LANES, 2 * wide - LANES), BF), edge, edge,
            ),
            grid_spec=pltpu.PrefetchScalarGridSpec(
                num_scalar_prefetch=1,
                grid=(tiles // step_tiles,),
                in_specs=[whole_spec()] * 2
                + [pl.BlockSpec((1,) + far_table.shape[1:], lambda s, d: (d[0], 0, 0))]
                + [pl.BlockSpec((step_tiles, nodes, LANES), lambda s, d: (s, 0, 0))]
                + [extra_spec, extra_spec]
                + [
                    pl.BlockSpec(
                        (segments, step_tiles, 2 * FAR, LANES), lambda s, d: (0, s, 0, 0)
                    )
                ],
                out_specs=(
                    pl.BlockSpec((step_tiles, LANES, 2 * wide - LANES), lambda s, d: (s, 0, 0)),
                    pl.BlockSpec((count, wide), lambda s, d: (0, 0)),
                    pl.BlockSpec((count, wide), lambda s, d: (0, 0)),
                ),
            ),
            compiler_params=params,
            name="combine",
        )(device, scale, turn, far_table, near, *moments)

    def finish(chunk, pack, above, below, before):
        return pl.pallas_call(
            functools.partial(finish_kernel, chunk * nl),
            out_shape=(jax.ShapeDtypeStruct((levels, rows, width), F32),) * 3,
            in_specs=[whole_spec()] * 5 + [anywhere] * (1 + len(before)),
            out_specs=(anywhere,) * 3,
            scratch_shapes=[
                pltpu.VMEM((2, 3 * LANES, lanes), F32),
                pltpu.VMEM((2 * count, lanes), F32),
                pltpu.VMEM((2, rows, LANES), F32),
                pltpu.VMEM((8 * pair, rows, width), F32),
                pltpu.SemaphoreType.DMA((2,)),
                pltpu.SemaphoreType.DMA((2, 3)),
            ],
            input_output_aliases={6 + i: i for i in range(len(before))},
            compiler_params=flat,
            name="finish",
        )(scale, spread_table, above, below, pack, tracer, *before)

    analysed = [analyse(chunk) for chunk in range(CHUNKS)]
    moments = [exchange(*got[1:4]) for got in analysed]
    edges, packs = [], []
    for got, moment in zip(analysed, moments):
        pack, top, bottom = combine(got[0], got[4], moment)
        above = lax.ppermute(bottom, "lat", [(i, i + 1) for i in range(lats - 1)])
        below = lax.ppermute(top, "lat", [(i + 1, i) for i in range(lats - 1)])
        packs.append(pack)
        edges.append((above, below))
    out = ()
    for chunk in range(CHUNKS):
        out = finish(chunk, packs[chunk], *edges[chunk], out)
    return out


def solution(mesh):
    segments, lats = mesh.shape["lon"], mesh.shape["lat"]
    tables = tuple(make_tables(NLON // segments, segments))
    line = P(None, "lat", "lon")
    return jax.shard_map(
        functools.partial(on_device, segments, lats, tables),
        mesh=mesh,
        in_specs=(line, line, line, P("lat"), P("lat")),
        out_specs=(line, line, line),
        check_vma=False,
    )
```

time: 65.2 us -> 62 us (0.951)
  starting transfers between devices: 15.5 us -> 12.8 us
  Pallas kernels: 36.3 us -> 33.7 us
  waiting for transfers between devices: 11 us -> 12.9 us
    ppermute x7 -> x2, starting transfers between devices: 10.7 us -> 2.69 us  [shifted(): lax.ppermute(array, 'lon', [(i, (i + by) % segments) for i in range(segme...]
    all_to_all x0 -> x1, starting transfers between devices: none -> 5.18 us  [exchange(): got = lax.all_to_all(every, 'lon', 0, 0)]
    ppermute x7 -> x2, waiting for transfers between devices: 6.2 us -> 8.33 us  [shifted(): lax.ppermute(array, 'lon', [(i, (i + by) % segments) for i in range(segme...]
    pallas_call x2, Pallas kernels: 19.7 us -> 18.1 us  [the longest x1 12.6 us: finish(): pl.pallas_call(functools.partial(finish_kernel, chunk * nl), out_shape=(j...]
    pallas_call x1, Pallas kernels: 16.6 us -> 15.6 us  [analyse(): pl.pallas_call(functools.partial(analyse_kernel, segments, chunk * nl, gr...]
    unnamed x18 -> x10, local copies, waits for them, and re-layouts: 1.37 us -> 1.43 us
  transfers between devices with their start and end apart: 9 -> 5, of which waited for: 5 -> 3; matrix products, arithmetic and copies ran while one was open for 0% -> 0% of each run, Pallas kernels for 0% -> 0%
where the time goes in v3:
time: 62 us; the launch traced here: 61.7 us
  Pallas kernels  33.7 us (54%)
  waiting for transfers between devices  12.9 us (21%)
  starting transfers between devices  12.8 us (21%)
  local copies, waits for them, and re-layouts  1.43 us (2%)
  between operations  0.84 us (1%)
    pallas_call x1, Pallas kernels, analyse(): pl.pallas_call(functools.partial(analyse_kernel, segments, chunk * nl, gr...  15.6 us
    pallas_call x1, Pallas kernels, finish(): pl.pallas_call(functools.partial(finish_kernel, chunk * nl), out_shape=(j...  12.6 us
    ppermute x2, waiting for transfers between devices, shifted(): lax.ppermute(array, 'lon', [(i, (i + by) % segments) for i in range(segme...  8.33 us
    pallas_call x1, Pallas kernels, combine(): pl.pallas_call(functools.partial(combine_kernel, per_field, rows), out_sh...  5.45 us
    all_to_all x1, starting transfers between devices, exchange(): got = lax.all_to_all(every, 'lon', 0, 0)  5.18 us
    ppermute x1, waiting for transfers between devices, on_device(): below = lax.ppermute(top, 'lat', [(i + 1, i) for i in range(lats - 1)])  4.13 us
    ppermute x1, starting transfers between devices, on_device(): above = lax.ppermute(bottom, 'lat', [(i, i + 1) for i in range(lats - 1)])  3.46 us
    ppermute x2, starting transfers between devices, shifted(): lax.ppermute(array, 'lon', [(i, (i + by) % segments) for i in range(segme...  2.69 us
  transfers between devices with their start and end apart: 5, of which 3 were waited for; matrix products, arithmetic and copies ran while one was open for 0% of the time, Pallas kernels for 0%

profile of v3, /device:TPU:0, one launch (start us, length us, event | category | flops | bytes accessed | tf_op | source)
XLA Modules:
  0.0 61.7 jit_solution(13434960583095055912)
XLA Ops:
  0.6 15.6 %analyse.1 = (f32[12,288,128]{2,1,0:T(8,128)}, f32[12,24,128]{2,1,0:T(8,128)}, f32[12,24,128]{2,1,0:T(8,128)}, f32[8,12,8,128]{3,2,1,0:T(8,128)}, f32[2,288,128]{2,1,0:T(8,128)}) custom-call(s32[1]{0:T(128)} %bitcast.1.device_ref, s32[1,64]{1,0:T(1,128)} %bitcast.5, f32[2,288,1]{2,1,0:T(8,128)} %constant.14.clone.places_ref, ...), custom_call_target="tpu_custom_call" | custom-call | tf_op jit(solution)/shard_map/analyse/pallas_call | solution.py:412
  16.3 5.2 %all-to-all-start = ((f32[8,12,8,128]{3,2,1,0:T(8,128)}), f32[8,12,8,128]{3,2,1,0:T(8,128)S(1)}, u32[]{:S(2)}, u32[]{:S(2)}) async-start(f32[8,12,8,128]{3,2,1,0:T(8,128)} %get-tuple-element.15), calls=%async_computation | async-start | bytes 786432 | tf_op jit(solution)/shard_map/all_to_all | solution.py:441
  21.4 0.5 collective-permute-start
  21.9 2.2 %collective-permute-start.1 = (f32[12,24,128]{2,1,0:T(8,128)}, f32[12,24,128]{2,1,0:T(8,128)S(1)}, u32[]{:S(2)}, u32[]{:S(2)}) collective-permute-start(f32[12,24,128]{2,1,0:T(8,128)} %get-tuple-element.14), channel_id=1, source_target_pairs={{0,7},{1,0},{2,1},{3,2},{4,3},{5,4},{6,5},{7,6},{8,15},{9,8},{10,9... | collective-permute-start | bytes 442376 | tf_op jit(solution)/shard_map/ppermute | solution.py:437
  24.1 8.3 %collective-permute-done.behind_ref = f32[12,24,128]{2,1,0:T(8,128)S(1)} collective-permute-done((f32[12,24,128]{2,1,0:T(8,128)}, f32[12,24,128]{2,1,0:T(8,128)S(1)}, u32[]{:S(2)}, u32[]{:S(2)}) %collective-permute-start) | collective-permute-done | bytes 147488 | tf_op jit(solution)/shard_map/ppermute | solution.py:437
  32.5 0.0 copy-start.1
  32.5 0.0 collective-permute-done.1.ahead_ref
  32.5 0.0 copy-start.2
  32.5 0.0 all-to-all-done.every_ref
  32.5 0.0 copy-start
  32.5 0.6 %copy-done.1 = f32[12,24,128]{2,1,0:T(8,128)} copy-done((f32[12,24,128]{2,1,0:T(8,128)}, f32[12,24,128]{2,1,0:T(8,128)S(1)}, u32[]{:S(2)}) %copy-start.1) | copy-done | bytes 147480
  33.1 0.1 copy-done.2
  33.2 0.1 copy-done
  33.3 5.4 %combine.1 = (bf16[12,128,640]{2,1,0:T(8,128)(2,1)}, f32[24,384]{1,0:T(8,128)}, f32[24,384]{1,0:T(8,128)}) custom-call(s32[1]{0:T(128)} %bitcast.1.device_ref, f32[1,64]{1,0:T(1,128)} %bitcast.3, f32[2,288,128]{2,1,0:T(8,128)} %get-tuple-element.11.turn_ref, bf16[8,576,336]{2,1,0:T(8,128)(2,1)} %constant.17.clone.table_in, ...), custom_call_target="tpu_custom_call" | custom-call | tf_op jit(solution)/shard_map/combine/pallas_call | solution.py:448
  38.8 3.5 %collective-permute-start.2 = (f32[24,384]{1,0:T(8,128)}, f32[24,384]{1,0:T(8,128)S(1)}, u32[]{:S(2)}, u32[]{:S(2)}) collective-permute-start(f32[24,384]{1,0:T(8,128)} %get-tuple-element.16), channel_id=1, source_target_pairs={{0,8},{8,16},{16,24},{1,9},{9,17},{17,25},{2,10},{10,18},{18,26},{... | collective-permute-start | bytes 110600 | tf_op jit(solution)/shard_map/ppermute | solution.py:499
  42.2 1.5 %collective-permute-start.3 = (f32[24,384]{1,0:T(8,128)}, f32[24,384]{1,0:T(8,128)S(1)}, u32[]{:S(2)}, u32[]{:S(2)}) collective-permute-start(f32[24,384]{1,0:T(8,128)} %get-tuple-element.17), channel_id=1, source_target_pairs={{8,0},{16,8},{24,16},{9,1},{17,9},{25,17},{10,2},{18,10},{26,18},{... | collective-permute-start | bytes 110600 | tf_op jit(solution)/shard_map/ppermute | solution.py:500
  43.7 0.5 collective-permute-done.2.above_ref
  44.1 0.0 copy-start.3
  44.1 4.1 %collective-permute-done.3.below_ref = f32[24,384]{1,0:T(8,128)S(1)} collective-permute-done((f32[24,384]{1,0:T(8,128)}, f32[24,384]{1,0:T(8,128)S(1)}, u32[]{:S(2)}, u32[]{:S(2)}) %collective-permute-start.3) | collective-permute-done | bytes 36896 | tf_op jit(solution)/shard_map/ppermute | solution.py:500
  48.3 0.0 copy-start.4
  48.3 0.0 copy-done.3
  48.3 0.6 copy-done.4
  48.9 12.6 %finish.1 = (f32[8,64,1500]{2,1,0:T(8,128)}, f32[8,64,1500]{2,1,0:T(8,128)}, f32[8,64,1500]{2,1,0:T(8,128)}) custom-call(f32[1,64]{1,0:T(1,128)} %bitcast.4, bf16[896,1536]{1,0:T(8,128)(2,1)} %constant.18.clone.spread_ref, f32[24,384]{1,0:T(8,128)} %copy-done.3, f32[24,384]{1,0:T(8,128)} %copy-done.4, bf16[12,128,640]{2,1,0:T(8,128)(2,1)} %get-tuple-element.18.pack_ref, ...), custom_call_target="tpu_custom_call" | custom-call | tf_op jit(solution)/shard_map/finish/pallas_call | solution.py:476
Async XLA Ops:
  16.3 16.2 %all-to-all-start = ((f32[8,12,8,128]{3,2,1,0:T(8,128)}), f32[8,12,8,128]{3,2,1,0:T(8,128)S(1)}, u32[]{:S(2)}, u32[]{:S(2)}) async-start(f32[8,12,8,128]{3,2,1,0:T(8,128)} %get-tuple-element.15), calls=%async_computation | async-start | bytes 786432 | tf_op jit(solution)/shard_map/all_to_all | solution.py:441
  21.4 11.0 %collective-permute-start = (f32[12,24,128]{2,1,0:T(8,128)}, f32[12,24,128]{2,1,0:T(8,128)S(1)}, u32[]{:S(2)}, u32[]{:S(2)}) collective-permute-start(f32[12,24,128]{2,1,0:T(8,128)} %get-tuple-element.13), channel_id=1, source_target_pairs={{0,1},{1,2},{2,3},{3,4},{4,5},{5,6},{6,7},{7,0},{8,9},{9,10},{10,1... | collective-permute-start | bytes 442376 | tf_op jit(solution)/shard_map/ppermute | solution.py:437
  21.9 10.5 %collective-permute-start.1 = (f32[12,24,128]{2,1,0:T(8,128)}, f32[12,24,128]{2,1,0:T(8,128)S(1)}, u32[]{:S(2)}, u32[]{:S(2)}) collective-permute-start(f32[12,24,128]{2,1,0:T(8,128)} %get-tuple-element.14), channel_id=1, source_target_pairs={{0,7},{1,0},{2,1},{3,2},{4,3},{5,4},{6,5},{7,6},{8,15},{9,8},{10,9... | collective-permute-start | bytes 442376 | tf_op jit(solution)/shard_map/ppermute | solution.py:437
  32.5 0.7 %copy-start.1 = (f32[12,24,128]{2,1,0:T(8,128)}, f32[12,24,128]{2,1,0:T(8,128)S(1)}, u32[]{:S(2)}) copy-start(f32[12,24,128]{2,1,0:T(8,128)S(1)} %collective-permute-done.behind_ref) | copy-start | bytes 442372
  32.5 0.7 %copy-start.2 = (f32[12,24,128]{2,1,0:T(8,128)}, f32[12,24,128]{2,1,0:T(8,128)S(1)}, u32[]{:S(2)}) copy-start(f32[12,24,128]{2,1,0:T(8,128)S(1)} %collective-permute-done.1.ahead_ref) | copy-start | bytes 442372
  32.5 0.8 %copy-start = (f32[8,12,8,128]{3,2,1,0:T(8,128)}, f32[8,12,8,128]{3,2,1,0:T(8,128)S(1)}, u32[]{:S(2)}) copy-start(f32[8,12,8,128]{3,2,1,0:T(8,128)S(1)} %all-to-all-done.every_ref) | copy-start | bytes 1179652
  38.8 5.4 %collective-permute-start.2 = (f32[24,384]{1,0:T(8,128)}, f32[24,384]{1,0:T(8,128)S(1)}, u32[]{:S(2)}, u32[]{:S(2)}) collective-permute-start(f32[24,384]{1,0:T(8,128)} %get-tuple-element.16), channel_id=1, source_target_pairs={{0,8},{8,16},{16,24},{1,9},{9,17},{17,25},{2,10},{10,18},{18,26},{... | collective-permute-start | bytes 110600 | tf_op jit(solution)/shard_map/ppermute | solution.py:499
  42.2 6.1 %collective-permute-start.3 = (f32[24,384]{1,0:T(8,128)}, f32[24,384]{1,0:T(8,128)S(1)}, u32[]{:S(2)}, u32[]{:S(2)}) collective-permute-start(f32[24,384]{1,0:T(8,128)} %get-tuple-element.17), channel_id=1, source_target_pairs={{8,0},{16,8},{24,16},{9,1},{17,9},{25,17},{10,2},{18,10},{26,18},{... | collective-permute-start | bytes 110600 | tf_op jit(solution)/shard_map/ppermute | solution.py:500
  44.1 4.1 %copy-start.3 = (f32[24,384]{1,0:T(8,128)}, f32[24,384]{1,0:T(8,128)S(1)}, u32[]{:S(2)}) copy-start(f32[24,384]{1,0:T(8,128)S(1)} %collective-permute-done.2.above_ref) | copy-start | bytes 110596
  48.3 0.6 copy-start.4

commit v4 on v3

--- a/solution.py
+++ b/solution.py
@@ -16,7 +16,8 @@
 FAR = 4
 EXTRA = 32
 LANES = 128
-CHUNKS = 1
+SPAN = 512
+CHUNKS = 2
 courant = 0.5
 BF = jnp.bfloat16
 F32 = jnp.float32
@@ -178,10 +179,10 @@
     return jnp.concatenate([high[:, :main], low[:, :main], last.astype(BF)], axis=1)
 
 
-def spread_lines(pack, spread_ref):
+def spread_lines(pack, spread_ref, columns):
     main = (pack.shape[1] - LANES) // 2
     held = jnp.concatenate([pack[:, :main], pack], axis=1)
-    return product(held, spread_ref[...], ((1,), (0,)))
+    return product(held, spread_ref[:, columns], ((1,), (0,)))
 
 
 def analyse_kernel(
@@ -211,48 +212,52 @@
             turn_ref[0], turn_ref[1] = cosine, sine
     every_ref[me] = jnp.zeros(every_ref.shape[1:], F32)
 
-    def cast(step):
-        values = lines_ref[step].reshape(lines, width)
+    spans = [slice(at, min(at + SPAN, width)) for at in range(0, width, SPAN)]
+
+    def cast(step, span):
+        values = lines_ref[step, :, :, span].reshape(lines, span.stop - span.start)
         high, low = parts(values)
-        high_ref[step % 2] = high
-        low_ref[step % 2] = low
-
-    def gather(step):
-        both = product(gather_ref[...], high_ref[step % 2], ((1,), (1,)))
-        rest = product(gather_ref[:nodes], low_ref[step % 2], ((1,), (1,)))
-        held_ref[step % 2] = both[:nodes] + both[nodes:] + rest
-
-    def local(step):
-        for part in range(lines // LANES):
-            tile = step * (lines // LANES) + part
-            mine = held_ref[step % 2, :, part * LANES : (part + 1) * LANES]
-            turned = jnp.concatenate([mine * table_ref[0], mine * table_ref[1]], axis=1)
-            out = product(local_ref[...], stacked(turned), ((1,), (0,)))
-            near_ref[tile] = (
-                turn_ref[1] * out[:nodes, :LANES] - turn_ref[0] * out[:nodes, LANES:]
-            )
-            at = nodes
-            for ref in (ahead_ref, behind_ref):
-                ref[tile, :NEAR] = out[at : at + NEAR, :LANES]
-                ref[tile, NEAR:] = out[at : at + NEAR, LANES:]
-                at += NEAR
-            for s in range(1, segments):
-                to = lax.rem(me + s, segments)
-                every_ref[to, tile, :FAR] = out[at : at + FAR, :LANES]
-                every_ref[to, tile, FAR:] = out[at : at + FAR, LANES:]
-                at += FAR
+        high_ref[step % 2, :, span] = high
+        low_ref[step % 2, :, span] = low
+
+    def gather(step, span):
+        both = product(gather_ref[:, span], high_ref[step % 2, :, span], ((1,), (1,)))
+        rest = product(gather_ref[:nodes, span], low_ref[step % 2, :, span], ((1,), (1,)))
+        more = both[:nodes] + both[nodes:] + rest
+        if span.start > 0:
+            more = more + held_ref[step % 2]
+        held_ref[step % 2] = more
+
+    def local(step, part):
+        tile = step * (lines // LANES) + part
+        mine = held_ref[step % 2, :, part * LANES : (part + 1) * LANES]
+        turned = jnp.concatenate([mine * table_ref[0], mine * table_ref[1]], axis=1)
+        out = product(local_ref[...], stacked(turned), ((1,), (0,)))
+        near_ref[tile] = turn_ref[1] * out[:nodes, :LANES] - turn_ref[0] * out[:nodes, LANES:]
+        at = nodes
+        for ref in (ahead_ref, behind_ref):
+            ref[tile, :NEAR] = out[at : at + NEAR, :LANES]
+            ref[tile, NEAR:] = out[at : at + NEAR, LANES:]
+            at += NEAR
+        for s in range(1, segments):
+            to = lax.rem(me + s, segments)
+            every_ref[to, tile, :FAR] = out[at : at + FAR, :LANES]
+            every_ref[to, tile, FAR:] = out[at : at + FAR, LANES:]
+            at += FAR
 
     copies[0].wait()
-    cast(0)
-    for step in range(steps):
+    for span in spans:
+        cast(0, span)
+    for step in range(steps + 1):
         if step + 1 < steps:
             copies[step + 1].wait()
-        gather(step)
-        if step + 1 < steps:
-            cast(step + 1)
-        if step > 0:
-            local(step - 1)
-    local(steps - 1)
+        for number in range(max(len(spans), lines // LANES)):
+            if step < steps and number < len(spans):
+                gather(step, spans[number])
+            if step + 1 < steps and number < len(spans):
+                cast(step + 1, spans[number])
+            if step > 0 and number < lines // LANES:
+                local(step - 1, number)
 
 
 def combine_kernel(
@@ -298,26 +303,24 @@
     count = above_ref.shape[0]
     levels = count // 3
     pair = LANES // rows
-    steps = levels // pair
-    tracer_slot = 6 * pair
+    steps = levels
+    per_field = levels // pair
+    tracer_slot = 6
 
     def load(step):
         return pltpu.make_async_copy(
-            tracer_ref.at[pl.ds(first + step * pair, pair)],
-            held_ref.at[pl.ds(tracer_slot + step % 2 * pair, pair)],
-            load_sems.at[step % 2],
+            tracer_ref.at[first + step], held_ref.at[tracer_slot + step % 2], load_sems.at[step % 2]
         )
 
     def store(step, number):
         return pltpu.make_async_copy(
-            held_ref.at[pl.ds((3 * (step % 2) + number) * pair, pair)],
-            outs[number].at[pl.ds(first + step * pair, pair)],
+            held_ref.at[3 * (step % 2) + number], outs[number].at[first + step],
             sems.at[step % 2, number],
         )
 
     load(0).start()
     edges = jnp.concatenate([above_ref[...], below_ref[...]], axis=0)
-    edge_ref[...] = spread_lines(packed(edges), spread_ref)
+    edge_ref[...] = spread_lines(packed(edges), spread_ref, slice(0, lanes))
     here = lax.broadcasted_iota(jnp.int32, (rows, rows), 0)
     there = lax.broadcasted_iota(jnp.int32, (rows, rows), 1)
     column = jnp.where(here == there, jnp.broadcast_to(scale_ref[...], (rows, rows)), 0.0)
@@ -326,41 +329,49 @@
     column_ref[1] = 1.0 / column_ref[0]
     row_number = lax.broadcasted_iota(jnp.int32, (rows, 1), 0)
 
-    def fill(step):
-        pack = jnp.concatenate([pack_ref[f * steps + step] for f in range(3)], axis=0)
-        filtered_ref[step % 2] = spread_lines(pack, spread_ref)
+    def fill(step, part):
+        tile, at = step // pair, step % pair * rows
+        pack = jnp.concatenate(
+            [pack_ref[f * per_field + tile, at : at + rows] for f in range(3)], axis=0
+        )
+        columns = slice(part * 2 * LANES, (part + 1) * 2 * LANES)
+        filtered_ref[step % 2, :, columns] = spread_lines(pack, spread_ref, columns)
 
     def east_west(values):
         return pltpu.roll(values, lanes - 1, 1) - pltpu.roll(values, 1, 1)
 
-    def stencil(step):
+    def north_south(step, values, number):
+        at = number * levels + step
+        above = edge_ref[at : at + 1]
+        below = edge_ref[count + at : count + at + 1]
+        later = jnp.where(row_number == rows - 1, below, pltpu.roll(values, rows - 1, 0))
+        earlier = jnp.where(row_number == 0, above, pltpu.roll(values, 1, 0))
+        return later - earlier
+
+    def field(step, number):
+        return filtered_ref[step % 2, number * rows : (number + 1) * rows]
+
+    def stencil(step, number):
         scale = column_ref[0][:, :1]
         inverse = column_ref[1][:, :1]
-        for part in range(pair):
-            level = step * pair + part
-
-            def field(number):
-                at = number * pair * rows + part * rows
-                return filtered_ref[step % 2, at : at + rows]
-
-            def north_south(values, number):
-                at = number * levels + level
-                above = edge_ref[at : at + 1]
-                below = edge_ref[count + at : count + at + 1]
-                later = jnp.where(row_number == rows - 1, below, pltpu.roll(values, rows - 1, 0))
-                earlier = jnp.where(row_number == 0, above, pltpu.roll(values, 1, 0))
-                return later - earlier
-
-            u, v, q = field(0), field(1), field(2)
-            div = scale * (east_west(u) + north_south(v * inverse, 1))
-            vort = scale * (east_west(v) - north_south(u * inverse, 0))
-            change = courant * (u * scale * east_west(q) + v * north_south(q, 2))
-            base = 3 * (step % 2) * pair + part
-            held_ref[base] = held_ref[tracer_slot + step % 2 * pair + part] - change[:, :width]
-            held_ref[base + pair] = div[:, :width]
-            held_ref[base + 2 * pair] = vort[:, :width]
-
-    fill(0)
+        base = 3 * (step % 2)
+        if number == 0:
+            across = north_south(step, field(step, 1) * inverse, 1)
+            value = scale * (east_west(field(step, 0)) + across)
+            held_ref[base + 1] = value[:, :width]
+        elif number == 1:
+            across = north_south(step, field(step, 0) * inverse, 0)
+            value = scale * (east_west(field(step, 1)) - across)
+            held_ref[base + 2] = value[:, :width]
+        else:
+            q = field(step, 2)
+            change = field(step, 0) * (courant * scale) * east_west(q)
+            change = change + (courant * field(step, 1)) * north_south(step, q, 2)
+            held_ref[base] = held_ref[tracer_slot + step % 2] - change[:, :width]
+
+    columns = lanes // (2 * LANES)
+    for part in range(columns):
+        fill(0, part)
     for step in range(steps):
         if step + 1 < steps:
             load(step + 1).start()
@@ -368,9 +379,11 @@
         if step >= 2:
             for number in range(3):
                 store(step - 2, number).wait()
-        stencil(step)
-        if step + 1 < steps:
-            fill(step + 1)
+        for part in range(max(columns, 3)):
+            if step + 1 < steps and part < columns:
+                fill(step + 1, part)
+            if part * 3 % columns < 3 and part * 3 // columns < 3:
+                stencil(step, part * 3 // columns)
         for number in range(3):
             store(step, number).start()
     for step in range(max(steps - 2, 0), steps):
@@ -429,6 +442,7 @@
                 pltpu.SemaphoreType.DMA((steps,)),
             ],
             compiler_params=flat,
+            cost_estimate=pl.CostEstimate(flops=0, bytes_accessed=57600000 // CHUNKS, transcendentals=0),
             name="analyse",
         )(device, cut, places, gather_table, local_table, wind_u, wind_v, tracer)
 
@@ -442,7 +456,7 @@
         return shifted(ahead, 1), shifted(behind, -1), got
 
     def combine(near, turn, moments):
-        step_tiles = 4
+        step_tiles = 3
         edge = jax.ShapeDtypeStruct((count, wide), F32)
         extra_spec = pl.BlockSpec((step_tiles, 2 * NEAR, LANES), lambda s, d: (s, 0, 0))
         return pl.pallas_call(
@@ -469,6 +483,7 @@
                 ),
             ),
             compiler_params=params,
+            cost_estimate=pl.CostEstimate(flops=0, bytes_accessed=21600000 // CHUNKS, transcendentals=0),
             name="combine",
         )(device, scale, turn, far_table, near, *moments)
 
@@ -479,15 +494,16 @@
             in_specs=[whole_spec()] * 5 + [anywhere] * (1 + len(before)),
             out_specs=(anywhere,) * 3,
             scratch_shapes=[
-                pltpu.VMEM((2, 3 * LANES, lanes), F32),
+                pltpu.VMEM((2, 3 * rows, lanes), F32),
                 pltpu.VMEM((2 * count, lanes), F32),
                 pltpu.VMEM((2, rows, LANES), F32),
-                pltpu.VMEM((8 * pair, rows, width), F32),
+                pltpu.VMEM((8, rows, width), F32),
                 pltpu.SemaphoreType.DMA((2,)),
                 pltpu.SemaphoreType.DMA((2, 3)),
             ],
             input_output_aliases={6 + i: i for i in range(len(before))},
             compiler_params=flat,
+            cost_estimate=pl.CostEstimate(flops=0, bytes_accessed=43200000 // CHUNKS, transcendentals=0),
             name="finish",
         )(scale, spread_table, above, below, pack, tracer, *before)
 

time: 62 us -> 77.8 us (1.25)
  the two profiles are of different devices: /device:TPU:0 before, /device:TPU:8 now
where the time goes in v4:
time: 77.8 us; the launch traced here: 76.8 us
  Pallas kernels  46.2 us (59%)
  starting transfers between devices  25.1 us (32%)
  local copies, waits for them, and re-layouts  2.55 us (3%)
  waiting for transfers between devices  1.97 us (3%)
  between operations  1.01 us (1%)
    pallas_call x2, Pallas kernels, analyse(): pl.pallas_call(functools.partial(analyse_kernel, segments, chunk * nl, gr...  22.1 us
    pallas_call x2, Pallas kernels, finish(): pl.pallas_call(functools.partial(finish_kernel, chunk * nl), out_shape=(j...  17.1 us
    all_to_all x2, starting transfers between devices, exchange(): got = lax.all_to_all(every, 'lon', 0, 0)  7.93 us
    pallas_call x2, Pallas kernels, combine(): pl.pallas_call(functools.partial(combine_kernel, per_field, rows), out_sh...  7.01 us
    ppermute x2, starting transfers between devices, on_device(): above = lax.ppermute(bottom, 'lat', [(i, i + 1) for i in range(lats - 1)])  6.95 us
    ppermute x4, starting transfers between devices, shifted(): lax.ppermute(array, 'lon', [(i, (i + by) % segments) for i in range(segme...  5.38 us
    ppermute x2, starting transfers between devices, on_device(): below = lax.ppermute(top, 'lat', [(i + 1, i) for i in range(lats - 1)])  4.88 us
    unnamed x24, local copies, waits for them, and re-layouts  2.55 us
  transfers between devices with their start and end apart: 10, of which 1 were waited for; matrix products, arithmetic and copies ran while one was open for 0% of the time, Pallas kernels for 35%

profile of v4, /device:TPU:8, one launch (start us, length us, event | category | flops | bytes accessed | tf_op | source)
XLA Modules:
  0.0 76.8 jit_solution(11828207845088679327)
XLA Ops:
  0.6 11.0 %analyse.3 = (f32[6,288,128]{2,1,0:T(8,128)}, f32[6,24,128]{2,1,0:T(8,128)}, f32[6,24,128]{2,1,0:T(8,128)}, f32[8,6,8,128]{3,2,1,0:T(8,128)}, f32[2,288,128]{2,1,0:T(8,128)}) custom-call(s32[1]{0:T(128)} %bitcast.1.device_ref, s32[1,64]{1,0:T(1,128)} %bitcast.7, f32[2,288,1]{2,1,0:T(8,128)} %constant.14.clone.places_ref, ...), custom_call_target="tpu_custom_call" | custom-call | bytes 28800000 | tf_op jit(solution)/shard_map/analyse/pallas_call | solution.py:425
  11.7 3.7 %all-to-all-start.1 = ((f32[8,6,8,128]{3,2,1,0:T(8,128)}), f32[8,6,8,128]{3,2,1,0:T(8,128)S(1)}, u32[]{:S(2)}, u32[]{:S(2)}) async-start(f32[8,6,8,128]{3,2,1,0:T(8,128)} %get-tuple-element.34), calls=%async_computation.1 | async-start | bytes 393216 | tf_op jit(solution)/shard_map/all_to_all | solution.py:455
  15.4 11.1 %analyse.2 = (f32[6,288,128]{2,1,0:T(8,128)}, f32[6,24,128]{2,1,0:T(8,128)}, f32[6,24,128]{2,1,0:T(8,128)}, f32[8,6,8,128]{3,2,1,0:T(8,128)}, f32[2,288,128]{2,1,0:T(8,128)}) custom-call(s32[1]{0:T(128)} %bitcast.1.device_ref, s32[1,64]{1,0:T(1,128)} %bitcast.8, f32[2,288,1]{2,1,0:T(8,128)} %constant.14.clone.places_ref, ...), custom_call_target="tpu_custom_call" | custom-call | bytes 28800000 | tf_op jit(solution)/shard_map/analyse/pallas_call | solution.py:425
  26.5 4.2 %all-to-all-start = ((f32[8,6,8,128]{3,2,1,0:T(8,128)}), f32[8,6,8,128]{3,2,1,0:T(8,128)S(1)}, u32[]{:S(2)}, u32[]{:S(2)}) async-start(f32[8,6,8,128]{3,2,1,0:T(8,128)} %get-tuple-element.26), calls=%async_computation | async-start | bytes 393216 | tf_op jit(solution)/shard_map/all_to_all | solution.py:455
  30.7 0.5 collective-permute-start.4
  31.2 2.2 %collective-permute-start.5 = (f32[6,24,128]{2,1,0:T(8,128)S(1)}, f32[6,24,128]{2,1,0:T(8,128)S(1)}, u32[]{:S(2)}, u32[]{:S(2)}) collective-permute-start(f32[6,24,128]{2,1,0:T(8,128)S(1)} %copy-done.10), channel_id=1, source_target_pairs={{0,7},{1,0},{2,1},{3,2},{4,3},{5,4},{6,5},{7,6},{8,15},{9,8},{10,9... | collective-permute-start | bytes 221192 | tf_op jit(solution)/shard_map/ppermute | solution.py:451
  33.4 2.6 %collective-permute-start.1 = (f32[6,24,128]{2,1,0:T(8,128)}, f32[6,24,128]{2,1,0:T(8,128)S(1)}, u32[]{:S(2)}, u32[]{:S(2)}) collective-permute-start(f32[6,24,128]{2,1,0:T(8,128)} %get-tuple-element.25), channel_id=1, source_target_pairs={{0,7},{1,0},{2,1},{3,2},{4,3},{5,4},{6,5},{7,6},{8,15},{9,8},{10,9... | collective-permute-start | bytes 221192 | tf_op jit(solution)/shard_map/ppermute | solution.py:451
  36.1 1.9 %collective-permute-done.4.behind_ref = f32[6,24,128]{2,1,0:T(8,128)S(1)} collective-permute-done((f32[6,24,128]{2,1,0:T(8,128)S(1)}, f32[6,24,128]{2,1,0:T(8,128)S(1)}, u32[]{:S(2)}, u32[]{:S(2)}) %collective-permute-start.4) | collective-permute-done | bytes 73760 | tf_op jit(solution)/shard_map/ppermute | solution.py:451
  38.0 0.6 copy-done.4
  38.7 0.0 copy-done.5
  38.7 3.5 %combine.3 = (bf16[6,128,640]{2,1,0:T(8,128)(2,1)}, f32[12,384]{1,0:T(8,128)}, f32[12,384]{1,0:T(8,128)}) custom-call(s32[1]{0:T(128)} %bitcast.1.device_ref, f32[1,64]{1,0:T(1,128)} %bitcast.3, f32[2,288,128]{2,1,0:T(8,128)} %get-tuple-element.30.turn_ref, bf16[8,576,336]{2,1,0:T(8,128)(2,1)} %constant.17.clone.table_in, ...), custom_call_target="tpu_custom_call" | custom-call | bytes 10800000 | tf_op jit(solution)/shard_map/combine/pallas_call | solution.py:462
  42.2 3.5 %collective-permute-start.6 = (f32[12,384]{1,0:T(8,128)}, f32[12,384]{1,0:T(8,128)S(1)}, u32[]{:S(2)}, u32[]{:S(2)}) collective-permute-start(f32[12,384]{1,0:T(8,128)} %get-tuple-element.35), channel_id=1, source_target_pairs={{0,8},{8,16},{16,24},{1,9},{9,17},{17,25},{2,10},{10,18},{18,26},{... | collective-permute-start | bytes 55304 | tf_op jit(solution)/shard_map/ppermute | solution.py:515
  45.7 2.4 %collective-permute-start.7 = (f32[12,384]{1,0:T(8,128)}, f32[12,384]{1,0:T(8,128)S(1)}, u32[]{:S(2)}, u32[]{:S(2)}) collective-permute-start(f32[12,384]{1,0:T(8,128)} %get-tuple-element.36), channel_id=1, source_target_pairs={{8,0},{16,8},{24,16},{9,1},{17,9},{25,17},{10,2},{18,10},{26,18},{... | collective-permute-start | bytes 55304 | tf_op jit(solution)/shard_map/ppermute | solution.py:516
  48.1 0.6 copy-done.2
  48.7 0.0 copy-done.3
  48.7 0.1 copy-done
  48.8 3.5 %combine.2 = (bf16[6,128,640]{2,1,0:T(8,128)(2,1)}, f32[12,384]{1,0:T(8,128)}, f32[12,384]{1,0:T(8,128)}) custom-call(s32[1]{0:T(128)} %bitcast.1.device_ref, f32[1,64]{1,0:T(1,128)} %bitcast.4, f32[2,288,128]{2,1,0:T(8,128)} %get-tuple-element.22.turn_ref, bf16[8,576,336]{2,1,0:T(8,128)(2,1)} %constant.17.clone.table_in, ...), custom_call_target="tpu_custom_call" | custom-call | bytes 10800000 | tf_op jit(solution)/shard_map/combine/pallas_call | solution.py:462
  52.3 3.5 %collective-permute-start.2 = (f32[12,384]{1,0:T(8,128)}, f32[12,384]{1,0:T(8,128)S(1)}, u32[]{:S(2)}, u32[]{:S(2)}) collective-permute-start(f32[12,384]{1,0:T(8,128)} %get-tuple-element.27), channel_id=1, source_target_pairs={{0,8},{8,16},{16,24},{1,9},{9,17},{17,25},{2,10},{10,18},{18,26},{... | collective-permute-start | bytes 55304 | tf_op jit(solution)/shard_map/ppermute | solution.py:515
  55.8 2.5 %collective-permute-start.3 = (f32[12,384]{1,0:T(8,128)}, f32[12,384]{1,0:T(8,128)S(1)}, u32[]{:S(2)}, u32[]{:S(2)}) collective-permute-start(f32[12,384]{1,0:T(8,128)} %get-tuple-element.28), channel_id=1, source_target_pairs={{8,0},{16,8},{24,16},{9,1},{17,9},{25,17},{10,2},{18,10},{26,18},{... | collective-permute-start | bytes 55304 | tf_op jit(solution)/shard_map/ppermute | solution.py:516
  58.4 0.6 copy-done.6
  58.9 0.0 copy-done.7
  59.0 8.5 %finish.2 = (f32[8,64,1500]{2,1,0:T(8,128)}, f32[8,64,1500]{2,1,0:T(8,128)}, f32[8,64,1500]{2,1,0:T(8,128)}) custom-call(f32[1,64]{1,0:T(1,128)} %bitcast.5, bf16[896,1536]{1,0:T(8,128)(2,1)} %constant.18.clone.spread_ref, f32[12,384]{1,0:T(8,128)} %copy-done.6, f32[12,384]{1,0:T(8,128)} %copy-done.7, bf16[6,128,640]{2,1,0:T(8,128)(2,1)} %get-tuple-element.37.pack_ref, ...), custom_call_target="tpu_custom_call" | custom-call | bytes 21600000 | tf_op jit(solution)/shard_map/finish/pallas_call | solution.py:491
  67.5 0.6 copy-done.8
  68.1 8.5 %finish.3 = (f32[8,64,1500]{2,1,0:T(8,128)}, f32[8,64,1500]{2,1,0:T(8,128)}, f32[8,64,1500]{2,1,0:T(8,128)}) custom-call(f32[1,64]{1,0:T(1,128)} %bitcast.6, bf16[896,1536]{1,0:T(8,128)(2,1)} %constant.18.clone.spread_ref, f32[12,384]{1,0:T(8,128)} %copy-done.8, f32[12,384]{1,0:T(8,128)} %copy-done.9, ...), custom_call_target="tpu_custom_call", output_to_operand_aliasing={{0}: (6, {}), {1}: (7, {}), {2}: (8, {})} | custom-call | bytes 21600000 | tf_op jit(solution)/shard_map/finish/pallas_call | solution.py:491
  (26 shorter events, 0.1 us)
Async XLA Ops:
  11.7 14.8 %all-to-all-start.1 = ((f32[8,6,8,128]{3,2,1,0:T(8,128)}), f32[8,6,8,128]{3,2,1,0:T(8,128)S(1)}, u32[]{:S(2)}, u32[]{:S(2)}) async-start(f32[8,6,8,128]{3,2,1,0:T(8,128)} %get-tuple-element.34), calls=%async_computation.1 | async-start | bytes 393216 | tf_op jit(solution)/shard_map/all_to_all | solution.py:455
  15.4 15.3 %copy-start.11 = (f32[6,24,128]{2,1,0:T(8,128)S(1)}, f32[6,24,128]{2,1,0:T(8,128)}, u32[]{:S(2)}) copy-start(f32[6,24,128]{2,1,0:T(8,128)} %get-tuple-element.32) | copy-start | bytes 221188
  15.4 15.8 %copy-start.10 = (f32[6,24,128]{2,1,0:T(8,128)S(1)}, f32[6,24,128]{2,1,0:T(8,128)}, u32[]{:S(2)}) copy-start(f32[6,24,128]{2,1,0:T(8,128)} %get-tuple-element.33) | copy-start | bytes 221188
  26.5 11.6 %copy-start.1 = (f32[8,6,8,128]{3,2,1,0:T(8,128)}, f32[8,6,8,128]{3,2,1,0:T(8,128)S(1)}, u32[]{:S(2)}) copy-start(f32[8,6,8,128]{3,2,1,0:T(8,128)S(1)} %all-to-all-done.1.every_ref) | copy-start | bytes 589828
  26.5 21.6 %all-to-all-start = ((f32[8,6,8,128]{3,2,1,0:T(8,128)}), f32[8,6,8,128]{3,2,1,0:T(8,128)S(1)}, u32[]{:S(2)}, u32[]{:S(2)}) async-start(f32[8,6,8,128]{3,2,1,0:T(8,128)} %get-tuple-element.26), calls=%async_computation | async-start | bytes 393216 | tf_op jit(solution)/shard_map/all_to_all | solution.py:455
  30.7 7.3 %collective-permute-start.4 = (f32[6,24,128]{2,1,0:T(8,128)S(1)}, f32[6,24,128]{2,1,0:T(8,128)S(1)}, u32[]{:S(2)}, u32[]{:S(2)}) collective-permute-start(f32[6,24,128]{2,1,0:T(8,128)S(1)} %copy-done.11), channel_id=1, source_target_pairs={{0,1},{1,2},{2,3},{3,4},{4,5},{5,6},{6,7},{7,0},{8,9},{9,10},{10,1... | collective-permute-start | bytes 221192 | tf_op jit(solution)/shard_map/ppermute | solution.py:451
  31.2 6.8 %collective-permute-start.5 = (f32[6,24,128]{2,1,0:T(8,128)S(1)}, f32[6,24,128]{2,1,0:T(8,128)S(1)}, u32[]{:S(2)}, u32[]{:S(2)}) collective-permute-start(f32[6,24,128]{2,1,0:T(8,128)S(1)} %copy-done.10), channel_id=1, source_target_pairs={{0,7},{1,0},{2,1},{3,2},{4,3},{5,4},{6,5},{7,6},{8,15},{9,8},{10,9... | collective-permute-start | bytes 221192 | tf_op jit(solution)/shard_map/ppermute | solution.py:451
  33.4 14.6 %collective-permute-start = (f32[6,24,128]{2,1,0:T(8,128)}, f32[6,24,128]{2,1,0:T(8,128)S(1)}, u32[]{:S(2)}, u32[]{:S(2)}) collective-permute-start(f32[6,24,128]{2,1,0:T(8,128)} %get-tuple-element.24), channel_id=1, source_target_pairs={{0,1},{1,2},{2,3},{3,4},{4,5},{5,6},{6,7},{7,0},{8,9},{9,10},{10,1... | collective-permute-start | bytes 221192 | tf_op jit(solution)/shard_map/ppermute | solution.py:451
  33.4 14.6 %collective-permute-start.1 = (f32[6,24,128]{2,1,0:T(8,128)}, f32[6,24,128]{2,1,0:T(8,128)S(1)}, u32[]{:S(2)}, u32[]{:S(2)}) collective-permute-start(f32[6,24,128]{2,1,0:T(8,128)} %get-tuple-element.25), channel_id=1, source_target_pairs={{0,7},{1,0},{2,1},{3,2},{4,3},{5,4},{6,5},{7,6},{8,15},{9,8},{10,9... | collective-permute-start | bytes 221192 | tf_op jit(solution)/shard_map/ppermute | solution.py:451
  38.0 0.6 copy-start.4
  38.0 0.7 copy-start.5
  42.2 16.1 %collective-permute-start.6 = (f32[12,384]{1,0:T(8,128)}, f32[12,384]{1,0:T(8,128)S(1)}, u32[]{:S(2)}, u32[]{:S(2)}) collective-permute-start(f32[12,384]{1,0:T(8,128)} %get-tuple-element.35), channel_id=1, source_target_pairs={{0,8},{8,16},{16,24},{1,9},{9,17},{17,25},{2,10},{10,18},{18,26},{... | collective-permute-start | bytes 55304 | tf_op jit(solution)/shard_map/ppermute | solution.py:515
  45.7 12.7 %collective-permute-start.7 = (f32[12,384]{1,0:T(8,128)}, f32[12,384]{1,0:T(8,128)S(1)}, u32[]{:S(2)}, u32[]{:S(2)}) collective-permute-start(f32[12,384]{1,0:T(8,128)} %get-tuple-element.36), channel_id=1, source_target_pairs={{8,0},{16,8},{24,16},{9,1},{17,9},{25,17},{10,2},{18,10},{26,18},{... | collective-permute-start | bytes 55304 | tf_op jit(solution)/shard_map/ppermute | solution.py:516
  48.0 0.6 copy-start.2
  48.1 0.6 copy-start.3
  48.1 0.7 copy-start
  52.3 15.2 %collective-permute-start.2 = (f32[12,384]{1,0:T(8,128)}, f32[12,384]{1,0:T(8,128)S(1)}, u32[]{:S(2)}, u32[]{:S(2)}) collective-permute-start(f32[12,384]{1,0:T(8,128)} %get-tuple-element.27), channel_id=1, source_target_pairs={{0,8},{8,16},{16,24},{1,9},{9,17},{17,25},{2,10},{10,18},{18,26},{... | collective-permute-start | bytes 55304 | tf_op jit(solution)/shard_map/ppermute | solution.py:515
  55.8 11.7 %collective-permute-start.3 = (f32[12,384]{1,0:T(8,128)}, f32[12,384]{1,0:T(8,128)S(1)}, u32[]{:S(2)}, u32[]{:S(2)}) collective-permute-start(f32[12,384]{1,0:T(8,128)} %get-tuple-element.28), channel_id=1, source_target_pairs={{8,0},{16,8},{24,16},{9,1},{17,9},{25,17},{10,2},{18,10},{26,18},{... | collective-permute-start | bytes 55304 | tf_op jit(solution)/shard_map/ppermute | solution.py:516
  58.3 0.6 copy-start.6
  58.3 0.6 copy-start.7
  67.5 0.6 copy-start.8
  67.5 0.6 copy-start.9

commit v5 on v3

v5 whole, which is shorter than its diff:
```python
import functools
import math

import jax
import jax.numpy as jnp
import ml_dtypes
import numpy as np
from jax import lax
from jax.experimental import pallas as pl
from jax.experimental.pallas import tpu as pltpu
from jax.sharding import PartitionSpec as P

NLON = 12000
KMAX = 1024
NEAR = 12
FAR = 4
EXTRA = 32
LANES = 128
courant = 0.5
BF = jnp.bfloat16
F32 = jnp.float32
VMEM_LIMIT = 56 * 1024 * 1024


def prolate(points, band, count):
    i = np.arange(points)
    diag = ((points - 1 - 2 * i) / 2.0) ** 2 * np.cos(2 * np.pi * band)
    off = i[1:] * (points - i[1:]) / 2.0
    mid = points // 2
    half = (count + 1) // 2
    out = np.zeros((points, 2 * half))
    dd, ee = diag[mid:], off[mid:].copy()
    scaled = ee.copy()
    scaled[0] *= math.sqrt(2.0)
    even = np.linalg.eigh(np.diag(dd) + np.diag(scaled, 1) + np.diag(scaled, -1))[1]
    even = even[:, ::-1][:, :half]
    wing = even[1:] / math.sqrt(2.0)
    out[mid, 0::2] = even[0]
    out[mid + 1 :, 0::2] = wing
    out[:mid, 0::2] = wing[::-1]
    odd = np.linalg.eigh(np.diag(dd[1:]) + np.diag(ee[1:], 1) + np.diag(ee[1:], -1))[1]
    wing = odd[:, ::-1][:, :half] / math.sqrt(2.0)
    out[mid + 1 :, 1::2] = wing
    out[:mid, 1::2] = -wing[::-1]
    return out


def interpolation(low, high, nodes, snap):
    fine = prolate(2 * (high - low) + 1, (KMAX - 0.5) / NLON / 2, nodes + 2)
    wave = fine[:, nodes]
    at = np.nonzero(wave[:-1] * wave[1:] < 0)[0]
    roots = (at + wave[at] / (wave[at] - wave[at + 1]))[: nodes // 2] / 2 + low
    left = snap(roots)
    for i in range(1, len(left)):
        left[i] = max(left[i], left[i - 1] + 1)
    places = np.concatenate([left, (low + high) - left[::-1]])
    kept = nodes - 4
    index = np.round((places - low) * 2).astype(int)
    return places, fine[::2, :kept] @ np.linalg.pinv(fine[index, :kept])


def near_kernel(distance):
    return 1.0 / (NLON * np.sin(np.pi * distance / NLON))


def two_parts(table):
    high = table.astype(np.float32).astype(ml_dtypes.bfloat16)
    low = (table - high.astype(np.float64)).astype(np.float32).astype(ml_dtypes.bfloat16)
    return high, low


@functools.lru_cache(maxsize=4)
def make_tables(width, segments):
    main = -(-2 * KMAX * width // NLON // LANES) * LANES
    nodes = main + EXTRA
    source, gather = interpolation(0, width - 1, nodes, np.round)
    target, spread = interpolation(-1, width, nodes, lambda r: np.floor(r) + 0.5)
    local = near_kernel(target[:, None] - source[None])
    offsets = [d for d in range(-(segments - 1), segments) if d]
    far = {d: near_kernel(target[:, None] + width * d - source[None]) for d in offsets}

    def leading(kernel, count):
        found = np.linalg.svd(kernel, full_matrices=False)[2][:count]
        peak = np.take_along_axis(found, np.abs(found).argmax(1)[:, None], 1)
        return found * np.sign(peak)

    ahead = range(1, segments)
    basis = {s: leading(far[s], FAR) for s in ahead}
    for s in (1, segments - 1):
        both = leading(far[s], FAR + NEAR)
        basis[s], basis[-s] = both[:FAR], both[FAR:]

    high, low = two_parts(gather.T)
    gather_table = np.concatenate([high, low], 0)
    more = [basis[-1], basis[1 - segments]] + [basis[s] for s in ahead]
    rows = np.concatenate(more, 0)
    rows = np.pad(rows, ((0, -len(rows) % 8), (0, 0)))
    high, low = two_parts(rows)
    moment_table = np.concatenate([high, low, high], 1)
    high, low = two_parts(local)
    local_table = np.concatenate([high, low, high], 1)
    blocks = []
    for d in range(segments):
        pieces = [far[d - (d - s) % segments] @ basis[-s].T for s in (1, segments - 1)]
        for e in range(segments):
            if e == d:
                pieces.append(np.zeros((nodes, FAR)))
            else:
                pieces.append(far[d - e] @ basis[(d - e) % segments].T)
        pieces = [np.pad(piece, ((0, main + LANES - nodes), (0, 0))).T for piece in pieces]
        left = [p for piece in pieces for p in (piece, 0 * piece)]
        right = [p for piece in pieces for p in (0 * piece, piece)]
        both = np.concatenate([np.concatenate(left, 0), np.concatenate(right, 0)], 1)
        high, low = two_parts(both)
        blocks.append(np.concatenate([high, low, high], 0))
    far_table = np.stack(blocks)
    lanes = -(-(width + 2) // LANES) * LANES
    wide = np.zeros((nodes, lanes))
    wide[:, : width + 1] = spread.T[:, 1:]
    wide[:, lanes - 1] = spread.T[:, 0]
    high, low = two_parts(wide)
    none = np.zeros((LANES - 3 * EXTRA, lanes), high.dtype)
    spread_table = np.concatenate(
        [high[:main], low[:main], high[:main], high[main:], low[main:], high[main:], none], 0
    )
    places = np.stack([2 * source - width, 2 * target - width]).astype(np.float32)
    return gather_table, moment_table, local_table, far_table, spread_table, places[:, :, None]


def phases(cut, places, device, segments, width):
    full = 4.0 * NLON
    odd = 2.0 * cut - 1.0
    inner = odd * places
    inner = inner - full * jnp.floor(inner * (1.0 / full) + 0.5)
    base = odd * (2.0 * device + 1.0)
    cycle = 4.0 * segments
    base = (base - cycle * jnp.floor(base * (1.0 / cycle))) * float(width)
    total = inner + base
    total = total - full * jnp.floor(total * (1.0 / full) + 0.5)
    quarter = jnp.floor(total * (4.0 / full) + 0.5)
    x = (total - (full / 4.0) * quarter) * (2.0 * math.pi / full)
    y = x * x
    sine = x + x * y * (
        -1.0 / 6 + y * (1.0 / 120 + y * (-1.0 / 5040 + y * (1.0 / 362880)))
    )
    cosine = 1.0 + y * (
        -0.5 + y * (1.0 / 24 + y * (-1.0 / 720 + y * (1.0 / 40320 + y * (-1.0 / 3628800))))
    )
    odd_quarter = jnp.abs(quarter) == 1.0
    turned_c = jnp.where(odd_quarter, -quarter * sine, cosine)
    turned_s = jnp.where(odd_quarter, quarter * cosine, sine)
    flip = jnp.where(jnp.abs(quarter) == 2.0, -1.0, 1.0)
    return turned_c * flip, turned_s * flip


def parts(values):
    high = values.astype(BF)
    return high, (values - high.astype(F32)).astype(BF)


def stacked(values):
    high, low = parts(values)
    return jnp.concatenate([high, high, low], axis=0)


def product(a, b, dims):
    return lax.dot_general(a, b, (dims, ((), ())), preferred_element_type=F32)


def lane_cut(cut_ref):
    cut = cut_ref[...].astype(F32)
    return jnp.concatenate([cut] * (LANES // cut.shape[1]), axis=1)


def packed(values):
    main = values.shape[1] - LANES
    high, low = parts(values)
    last, last_low = high[:, main:].astype(F32), low[:, main:].astype(F32)
    last = last + pltpu.roll(last, EXTRA, 1) + pltpu.roll(last_low, 2 * EXTRA, 1)
    return jnp.concatenate([high[:, :main], low[:, :main], last.astype(BF)], axis=1)


def spread_lines(pack, spread_ref):
    main = (pack.shape[1] - LANES) // 2
    held = jnp.concatenate([pack[:, :main], pack], axis=1)
    return product(held, spread_ref[...], ((1,), (0,)))


def analyse_kernel(
    segments, groups, device_ref, cut_ref, places_ref, gather_ref, moment_ref,
    u_ref, v_ref, q_ref, node_ref, ahead_ref, behind_ref, every_ref, table_ref,
    lines_ref, high_ref, low_ref, sems,
):
    width = u_ref.shape[2]
    steps, levels, rows, _ = lines_ref.shape
    lines = levels * rows
    nodes = gather_ref.shape[0] // 2
    me = device_ref[0]

    copies = []
    for step in range(steps):
        ref = (u_ref, v_ref, q_ref)[step // groups]
        levels_at = pl.ds((step % groups) * levels, levels)
        copies.append(pltpu.make_async_copy(ref.at[levels_at], lines_ref.at[step], sems.at[step]))
        copies[-1].start()
    for side in range(2):
        cosine, sine = phases(
            lane_cut(cut_ref), places_ref[side], me.astype(F32), segments, width
        )
        table_ref[2 * side], table_ref[2 * side + 1] = cosine, sine
    every_ref[me] = jnp.zeros(every_ref.shape[1:], F32)

    def cast(step):
        values = lines_ref[step].reshape(lines, width)
        high, low = parts(values)
        high_ref[step % 2] = high
        low_ref[step % 2] = low

    def gather(step):
        both = product(gather_ref[...], high_ref[step % 2], ((1,), (1,)))
        rest = product(gather_ref[:nodes], low_ref[step % 2], ((1,), (1,)))
        held = both[:nodes] + both[nodes:] + rest
        for part in range(lines // LANES):
            node_ref[step * (lines // LANES) + part] = held[:, part * LANES : (part + 1) * LANES]

    def moments(step):
        for part in range(lines // LANES):
            tile = step * (lines // LANES) + part
            mine = node_ref[tile]
            turned = jnp.concatenate([mine * table_ref[0], mine * table_ref[1]], axis=1)
            out = product(moment_ref[...], stacked(turned), ((1,), (0,)))
            at = 0
            for ref in (ahead_ref, behind_ref):
                ref[tile, :NEAR] = out[at : at + NEAR, :LANES]
                ref[tile, NEAR:] = out[at : at + NEAR, LANES:]
                at += NEAR
            for s in range(1, segments):
                to = lax.rem(me + s, segments)
                every_ref[to, tile, :FAR] = out[at : at + FAR, :LANES]
                every_ref[to, tile, FAR:] = out[at : at + FAR, LANES:]
                at += FAR

    copies[0].wait()
    cast(0)
    for step in range(steps):
        if step + 1 < steps:
            copies[step + 1].wait()
        gather(step)
        if step + 1 < steps:
            cast(step + 1)
        if step > 0:
            moments(step - 1)
    moments(steps - 1)


def turned_over(values):
    none = jnp.zeros((LANES - EXTRA, LANES), F32)
    return jnp.transpose(jnp.concatenate([values, none], axis=0))


def near_kernel_call(local_ref, table_ref, node_ref, near_ref, turn_ref):
    tiles, nodes, _ = node_ref.shape

    @pl.when(pl.program_id(0) == 0)
    def _():
        turn_ref[0] = turned_over(table_ref[2])
        turn_ref[1] = turned_over(table_ref[3])

    columns = []
    for tile in range(tiles):
        columns += [node_ref[tile] * table_ref[0], node_ref[tile] * table_ref[1]]
    out = product(local_ref[...], stacked(jnp.concatenate(columns, axis=1)), ((1,), (0,)))
    for tile in range(tiles):
        at = 2 * tile * LANES
        cosine, sine = out[:, at : at + LANES], out[:, at + LANES : at + 2 * LANES]
        near_ref[tile] = turned_over(table_ref[3] * cosine - table_ref[2] * sine)


def combine_kernel(
    per_field, rows, device_ref, scale_ref, turn_ref, far_ref, near_ref, behind_ref, ahead_ref,
    every_ref, pack_ref, top_ref, bottom_ref,
):
    step = pl.program_id(0)
    tiles, _, wide = near_ref.shape
    segments = every_ref.shape[0]
    columns = []
    for tile in range(tiles):
        pieces = [behind_ref[tile], ahead_ref[tile]]
        pieces += [every_ref[e, tile] for e in range(segments)]
        columns.append(jnp.concatenate(pieces, axis=0))
    got = product(stacked(jnp.concatenate(columns, axis=1)), far_ref[0], ((0,), (0,)))
    inverse = 1.0 / scale_ref[...]
    for tile in range(tiles):
        mine = got[tile * LANES : (tile + 1) * LANES]
        values = near_ref[tile] + turn_ref[1] * mine[:, :wide] - turn_ref[0] * mine[:, wide:]
        pack_ref[tile] = packed(values)
        number = step * tiles + tile
        wind = number < 2 * per_field
        top_weight = jnp.where(wind, inverse[:, :1], 1.0)
        bottom_weight = jnp.where(wind, inverse[:, rows - 1 :], 1.0)
        pair = LANES // rows
        for part in range(pair):
            line = number * pair + part
            top_ref[pl.ds(line, 1), :] = values[part * rows : part * rows + 1] * top_weight
            last = part * rows + rows - 1
            bottom_ref[pl.ds(line, 1), :] = values[last : last + 1] * bottom_weight


def finish_kernel(
    scale_ref, spread_ref, above_ref, below_ref, pack_ref, tracer_ref, *refs
):
    outs = refs[:3]
    filtered_ref, edge_ref, column_ref, held_ref, load_sems, sems = refs[3:]
    levels, rows, width = tracer_ref.shape
    lanes = spread_ref.shape[1]
    count = above_ref.shape[0]
    tracer_slot = 6

    def load(step):
        return pltpu.make_async_copy(
            tracer_ref.at[step], held_ref.at[tracer_slot + step % 2], load_sems.at[step % 2]
        )

    def store(step, number):
        return pltpu.make_async_copy(
            held_ref.at[3 * (step % 2) + number], outs[number].at[step], sems.at[step % 2, number]
        )

    load(0).start()
    pack = pack_ref[...].reshape(filtered_ref.shape[0], pack_ref.shape[2])
    filtered_ref[...] = spread_lines(pack, spread_ref)
    edges = jnp.concatenate([above_ref[...], below_ref[...]], axis=0)
    edge_ref[...] = spread_lines(packed(edges), spread_ref)
    here = lax.broadcasted_iota(jnp.int32, (rows, rows), 0)
    there = lax.broadcasted_iota(jnp.int32, (rows, rows), 1)
    column = jnp.where(here == there, jnp.broadcast_to(scale_ref[...], (rows, rows)), 0.0)
    column = jnp.sum(column, axis=1, keepdims=True)
    column_ref[0] = jnp.broadcast_to(column, (rows, LANES))
    column_ref[1] = 1.0 / column_ref[0]
    row_number = lax.broadcasted_iota(jnp.int32, (rows, 1), 0)

    def east_west(values):
        return pltpu.roll(values, lanes - 1, 1) - pltpu.roll(values, 1, 1)

    def stencil(level):
        scale = column_ref[0][:, :1]
        inverse = column_ref[1][:, :1]

        def field(number):
            at = (number * levels + level) * rows
            return filtered_ref[at : at + rows]

        def north_south(values, number):
            at = number * levels + level
            above = edge_ref[at : at + 1]
            below = edge_ref[count + at : count + at + 1]
            later = jnp.where(row_number == rows - 1, below, pltpu.roll(values, rows - 1, 0))
            earlier = jnp.where(row_number == 0, above, pltpu.roll(values, 1, 0))
            return later - earlier

        u, v, q = field(0), field(1), field(2)
        div = scale * (east_west(u) + north_south(v * inverse, 1))
        vort = scale * (east_west(v) - north_south(u * inverse, 0))
        change = u * (courant * scale) * east_west(q) + (courant * v) * north_south(q, 2)
        base = 3 * (level % 2)
        held_ref[base] = held_ref[tracer_slot + level % 2] - change[:, :width]
        held_ref[base + 1] = div[:, :width]
        held_ref[base + 2] = vort[:, :width]

    for level in range(levels):
        if level + 1 < levels:
            load(level + 1).start()
        load(level).wait()
        if level >= 2:
            for number in range(3):
                store(level - 2, number).wait()
        stencil(level)
        for number in range(3):
            store(level, number).start()
    for level in range(max(levels - 2, 0), levels):
        for number in range(3):
            store(level, number).wait()


def whole_spec():
    return pl.BlockSpec(memory_space=pltpu.VMEM)


def on_device(segments, lats, tables, wind_u, wind_v, tracer, cutoff, row_scale):
    levels, rows, width = wind_u.shape
    gather_table, moment_table, local_table, far_table, spread_table, places = tables
    nodes = gather_table.shape[0] // 2
    lanes = spread_table.shape[1]
    wide = nodes - EXTRA + LANES
    pair = LANES // rows
    group = 2 * pair
    groups = levels // group
    per_field = levels // pair
    tiles = 3 * per_field
    count = 3 * levels
    device = lax.axis_index("lon").astype(jnp.int32)[None]
    cut = cutoff.reshape(1, rows)
    scale = row_scale.reshape(1, rows)

    smem = pl.BlockSpec(memory_space=pltpu.SMEM)
    anywhere = pl.BlockSpec(memory_space=pl.ANY)
    params = pltpu.CompilerParams(
        dimension_semantics=("arbitrary",), vmem_limit_bytes=VMEM_LIMIT
    )
    flat = pltpu.CompilerParams(vmem_limit_bytes=VMEM_LIMIT)

    def cost(us):
        return pl.CostEstimate(flops=0, bytes_accessed=us * 3600000, transcendentals=0)

    steps = 3 * groups
    extra = jax.ShapeDtypeStruct((tiles, 2 * NEAR, LANES), F32)
    values, ahead, behind, every, table = pl.pallas_call(
        functools.partial(analyse_kernel, segments, groups),
        out_shape=(
            jax.ShapeDtypeStruct((tiles, nodes, LANES), F32),
            extra,
            extra,
            jax.ShapeDtypeStruct((segments, tiles, 2 * FAR, LANES), F32),
            jax.ShapeDtypeStruct((4, nodes, LANES), F32),
        ),
        in_specs=[smem] + [whole_spec()] * 4 + [anywhere] * 3,
        out_specs=(whole_spec(),) * 5,
        scratch_shapes=[
            pltpu.VMEM((steps, group, rows, width), F32),
            pltpu.VMEM((2, group * rows, width), BF),
            pltpu.VMEM((2, group * rows, width), BF),
            pltpu.SemaphoreType.DMA((steps,)),
        ],
        compiler_params=flat,
        cost_estimate=cost(12),
        name="analyse",
    )(device, cut, places, gather_table, moment_table, wind_u, wind_v, tracer)

    def shifted(array, by):
        return lax.ppermute(array, "lon", [(i, (i + by) % segments) for i in range(segments)])

    every = lax.all_to_all(every, "lon", 0, 0)
    ahead, behind = shifted(ahead, 1), shifted(behind, -1)

    step_tiles = 4
    near, turn = pl.pallas_call(
        near_kernel_call,
        out_shape=(
            jax.ShapeDtypeStruct((tiles, LANES, wide), F32),
            jax.ShapeDtypeStruct((2, LANES, wide), F32),
        ),
        grid=(tiles // step_tiles,),
        in_specs=[whole_spec()] * 2
        + [pl.BlockSpec((step_tiles, nodes, LANES), lambda s: (s, 0, 0))],
        out_specs=(
            pl.BlockSpec((step_tiles, LANES, wide), lambda s: (s, 0, 0)),
            pl.BlockSpec((2, LANES, wide), lambda s: (0, 0, 0)),
        ),
        compiler_params=params,
        cost_estimate=cost(6),
        name="near",
    )(local_table, table, values)

    edge = jax.ShapeDtypeStruct((count, wide), F32)
    extra_spec = pl.BlockSpec((step_tiles, 2 * NEAR, LANES), lambda s, d: (s, 0, 0))
    pack, top, bottom = pl.pallas_call(
        functools.partial(combine_kernel, per_field, rows),
        out_shape=(jax.ShapeDtypeStruct((tiles, LANES, 2 * wide - LANES), BF), edge, edge),
        grid_spec=pltpu.PrefetchScalarGridSpec(
            num_scalar_prefetch=1,
            grid=(tiles // step_tiles,),
            in_specs=[whole_spec()] * 2
            + [pl.BlockSpec((1,) + far_table.shape[1:], lambda s, d: (d[0], 0, 0))]
            + [pl.BlockSpec((step_tiles, LANES, wide), lambda s, d: (s, 0, 0))]
            + [extra_spec, extra_spec]
            + [pl.BlockSpec((segments, step_tiles, 2 * FAR, LANES), lambda s, d: (0, s, 0, 0))],
            out_specs=(
                pl.BlockSpec((step_tiles, LANES, 2 * wide - LANES), lambda s, d: (s, 0, 0)),
                pl.BlockSpec((count, wide), lambda s, d: (0, 0)),
                pl.BlockSpec((count, wide), lambda s, d: (0, 0)),
            ),
        ),
        compiler_params=params,
        cost_estimate=cost(4),
        name="combine",
    )(device, scale, turn, far_table, near, ahead, behind, every)

    above = lax.ppermute(bottom, "lat", [(i, i + 1) for i in range(lats - 1)])
    below = lax.ppermute(top, "lat", [(i + 1, i) for i in range(lats - 1)])

    return pl.pallas_call(
        finish_kernel,
        out_shape=(jax.ShapeDtypeStruct((levels, rows, width), F32),) * 3,
        in_specs=[whole_spec()] * 5 + [anywhere],
        out_specs=(anywhere,) * 3,
        scratch_shapes=[
            pltpu.VMEM((tiles * LANES, lanes), F32),
            pltpu.VMEM((2 * count, lanes), F32),
            pltpu.VMEM((2, rows, LANES), F32),
            pltpu.VMEM((8, rows, width), F32),
            pltpu.SemaphoreType.DMA((2,)),
            pltpu.SemaphoreType.DMA((2, 3)),
        ],
        compiler_params=flat,
        cost_estimate=cost(12),
        name="finish",
    )(scale, spread_table, above, below, pack, tracer)


def solution(mesh):
    segments, lats = mesh.shape["lon"], mesh.shape["lat"]
    tables = tuple(make_tables(NLON // segments, segments))
    line = P(None, "lat", "lon")
    return jax.shard_map(
        functools.partial(on_device, segments, lats, tables),
        mesh=mesh,
        in_specs=(line, line, line, P("lat"), P("lat")),
        out_specs=(line, line, line),
        check_vma=False,
    )
```

time: 62 us -> 65.6 us (1.058)
  Pallas kernels: 33.7 us -> 42.7 us
  waiting for transfers between devices: 12.9 us -> 7.27 us
    pallas_call x3 -> x4, Pallas kernels: 33.7 us -> 42.7 us  [the longest x1 17.3 us: on_device(): pl.pallas_call(finish_kernel, out_shape=(jax.ShapeDtypeStruct((levels, ro...]
    ppermute x2, waiting for transfers between devices: 8.33 us -> 2.69 us  [shifted(): lax.ppermute(array, 'lon', [(i, (i + by) % segments) for i in range(segme...]
  transfers between devices with their start and end apart: 5 -> 5, of which waited for: 3 -> 3; matrix products, arithmetic and copies ran while one was open for 0% -> 0% of each run, Pallas kernels for 0% -> 9%
where the time goes in v5:
time: 65.6 us; the launch traced here: 65 us
  Pallas kernels  42.7 us (65%)
  starting transfers between devices  12.8 us (20%)
  waiting for transfers between devices  7.27 us (11%)
  local copies, waits for them, and re-layouts  1.44 us (2%)
  between operations  0.84 us (1%)
    pallas_call x1, Pallas kernels, on_device(): pl.pallas_call(finish_kernel, out_shape=(jax.ShapeDtypeStruct((levels, ro...  17.3 us
    pallas_call x1, Pallas kernels, on_device(): pl.pallas_call(functools.partial(analyse_kernel, segments, groups), out_s...  14.4 us
    pallas_call x1, Pallas kernels, on_device(): pl.pallas_call(near_kernel_call, out_shape=(jax.ShapeDtypeStruct((tiles,...  5.65 us
    pallas_call x1, Pallas kernels, on_device(): pl.pallas_call(functools.partial(combine_kernel, per_field, rows), out_sh...  5.33 us
    all_to_all x1, starting transfers between devices, on_device(): every = lax.all_to_all(every, 'lon', 0, 0)  5.19 us
    ppermute x1, waiting for transfers between devices, on_device(): below = lax.ppermute(top, 'lat', [(i + 1, i) for i in range(lats - 1)])  4.13 us
    ppermute x1, starting transfers between devices, on_device(): above = lax.ppermute(bottom, 'lat', [(i, i + 1) for i in range(lats - 1)])  3.46 us
    ppermute x2, starting transfers between devices, shifted(): lax.ppermute(array, 'lon', [(i, (i + by) % segments) for i in range(segme...  2.69 us
  transfers between devices with their start and end apart: 5, of which 3 were waited for; matrix products, arithmetic and copies ran while one was open for 0% of the time, Pallas kernels for 9%

profile of v5, /device:TPU:0, one launch (start us, length us, event | category | flops | bytes accessed | tf_op | source)
XLA Modules:
  0.0 65.0 jit_solution(13937335233234270568)
XLA Ops:
  0.6 14.4 %analyse.1 = (f32[12,288,128]{2,1,0:T(8,128)}, f32[12,24,128]{2,1,0:T(8,128)}, f32[12,24,128]{2,1,0:T(8,128)}, f32[8,12,8,128]{3,2,1,0:T(8,128)}, f32[4,288,128]{2,1,0:T(8,128)}) custom-call(s32[1]{0:T(128)} %bitcast.1.device_ref, s32[1,64]{1,0:T(1,128)} %bitcast.5, f32[2,288,1]{2,1,0:T(8,128)} %constant.16.clone.places_ref, ...), custom_call_target="tpu_custom_call" | custom-call | bytes 43200000 | tf_op jit(solution)/shard_map/analyse/pallas_call | solution.py:417
  15.0 5.2 %all-to-all-start = ((f32[8,12,8,128]{3,2,1,0:T(8,128)}), f32[8,12,8,128]{3,2,1,0:T(8,128)S(1)}, u32[]{:S(2)}, u32[]{:S(2)}) async-start(f32[8,12,8,128]{3,2,1,0:T(8,128)} %get-tuple-element.19), calls=%async_computation | async-start | bytes 786432 | tf_op jit(solution)/shard_map/all_to_all | solution.py:442
  20.2 0.5 collective-permute-start
  20.7 2.2 %collective-permute-start.1 = (f32[12,24,128]{2,1,0:T(8,128)}, f32[12,24,128]{2,1,0:T(8,128)S(1)}, u32[]{:S(2)}, u32[]{:S(2)}) collective-permute-start(f32[12,24,128]{2,1,0:T(8,128)} %get-tuple-element.18), channel_id=1, source_target_pairs={{0,7},{1,0},{2,1},{3,2},{4,3},{5,4},{6,5},{7,6},{8,15},{9,8},{10,9... | collective-permute-start | bytes 442376 | tf_op jit(solution)/shard_map/ppermute | solution.py:440
  22.9 5.6 %near.1 = (f32[12,128,384]{2,1,0:T(8,128)}, f32[2,128,384]{2,1,0:T(8,128)}) custom-call(bf16[288,864]{1,0:T(8,128)(2,1)} %constant.19.clone.local_ref, f32[4,288,128]{2,1,0:T(8,128)} %get-tuple-element.13.table_ref, f32[12,288,128]{2,1,0:T(8,128)} %get-tuple-element.14.node_ref), custom_call_target="tpu_custom_call" | custom-call | bytes 21600000 | tf_op jit(solution)/shard_map/near/pallas_call | solution.py:446
  28.6 2.7 %collective-permute-done.behind_ref = f32[12,24,128]{2,1,0:T(8,128)S(1)} collective-permute-done((f32[12,24,128]{2,1,0:T(8,128)}, f32[12,24,128]{2,1,0:T(8,128)S(1)}, u32[]{:S(2)}, u32[]{:S(2)}) %collective-permute-start) | collective-permute-done | bytes 147488 | tf_op jit(solution)/shard_map/ppermute | solution.py:440
  31.3 0.0 copy-start.1
  31.3 0.0 collective-permute-done.1.ahead_ref
  31.3 0.0 copy-start.2
  31.3 0.0 all-to-all-done.every_ref
  31.3 0.0 copy-start
  31.3 0.6 copy-done.1
  31.9 0.0 copy-done.2
  32.0 0.1 copy-done
  32.1 5.3 %combine.1 = (bf16[12,128,640]{2,1,0:T(8,128)(2,1)}, f32[24,384]{1,0:T(8,128)}, f32[24,384]{1,0:T(8,128)}) custom-call(s32[1]{0:T(128)} %bitcast.1.device_ref, f32[1,64]{1,0:T(1,128)} %bitcast.3, f32[2,128,384]{2,1,0:T(8,128)} %get-tuple-element.15.turn_ref, bf16[8,336,768]{2,1,0:T(8,128)(2,1)} %constant.20.clone.far_ref, ...), custom_call_target="tpu_custom_call" | custom-call | bytes 14400000 | tf_op jit(solution)/shard_map/combine/pallas_call | solution.py:466
  37.4 3.5 %collective-permute-start.2 = (f32[24,384]{1,0:T(8,128)}, f32[24,384]{1,0:T(8,128)S(1)}, u32[]{:S(2)}, u32[]{:S(2)}) collective-permute-start(f32[24,384]{1,0:T(8,128)} %get-tuple-element.20), channel_id=1, source_target_pairs={{0,8},{8,16},{16,24},{1,9},{9,17},{17,25},{2,10},{10,18},{18,26},{... | collective-permute-start | bytes 110600 | tf_op jit(solution)/shard_map/ppermute | solution.py:488
  40.9 1.5 %collective-permute-start.3 = (f32[24,384]{1,0:T(8,128)}, f32[24,384]{1,0:T(8,128)S(1)}, u32[]{:S(2)}, u32[]{:S(2)}) collective-permute-start(f32[24,384]{1,0:T(8,128)} %get-tuple-element.21), channel_id=1, source_target_pairs={{8,0},{16,8},{24,16},{9,1},{17,9},{25,17},{10,2},{18,10},{26,18},{... | collective-permute-start | bytes 110600 | tf_op jit(solution)/shard_map/ppermute | solution.py:489
  42.4 0.5 collective-permute-done.2.above_ref
  42.8 0.0 copy-start.3
  42.8 4.1 %collective-permute-done.3.below_ref = f32[24,384]{1,0:T(8,128)S(1)} collective-permute-done((f32[24,384]{1,0:T(8,128)}, f32[24,384]{1,0:T(8,128)S(1)}, u32[]{:S(2)}, u32[]{:S(2)}) %collective-permute-start.3) | collective-permute-done | bytes 36896 | tf_op jit(solution)/shard_map/ppermute | solution.py:489
  47.0 0.0 copy-start.4
  47.0 0.0 copy-done.3
  47.0 0.6 copy-done.4
  47.6 17.3 %finish.1 = (f32[8,64,1500]{2,1,0:T(8,128)}, f32[8,64,1500]{2,1,0:T(8,128)}, f32[8,64,1500]{2,1,0:T(8,128)}) custom-call(f32[1,64]{1,0:T(1,128)} %bitcast.4, bf16[896,1536]{1,0:T(8,128)(2,1)} %constant.21.clone.spread_ref, f32[24,384]{1,0:T(8,128)} %copy-done.3, f32[24,384]{1,0:T(8,128)} %copy-done.4, bf16[12,128,640]{2,1,0:T(8,128)(2,1)} %get-tuple-element.22.pack_ref, ...), custom_call_target="tpu_custom_call" | custom-call | bytes 43200000 | tf_op jit(solution)/shard_map/finish/pallas_call | solution.py:491
Async XLA Ops:
  15.0 16.2 %all-to-all-start = ((f32[8,12,8,128]{3,2,1,0:T(8,128)}), f32[8,12,8,128]{3,2,1,0:T(8,128)S(1)}, u32[]{:S(2)}, u32[]{:S(2)}) async-start(f32[8,12,8,128]{3,2,1,0:T(8,128)} %get-tuple-element.19), calls=%async_computation | async-start | bytes 786432 | tf_op jit(solution)/shard_map/all_to_all | solution.py:442
  20.2 11.0 %collective-permute-start = (f32[12,24,128]{2,1,0:T(8,128)}, f32[12,24,128]{2,1,0:T(8,128)S(1)}, u32[]{:S(2)}, u32[]{:S(2)}) collective-permute-start(f32[12,24,128]{2,1,0:T(8,128)} %get-tuple-element.17), channel_id=1, source_target_pairs={{0,1},{1,2},{2,3},{3,4},{4,5},{5,6},{6,7},{7,0},{8,9},{9,10},{10,1... | collective-permute-start | bytes 442376 | tf_op jit(solution)/shard_map/ppermute | solution.py:440
  20.7 10.5 %collective-permute-start.1 = (f32[12,24,128]{2,1,0:T(8,128)}, f32[12,24,128]{2,1,0:T(8,128)S(1)}, u32[]{:S(2)}, u32[]{:S(2)}) collective-permute-start(f32[12,24,128]{2,1,0:T(8,128)} %get-tuple-element.18), channel_id=1, source_target_pairs={{0,7},{1,0},{2,1},{3,2},{4,3},{5,4},{6,5},{7,6},{8,15},{9,8},{10,9... | collective-permute-start | bytes 442376 | tf_op jit(solution)/shard_map/ppermute | solution.py:440
  31.3 0.7 %copy-start.1 = (f32[12,24,128]{2,1,0:T(8,128)}, f32[12,24,128]{2,1,0:T(8,128)S(1)}, u32[]{:S(2)}) copy-start(f32[12,24,128]{2,1,0:T(8,128)S(1)} %collective-permute-done.behind_ref) | copy-start | bytes 442372
  31.3 0.7 %copy-start.2 = (f32[12,24,128]{2,1,0:T(8,128)}, f32[12,24,128]{2,1,0:T(8,128)S(1)}, u32[]{:S(2)}) copy-start(f32[12,24,128]{2,1,0:T(8,128)S(1)} %collective-permute-done.1.ahead_ref) | copy-start | bytes 442372
  31.3 0.8 %copy-start = (f32[8,12,8,128]{3,2,1,0:T(8,128)}, f32[8,12,8,128]{3,2,1,0:T(8,128)S(1)}, u32[]{:S(2)}) copy-start(f32[8,12,8,128]{3,2,1,0:T(8,128)S(1)} %all-to-all-done.every_ref) | copy-start | bytes 1179652
  37.4 5.4 %collective-permute-start.2 = (f32[24,384]{1,0:T(8,128)}, f32[24,384]{1,0:T(8,128)S(1)}, u32[]{:S(2)}, u32[]{:S(2)}) collective-permute-start(f32[24,384]{1,0:T(8,128)} %get-tuple-element.20), channel_id=1, source_target_pairs={{0,8},{8,16},{16,24},{1,9},{9,17},{17,25},{2,10},{10,18},{18,26},{... | collective-permute-start | bytes 110600 | tf_op jit(solution)/shard_map/ppermute | solution.py:488
  40.9 6.1 %collective-permute-start.3 = (f32[24,384]{1,0:T(8,128)}, f32[24,384]{1,0:T(8,128)S(1)}, u32[]{:S(2)}, u32[]{:S(2)}) collective-permute-start(f32[24,384]{1,0:T(8,128)} %get-tuple-element.21), channel_id=1, source_target_pairs={{8,0},{16,8},{24,16},{9,1},{17,9},{25,17},{10,2},{18,10},{26,18},{... | collective-permute-start | bytes 110600 | tf_op jit(solution)/shard_map/ppermute | solution.py:489
  42.8 4.1 %copy-start.3 = (f32[24,384]{1,0:T(8,128)}, f32[24,384]{1,0:T(8,128)S(1)}, u32[]{:S(2)}) copy-start(f32[24,384]{1,0:T(8,128)S(1)} %collective-permute-done.2.above_ref) | copy-start | bytes 110596
  47.0 0.6 copy-start.4

commit v6 on v5

--- a/solution.py
+++ b/solution.py
@@ -16,10 +16,10 @@
 FAR = 4
 EXTRA = 32
 LANES = 128
+GROUP = 4
 courant = 0.5
 BF = jnp.bfloat16
 F32 = jnp.float32
-VMEM_LIMIT = 56 * 1024 * 1024
 
 
 def prolate(points, band, count):
@@ -259,76 +259,84 @@
 
 
 def near_kernel_call(local_ref, table_ref, node_ref, near_ref, turn_ref):
-    tiles, nodes, _ = node_ref.shape
-
-    @pl.when(pl.program_id(0) == 0)
-    def _():
-        turn_ref[0] = turned_over(table_ref[2])
-        turn_ref[1] = turned_over(table_ref[3])
-
-    columns = []
-    for tile in range(tiles):
-        columns += [node_ref[tile] * table_ref[0], node_ref[tile] * table_ref[1]]
-    out = product(local_ref[...], stacked(jnp.concatenate(columns, axis=1)), ((1,), (0,)))
-    for tile in range(tiles):
-        at = 2 * tile * LANES
-        cosine, sine = out[:, at : at + LANES], out[:, at + LANES : at + 2 * LANES]
-        near_ref[tile] = turned_over(table_ref[3] * cosine - table_ref[2] * sine)
+    turn_ref[0] = turned_over(table_ref[2])
+    turn_ref[1] = turned_over(table_ref[3])
+    for start in range(0, node_ref.shape[0], GROUP):
+        columns = []
+        for tile in range(start, start + GROUP):
+            columns += [node_ref[tile] * table_ref[0], node_ref[tile] * table_ref[1]]
+        out = product(local_ref[...], stacked(jnp.concatenate(columns, axis=1)), ((1,), (0,)))
+        for tile in range(GROUP):
+            at = 2 * tile * LANES
+            cosine, sine = out[:, at : at + LANES], out[:, at + LANES : at + 2 * LANES]
+            near_ref[start + tile] = turned_over(table_ref[3] * cosine - table_ref[2] * sine)
 
 
 def combine_kernel(
-    per_field, rows, device_ref, scale_ref, turn_ref, far_ref, near_ref, behind_ref, ahead_ref,
+    per_field, rows, device_ref, scale_ref, turn_ref, far_ref, near_ref, before_ref, after_ref,
     every_ref, pack_ref, top_ref, bottom_ref,
 ):
-    step = pl.program_id(0)
     tiles, _, wide = near_ref.shape
     segments = every_ref.shape[0]
-    columns = []
-    for tile in range(tiles):
-        pieces = [behind_ref[tile], ahead_ref[tile]]
-        pieces += [every_ref[e, tile] for e in range(segments)]
-        columns.append(jnp.concatenate(pieces, axis=0))
-    got = product(stacked(jnp.concatenate(columns, axis=1)), far_ref[0], ((0,), (0,)))
     inverse = 1.0 / scale_ref[...]
-    for tile in range(tiles):
-        mine = got[tile * LANES : (tile + 1) * LANES]
-        values = near_ref[tile] + turn_ref[1] * mine[:, :wide] - turn_ref[0] * mine[:, wide:]
-        pack_ref[tile] = packed(values)
-        number = step * tiles + tile
-        wind = number < 2 * per_field
-        top_weight = jnp.where(wind, inverse[:, :1], 1.0)
-        bottom_weight = jnp.where(wind, inverse[:, rows - 1 :], 1.0)
-        pair = LANES // rows
-        for part in range(pair):
-            line = number * pair + part
-            top_ref[pl.ds(line, 1), :] = values[part * rows : part * rows + 1] * top_weight
-            last = part * rows + rows - 1
-            bottom_ref[pl.ds(line, 1), :] = values[last : last + 1] * bottom_weight
+    pair = LANES // rows
+    for start in range(0, tiles, GROUP):
+        columns = []
+        for tile in range(start, start + GROUP):
+            pieces = [before_ref[tile], after_ref[tile]]
+            pieces += [every_ref[e, tile] for e in range(segments)]
+            columns.append(jnp.concatenate(pieces, axis=0))
+        got = product(stacked(jnp.concatenate(columns, axis=1)), far_ref[0], ((0,), (0,)))
+        for tile in range(start, start + GROUP):
+            mine = got[(tile - start) * LANES : (tile - start + 1) * LANES]
+            values = near_ref[tile] + turn_ref[1] * mine[:, :wide] - turn_ref[0] * mine[:, wide:]
+            pack_ref[tile] = packed(values)
+            wind = tile < 2 * per_field
+            for part in range(pair):
+                line = tile * pair + part
+                first, last = part * rows, part * rows + rows - 1
+                top, bottom = values[first : first + 1], values[last : last + 1]
+                if wind:
+                    top, bottom = top * inverse[:, :1], bottom * inverse[:, rows - 1 :]
+                top_ref[line : line + 1] = top
+                bottom_ref[line : line + 1] = bottom
+
+
+def early_kernel(early, spread_ref, pack_ref, filtered_ref):
+    per_field = pack_ref.shape[0] // 3
+    pack = [pack_ref[f * per_field + tile] for tile in range(early) for f in range(3)]
+    values = spread_lines(jnp.concatenate(pack, axis=0), spread_ref)
+    filtered_ref[...] = values.reshape(filtered_ref.shape)
 
 
 def finish_kernel(
-    scale_ref, spread_ref, above_ref, below_ref, pack_ref, tracer_ref, *refs
+    scale_ref, spread_ref, above_ref, below_ref, pack_ref, early_ref, tracer_ref, *refs
 ):
     outs = refs[:3]
     filtered_ref, edge_ref, column_ref, held_ref, load_sems, sems = refs[3:]
     levels, rows, width = tracer_ref.shape
     lanes = spread_ref.shape[1]
     count = above_ref.shape[0]
-    tracer_slot = 6
+    pair = LANES // rows
+    steps = levels // pair
+    early = early_ref.shape[0]
+    tracer_slot = 6 * pair
 
     def load(step):
         return pltpu.make_async_copy(
-            tracer_ref.at[step], held_ref.at[tracer_slot + step % 2], load_sems.at[step % 2]
+            tracer_ref.at[pl.ds(step * pair, pair)],
+            held_ref.at[pl.ds(tracer_slot + step % 2 * pair, pair)],
+            load_sems.at[step % 2],
         )
 
     def store(step, number):
         return pltpu.make_async_copy(
-            held_ref.at[3 * (step % 2) + number], outs[number].at[step], sems.at[step % 2, number]
+            held_ref.at[pl.ds((3 * (step % 2) + number) * pair, pair)],
+            outs[number].at[pl.ds(step * pair, pair)],
+            sems.at[step % 2, number],
         )
 
     load(0).start()
-    pack = pack_ref[...].reshape(filtered_ref.shape[0], pack_ref.shape[2])
-    filtered_ref[...] = spread_lines(pack, spread_ref)
     edges = jnp.concatenate([above_ref[...], below_ref[...]], axis=0)
     edge_ref[...] = spread_lines(packed(edges), spread_ref)
     here = lax.broadcasted_iota(jnp.int32, (rows, rows), 0)
@@ -339,47 +347,57 @@
     column_ref[1] = 1.0 / column_ref[0]
     row_number = lax.broadcasted_iota(jnp.int32, (rows, 1), 0)
 
+    def fill(step):
+        pack = jnp.concatenate([pack_ref[f * steps + step] for f in range(3)], axis=0)
+        filtered_ref[step - early] = spread_lines(pack, spread_ref)
+
     def east_west(values):
         return pltpu.roll(values, lanes - 1, 1) - pltpu.roll(values, 1, 1)
 
-    def stencil(level):
+    def stencil(step):
         scale = column_ref[0][:, :1]
         inverse = column_ref[1][:, :1]
-
-        def field(number):
-            at = (number * levels + level) * rows
-            return filtered_ref[at : at + rows]
-
-        def north_south(values, number):
-            at = number * levels + level
-            above = edge_ref[at : at + 1]
-            below = edge_ref[count + at : count + at + 1]
-            later = jnp.where(row_number == rows - 1, below, pltpu.roll(values, rows - 1, 0))
-            earlier = jnp.where(row_number == 0, above, pltpu.roll(values, 1, 0))
-            return later - earlier
-
-        u, v, q = field(0), field(1), field(2)
-        div = scale * (east_west(u) + north_south(v * inverse, 1))
-        vort = scale * (east_west(v) - north_south(u * inverse, 0))
-        change = u * (courant * scale) * east_west(q) + (courant * v) * north_south(q, 2)
-        base = 3 * (level % 2)
-        held_ref[base] = held_ref[tracer_slot + level % 2] - change[:, :width]
-        held_ref[base + 1] = div[:, :width]
-        held_ref[base + 2] = vort[:, :width]
-
-    for level in range(levels):
-        if level + 1 < levels:
-            load(level + 1).start()
-        load(level).wait()
-        if level >= 2:
+        for part in range(pair):
+            level = step * pair + part
+
+            def field(number):
+                at = number * pair * rows + part * rows
+                if step < early:
+                    return early_ref[step, at : at + rows]
+                return filtered_ref[step - early, at : at + rows]
+
+            def north_south(values, number):
+                at = number * levels + level
+                above = edge_ref[at : at + 1]
+                below = edge_ref[count + at : count + at + 1]
+                later = jnp.where(row_number == rows - 1, below, pltpu.roll(values, rows - 1, 0))
+                earlier = jnp.where(row_number == 0, above, pltpu.roll(values, 1, 0))
+                return later - earlier
+
+            u, v, q = field(0), field(1), field(2)
+            div = scale * (east_west(u) + north_south(v * inverse, 1))
+            vort = scale * (east_west(v) - north_south(u * inverse, 0))
+            change = u * (courant * scale) * east_west(q) + (courant * v) * north_south(q, 2)
+            base = 3 * (step % 2) * pair + part
+            held_ref[base] = held_ref[tracer_slot + step % 2 * pair + part] - change[:, :width]
+            held_ref[base + pair] = div[:, :width]
+            held_ref[base + 2 * pair] = vort[:, :width]
+
+    for step in range(steps):
+        if step + 1 < steps:
+            load(step + 1).start()
+        load(step).wait()
+        if step >= 2:
             for number in range(3):
-                store(level - 2, number).wait()
-        stencil(level)
+                store(step - 2, number).wait()
+        stencil(step)
+        if step + early < steps:
+            fill(step + early)
         for number in range(3):
-            store(level, number).start()
-    for level in range(max(levels - 2, 0), levels):
+            store(step, number).start()
+    for step in range(max(steps - 2, 0), steps):
         for number in range(3):
-            store(level, number).wait()
+            store(step, number).wait()
 
 
 def whole_spec():
@@ -404,10 +422,8 @@
 
     smem = pl.BlockSpec(memory_space=pltpu.SMEM)
     anywhere = pl.BlockSpec(memory_space=pl.ANY)
-    params = pltpu.CompilerParams(
-        dimension_semantics=("arbitrary",), vmem_limit_bytes=VMEM_LIMIT
-    )
-    flat = pltpu.CompilerParams(vmem_limit_bytes=VMEM_LIMIT)
+    def limit(mib):
+        return pltpu.CompilerParams(vmem_limit_bytes=mib * 1024 * 1024)
 
     def cost(us):
         return pl.CostEstimate(flops=0, bytes_accessed=us * 3600000, transcendentals=0)
@@ -431,7 +447,7 @@
             pltpu.VMEM((2, group * rows, width), BF),
             pltpu.SemaphoreType.DMA((steps,)),
         ],
-        compiler_params=flat,
+        compiler_params=limit(50),
         cost_estimate=cost(12),
         name="analyse",
     )(device, cut, places, gather_table, moment_table, wind_u, wind_v, tracer)
@@ -442,45 +458,32 @@
     every = lax.all_to_all(every, "lon", 0, 0)
     ahead, behind = shifted(ahead, 1), shifted(behind, -1)
 
-    step_tiles = 4
     near, turn = pl.pallas_call(
         near_kernel_call,
         out_shape=(
             jax.ShapeDtypeStruct((tiles, LANES, wide), F32),
             jax.ShapeDtypeStruct((2, LANES, wide), F32),
         ),
-        grid=(tiles // step_tiles,),
-        in_specs=[whole_spec()] * 2
-        + [pl.BlockSpec((step_tiles, nodes, LANES), lambda s: (s, 0, 0))],
-        out_specs=(
-            pl.BlockSpec((step_tiles, LANES, wide), lambda s: (s, 0, 0)),
-            pl.BlockSpec((2, LANES, wide), lambda s: (0, 0, 0)),
-        ),
-        compiler_params=params,
+        in_specs=[whole_spec()] * 3,
+        out_specs=(whole_spec(),) * 2,
+        compiler_params=limit(24),
         cost_estimate=cost(6),
         name="near",
     )(local_table, table, values)
 
     edge = jax.ShapeDtypeStruct((count, wide), F32)
-    extra_spec = pl.BlockSpec((step_tiles, 2 * NEAR, LANES), lambda s, d: (s, 0, 0))
     pack, top, bottom = pl.pallas_call(
         functools.partial(combine_kernel, per_field, rows),
         out_shape=(jax.ShapeDtypeStruct((tiles, LANES, 2 * wide - LANES), BF), edge, edge),
         grid_spec=pltpu.PrefetchScalarGridSpec(
             num_scalar_prefetch=1,
-            grid=(tiles // step_tiles,),
+            grid=(1,),
             in_specs=[whole_spec()] * 2
             + [pl.BlockSpec((1,) + far_table.shape[1:], lambda s, d: (d[0], 0, 0))]
-            + [pl.BlockSpec((step_tiles, LANES, wide), lambda s, d: (s, 0, 0))]
-            + [extra_spec, extra_spec]
-            + [pl.BlockSpec((segments, step_tiles, 2 * FAR, LANES), lambda s, d: (0, s, 0, 0))],
-            out_specs=(
-                pl.BlockSpec((step_tiles, LANES, 2 * wide - LANES), lambda s, d: (s, 0, 0)),
-                pl.BlockSpec((count, wide), lambda s, d: (0, 0)),
-                pl.BlockSpec((count, wide), lambda s, d: (0, 0)),
-            ),
+            + [whole_spec()] * 4,
+            out_specs=(whole_spec(),) * 3,
         ),
-        compiler_params=params,
+        compiler_params=limit(24),
         cost_estimate=cost(4),
         name="combine",
     )(device, scale, turn, far_table, near, ahead, behind, every)
@@ -488,23 +491,34 @@
     above = lax.ppermute(bottom, "lat", [(i, i + 1) for i in range(lats - 1)])
     below = lax.ppermute(top, "lat", [(i + 1, i) for i in range(lats - 1)])
 
+    early = per_field // 2
+    filtered = pl.pallas_call(
+        functools.partial(early_kernel, early),
+        out_shape=jax.ShapeDtypeStruct((early, 3 * LANES, lanes), F32),
+        in_specs=[whole_spec()] * 2,
+        out_specs=whole_spec(),
+        compiler_params=limit(24),
+        cost_estimate=cost(4),
+        name="early",
+    )(spread_table, pack)
+
     return pl.pallas_call(
         finish_kernel,
         out_shape=(jax.ShapeDtypeStruct((levels, rows, width), F32),) * 3,
-        in_specs=[whole_spec()] * 5 + [anywhere],
+        in_specs=[whole_spec()] * 6 + [anywhere],
         out_specs=(anywhere,) * 3,
         scratch_shapes=[
-            pltpu.VMEM((tiles * LANES, lanes), F32),
+            pltpu.VMEM((per_field - early, 3 * LANES, lanes), F32),
             pltpu.VMEM((2 * count, lanes), F32),
             pltpu.VMEM((2, rows, LANES), F32),
-            pltpu.VMEM((8, rows, width), F32),
+            pltpu.VMEM((8 * pair, rows, width), F32),
             pltpu.SemaphoreType.DMA((2,)),
             pltpu.SemaphoreType.DMA((2, 3)),
         ],
-        compiler_params=flat,
-        cost_estimate=cost(12),
+        compiler_params=limit(32),
+        cost_estimate=cost(10),
         name="finish",
-    )(scale, spread_table, above, below, pack, tracer)
+    )(scale, spread_table, above, below, pack, filtered, tracer)
 
 
 def solution(mesh):

time: 65.6 us -> 60.9 us (0.928)
  Pallas kernels: 42.7 us -> 30.2 us
  local copies, waits for them, and re-layouts: 1.44 us -> 11.7 us
  waiting for transfers between devices: 7.27 us -> 4.64 us
    unnamed x10 -> x28, local copies, waits for them, and re-layouts: 1.44 us -> 11.7 us
    pallas_call x1, Pallas kernels: 17.3 us -> 9.8 us  [on_device(): pl.pallas_call(finish_kernel, out_shape=(jax.ShapeDtypeStruct((levels, ro...]
    pallas_call x1, Pallas kernels: 5.33 us -> 1.83 us  [on_device(): pl.pallas_call(functools.partial(combine_kernel, per_field, rows), out_sh...]
    pallas_call x1, Pallas kernels: 5.65 us -> 2.18 us  [on_device(): pl.pallas_call(near_kernel_call, out_shape=(jax.ShapeDtypeStruct((tiles,...]
    pallas_call x0 -> x1, Pallas kernels: none -> 2.59 us  [on_device(): pl.pallas_call(functools.partial(early_kernel, early), out_shape=jax.Shap...]
    ppermute x1, waiting for transfers between devices: 4.13 us -> 1.74 us  [on_device(): below = lax.ppermute(top, 'lat', [(i + 1, i) for i in range(lats - 1)])]
  transfers between devices with their start and end apart: 5 -> 5, of which waited for: 3 -> 2; matrix products, arithmetic and copies ran while one was open for 0% -> 0% of each run, Pallas kernels for 9% -> 8%
where the time goes in v6:
time: 60.9 us; the launch traced here: 60.4 us
  Pallas kernels  30.2 us (50%)
  starting transfers between devices  13 us (21%)
  local copies, waits for them, and re-layouts  11.7 us (19%)
  waiting for transfers between devices  4.64 us (8%)
  between operations  0.89 us (1%)
    pallas_call x1, Pallas kernels, on_device(): pl.pallas_call(functools.partial(analyse_kernel, segments, groups), out_s...  13.8 us
    unnamed x28, local copies, waits for them, and re-layouts  11.7 us
    pallas_call x1, Pallas kernels, on_device(): pl.pallas_call(finish_kernel, out_shape=(jax.ShapeDtypeStruct((levels, ro...  9.8 us
    all_to_all x1, starting transfers between devices, on_device(): every = lax.all_to_all(every, 'lon', 0, 0)  5.3 us
    ppermute x1, starting transfers between devices, on_device(): above = lax.ppermute(bottom, 'lat', [(i, i + 1) for i in range(lats - 1)])  3.48 us
    ppermute x2, waiting for transfers between devices, shifted(): lax.ppermute(array, 'lon', [(i, (i + by) % segments) for i in range(segme...  2.89 us
    ppermute x2, starting transfers between devices, shifted(): lax.ppermute(array, 'lon', [(i, (i + by) % segments) for i in range(segme...  2.69 us
    pallas_call x1, Pallas kernels, on_device(): pl.pallas_call(functools.partial(early_kernel, early), out_shape=jax.Shap...  2.59 us
  transfers between devices with their start and end apart: 5, of which 2 were waited for; matrix products, arithmetic and copies ran while one was open for 0% of the time, Pallas kernels for 8%

profile of v6, /device:TPU:0, one launch (start us, length us, event | category | flops | bytes accessed | tf_op | source)
XLA Modules:
  0.0 60.4 jit_solution(16584058882980846390)
XLA Ops:
  0.6 0.0 copy-start.8
  0.6 1.0 %copy-done.8 = f32[2,288,1]{2,1,0:T(8,128)S(1)} copy-done((f32[2,288,1]{2,1,0:T(8,128)S(1)}, f32[2,288,1]{2,1,0:T(8,128)}, u32[]{:S(2)}) %copy-start.8) | copy-done | bytes 2328
  1.6 0.9 %copy-done.11 = bf16[56,864]{1,0:T(8,128)(2,1)S(1)} copy-done((bf16[56,864]{1,0:T(8,128)(2,1)S(1)}, bf16[56,864]{1,0:T(8,128)(2,1)}, u32[]{:S(2)}) %copy-start.11) | copy-done | bytes 96792
  2.5 0.7 %copy-done.13 = s32[64]{0:T(128)S(1)} copy-done((s32[64]{0:T(128)S(1)}, s32[64]{0:T(128)}, u32[]{:S(2)}) %copy-start.13) | copy-done | bytes 280
  3.1 13.8 %analyse.1 = (f32[12,288,128]{2,1,0:T(8,128)S(1)}, f32[12,24,128]{2,1,0:T(8,128)}, f32[12,24,128]{2,1,0:T(8,128)}, f32[8,12,8,128]{3,2,1,0:T(8,128)}, f32[4,288,128]{2,1,0:T(8,128)S(1)}) custom-call(s32[1]{0:T(128)} %bitcast.1.device_ref, s32[1,64]{1,0:T(1,128)S(1)} %bitcast.5, f32[2,288,1]{2,1,0:T(8,128)S(1)} %copy-done.8, ...), custom_call_target="tpu_custom_call" | custom-call | bytes 43200000 | tf_op jit(solution)/shard_map/analyse/pallas_call | solution.py:433
  17.0 1.2 %copy-done.3 = f32[12,288,128]{2,1,0:T(8,128)} copy-done((f32[12,288,128]{2,1,0:T(8,128)}, f32[12,288,128]{2,1,0:T(8,128)S(1)}, u32[]{:S(2)}) %copy-start.3) | copy-done | bytes 1769496
  18.2 5.3 %all-to-all-start = ((f32[8,12,8,128]{3,2,1,0:T(8,128)}), f32[8,12,8,128]{3,2,1,0:T(8,128)S(1)}, u32[]{:S(2)}, u32[]{:S(2)}) async-start(f32[8,12,8,128]{3,2,1,0:T(8,128)} %get-tuple-element.19), calls=%async_computation | async-start | bytes 786432 | tf_op jit(solution)/shard_map/all_to_all | solution.py:458
  23.5 0.5 collective-permute-start
  24.0 2.2 %collective-permute-start.1 = (f32[12,24,128]{2,1,0:T(8,128)}, f32[12,24,128]{2,1,0:T(8,128)S(1)}, u32[]{:S(2)}, u32[]{:S(2)}) collective-permute-start(f32[12,24,128]{2,1,0:T(8,128)} %get-tuple-element.18), channel_id=1, source_target_pairs={{0,7},{1,0},{2,1},{3,2},{4,3},{5,4},{6,5},{7,6},{8,15},{9,8},{10,9... | collective-permute-start | bytes 442376 | tf_op jit(solution)/shard_map/ppermute | solution.py:456
  26.2 1.5 %copy-done.4 = f32[12,288,128]{2,1,0:T(8,128)S(1)} copy-done((f32[12,288,128]{2,1,0:T(8,128)S(1)}, f32[12,288,128]{2,1,0:T(8,128)}, u32[]{:S(2)}) %copy-start.4) | copy-done | bytes 1769496
  27.7 1.0 %copy-done.5 = bf16[288,864]{1,0:T(8,128)(2,1)S(1)} copy-done((bf16[288,864]{1,0:T(8,128)(2,1)S(1)}, bf16[288,864]{1,0:T(8,128)(2,1)}, u32[]{:S(2)}) %copy-start.5) | copy-done | bytes 497688
  28.7 2.2 %near.1 = (f32[12,128,384]{2,1,0:T(8,128)S(1)}, f32[2,128,384]{2,1,0:T(8,128)S(1)}) custom-call(bf16[288,864]{1,0:T(8,128)(2,1)S(1)} %copy-done.5, f32[4,288,128]{2,1,0:T(8,128)S(1)} %get-tuple-element.13.table_ref, f32[12,288,128]{2,1,0:T(8,128)S(1)} %copy-done.4), custom_call_target="tpu_custom_call" | custom-call | bytes 21600000 | tf_op jit(solution)/shard_map/near/pallas_call | solution.py:461
  30.9 0.7 %copy-done.6 = f32[2,128,384]{2,1,0:T(8,128)} copy-done((f32[2,128,384]{2,1,0:T(8,128)}, f32[2,128,384]{2,1,0:T(8,128)S(1)}, u32[]{:S(2)}) %copy-start.6) | copy-done | bytes 393240
  31.6 2.9 %collective-permute-done.before_ref = f32[12,24,128]{2,1,0:T(8,128)S(1)} collective-permute-done((f32[12,24,128]{2,1,0:T(8,128)}, f32[12,24,128]{2,1,0:T(8,128)S(1)}, u32[]{:S(2)}, u32[]{:S(2)}) %collective-permute-start) | collective-permute-done | bytes 147488 | tf_op jit(solution)/shard_map/ppermute | solution.py:456
  34.5 0.7 %copy-done.9 = f32[12,24,128]{2,1,0:T(8,128)} copy-done((f32[12,24,128]{2,1,0:T(8,128)}, f32[12,24,128]{2,1,0:T(8,128)S(1)}, u32[]{:S(2)}) %copy-start.9) | copy-done | bytes 147480
  35.2 2.2 %copy-done.2 = bf16[8,336,768]{2,1,0:T(8,128)(2,1)S(1)} copy-done((bf16[8,336,768]{2,1,0:T(8,128)(2,1)S(1)}, bf16[8,336,768]{2,1,0:T(8,128)(2,1)}, u32[]{:S(2)}) %copy-start.2) | copy-done | bytes 4128792
  37.4 1.0 %copy-done.7 = f32[2,128,384]{2,1,0:T(8,128)S(1)} copy-done((f32[2,128,384]{2,1,0:T(8,128)S(1)}, f32[2,128,384]{2,1,0:T(8,128)}, u32[]{:S(2)}) %copy-start.7) | copy-done | bytes 393240
  38.4 0.9 %copy-done.10 = f32[12,24,128]{2,1,0:T(8,128)S(1)} copy-done((f32[12,24,128]{2,1,0:T(8,128)S(1)}, f32[12,24,128]{2,1,0:T(8,128)}, u32[]{:S(2)}) %copy-start.10) | copy-done | bytes 147480
  39.3 1.8 %combine.1 = (bf16[12,128,640]{2,1,0:T(8,128)(2,1)S(1)}, f32[24,384]{1,0:T(8,128)S(1)}, f32[24,384]{1,0:T(8,128)S(1)}) custom-call(s32[1]{0:T(128)} %bitcast.1.device_ref, f32[1,64]{1,0:T(1,128)S(1)} %bitcast.3, f32[2,128,384]{2,1,0:T(8,128)S(1)} %copy-done.7, bf16[8,336,768]{2,1,0:T(8,128)(2,1)S(1)} %copy-done.2, ...), custom_call_target="tpu_custom_call" | custom-call | bytes 14400000 | tf_op jit(solution)/shard_map/combine/pallas_call | solution.py:475
  41.1 3.5 %collective-permute-start.2 = (f32[24,384]{1,0:T(8,128)S(1)}, f32[24,384]{1,0:T(8,128)S(1)}, u32[]{:S(2)}, u32[]{:S(2)}) collective-permute-start(f32[24,384]{1,0:T(8,128)S(1)} %get-tuple-element.20), channel_id=1, source_target_pairs={{0,8},{8,16},{16,24},{1,9},{9,17},{17,25},{2,10},{10,18},{18,26},{... | collective-permute-start | bytes 110600 | tf_op jit(solution)/shard_map/ppermute | solution.py:491
  44.6 1.5 %collective-permute-start.3 = (f32[24,384]{1,0:T(8,128)S(1)}, f32[24,384]{1,0:T(8,128)S(1)}, u32[]{:S(2)}, u32[]{:S(2)}) collective-permute-start(f32[24,384]{1,0:T(8,128)S(1)} %get-tuple-element.21), channel_id=1, source_target_pairs={{8,0},{16,8},{24,16},{9,1},{17,9},{25,17},{10,2},{18,10},{26,18},{... | collective-permute-start | bytes 110600 | tf_op jit(solution)/shard_map/ppermute | solution.py:492
  46.1 2.6 %early.1.early_ref = f32[2,384,1536]{2,1,0:T(8,128)S(1)} custom-call(bf16[896,1536]{1,0:T(8,128)(2,1)S(1)} %copy-done.1, bf16[12,128,640]{2,1,0:T(8,128)(2,1)S(1)} %get-tuple-element.22.pack_ref), custom_call_target="tpu_custom_call" | custom-call | bytes 14400000 | tf_op jit(solution)/shard_map/early/pallas_call | solution.py:495
  48.7 1.7 %collective-permute-done.3.below_ref = f32[24,384]{1,0:T(8,128)S(1)} collective-permute-done((f32[24,384]{1,0:T(8,128)S(1)}, f32[24,384]{1,0:T(8,128)S(1)}, u32[]{:S(2)}, u32[]{:S(2)}) %collective-permute-start.3) | collective-permute-done | bytes 36896 | tf_op jit(solution)/shard_map/ppermute | solution.py:492
  50.5 9.8 %finish.1 = (f32[8,64,1500]{2,1,0:T(8,128)}, f32[8,64,1500]{2,1,0:T(8,128)}, f32[8,64,1500]{2,1,0:T(8,128)}) custom-call(f32[1,64]{1,0:T(1,128)S(1)} %bitcast.4, bf16[896,1536]{1,0:T(8,128)(2,1)S(1)} %copy-done.1, f32[24,384]{1,0:T(8,128)S(1)} %collective-permute-done.2.above_ref, f32[24,384]{1,0:T(8,128)S(1)} %collective-permute-done.3.below_ref, ...), custom_call_target="tpu_custom_call" | custom-call | bytes 36000000 | tf_op jit(solution)/shard_map/finish/pallas_call | solution.py:505
  (19 shorter events, 0.0 us)
Async XLA Ops:
  0.6 1.0 %copy-start.8 = (f32[2,288,1]{2,1,0:T(8,128)S(1)}, f32[2,288,1]{2,1,0:T(8,128)}, u32[]{:S(2)}) copy-start(f32[2,288,1]{2,1,0:T(8,128)} %constant.16.clone.places_ref) | copy-start | bytes 6916
  1.6 0.9 %copy-start.11 = (bf16[56,864]{1,0:T(8,128)(2,1)S(1)}, bf16[56,864]{1,0:T(8,128)(2,1)}, u32[]{:S(2)}) copy-start(bf16[56,864]{1,0:T(8,128)(2,1)} %constant.18.clone.moment_ref) | copy-start | bytes 290308
  2.5 0.7 %copy-start.13 = (s32[64]{0:T(128)S(1)}, s32[64]{0:T(128)}, u32[]{:S(2)}) copy-start(s32[64]{0:T(128)} %param.14) | copy-start | bytes 772
  17.0 1.2 %copy-start.3 = (f32[12,288,128]{2,1,0:T(8,128)}, f32[12,288,128]{2,1,0:T(8,128)S(1)}, u32[]{:S(2)}) copy-start(f32[12,288,128]{2,1,0:T(8,128)S(1)} %get-tuple-element.14.node_ref) | copy-start | bytes 5308420
  18.2 17.0 %copy-start.12 = (f32[64]{0:T(128)S(1)}, f32[64]{0:T(128)}, u32[]{:S(2)}) copy-start(f32[64]{0:T(128)} %param.15) | copy-start | bytes 772
  18.2 17.0 %all-to-all-start = ((f32[8,12,8,128]{3,2,1,0:T(8,128)}), f32[8,12,8,128]{3,2,1,0:T(8,128)S(1)}, u32[]{:S(2)}, u32[]{:S(2)}) async-start(f32[8,12,8,128]{3,2,1,0:T(8,128)} %get-tuple-element.19), calls=%async_computation | async-start | bytes 786432 | tf_op jit(solution)/shard_map/all_to_all | solution.py:458
  23.5 11.0 %collective-permute-start = (f32[12,24,128]{2,1,0:T(8,128)}, f32[12,24,128]{2,1,0:T(8,128)S(1)}, u32[]{:S(2)}, u32[]{:S(2)}) collective-permute-start(f32[12,24,128]{2,1,0:T(8,128)} %get-tuple-element.17), channel_id=1, source_target_pairs={{0,1},{1,2},{2,3},{3,4},{4,5},{5,6},{6,7},{7,0},{8,9},{9,10},{10,1... | collective-permute-start | bytes 442376 | tf_op jit(solution)/shard_map/ppermute | solution.py:456
  24.0 10.5 %collective-permute-start.1 = (f32[12,24,128]{2,1,0:T(8,128)}, f32[12,24,128]{2,1,0:T(8,128)S(1)}, u32[]{:S(2)}, u32[]{:S(2)}) collective-permute-start(f32[12,24,128]{2,1,0:T(8,128)} %get-tuple-element.18), channel_id=1, source_target_pairs={{0,7},{1,0},{2,1},{3,2},{4,3},{5,4},{6,5},{7,6},{8,15},{9,8},{10,9... | collective-permute-start | bytes 442376 | tf_op jit(solution)/shard_map/ppermute | solution.py:456
  26.2 1.5 %copy-start.4 = (f32[12,288,128]{2,1,0:T(8,128)S(1)}, f32[12,288,128]{2,1,0:T(8,128)}, u32[]{:S(2)}) copy-start(f32[12,288,128]{2,1,0:T(8,128)} %copy-done.3) | copy-start | bytes 5308420
  27.7 1.0 %copy-start.5 = (bf16[288,864]{1,0:T(8,128)(2,1)S(1)}, bf16[288,864]{1,0:T(8,128)(2,1)}, u32[]{:S(2)}) copy-start(bf16[288,864]{1,0:T(8,128)(2,1)} %constant.19.clone.local_ref) | copy-start | bytes 1492996
  30.9 0.8 %copy-start.6 = (f32[2,128,384]{2,1,0:T(8,128)}, f32[2,128,384]{2,1,0:T(8,128)S(1)}, u32[]{:S(2)}) copy-start(f32[2,128,384]{2,1,0:T(8,128)S(1)} %get-tuple-element.15.turn_ref) | copy-start | bytes 1179652
  34.5 0.7 %copy-start.9 = (f32[12,24,128]{2,1,0:T(8,128)}, f32[12,24,128]{2,1,0:T(8,128)S(1)}, u32[]{:S(2)}) copy-start(f32[12,24,128]{2,1,0:T(8,128)S(1)} %collective-permute-done.1.after_ref) | copy-start | bytes 442372
  35.2 2.2 %copy-start.2 = (bf16[8,336,768]{2,1,0:T(8,128)(2,1)S(1)}, bf16[8,336,768]{2,1,0:T(8,128)(2,1)}, u32[]{:S(2)}) copy-start(bf16[8,336,768]{2,1,0:T(8,128)(2,1)} %constant.20.clone.far_ref) | copy-start | bytes 12386308
  37.4 1.0 %copy-start.7 = (f32[2,128,384]{2,1,0:T(8,128)S(1)}, f32[2,128,384]{2,1,0:T(8,128)}, u32[]{:S(2)}) copy-start(f32[2,128,384]{2,1,0:T(8,128)} %copy-done.6) | copy-start | bytes 1179652
  38.4 0.9 %copy-start.10 = (f32[12,24,128]{2,1,0:T(8,128)S(1)}, f32[12,24,128]{2,1,0:T(8,128)}, u32[]{:S(2)}) copy-start(f32[12,24,128]{2,1,0:T(8,128)} %copy-done.9) | copy-start | bytes 442372
  39.3 6.8 %copy-start.1 = (bf16[896,1536]{1,0:T(8,128)(2,1)S(1)}, bf16[896,1536]{1,0:T(8,128)(2,1)}, u32[]{:S(2)}) copy-start(bf16[896,1536]{1,0:T(8,128)(2,1)} %constant.21.clone.spread_ref) | copy-start | bytes 8257540
  41.1 7.6 %collective-permute-start.2 = (f32[24,384]{1,0:T(8,128)S(1)}, f32[24,384]{1,0:T(8,128)S(1)}, u32[]{:S(2)}, u32[]{:S(2)}) collective-permute-start(f32[24,384]{1,0:T(8,128)S(1)} %get-tuple-element.20), channel_id=1, source_target_pairs={{0,8},{8,16},{16,24},{1,9},{9,17},{17,25},{2,10},{10,18},{18,26},{... | collective-permute-start | bytes 110600 | tf_op jit(solution)/shard_map/ppermute | solution.py:491
  44.6 5.9 %collective-permute-start.3 = (f32[24,384]{1,0:T(8,128)S(1)}, f32[24,384]{1,0:T(8,128)S(1)}, u32[]{:S(2)}, u32[]{:S(2)}) collective-permute-start(f32[24,384]{1,0:T(8,128)S(1)} %get-tuple-element.21), channel_id=1, source_target_pairs={{8,0},{16,8},{24,16},{9,1},{17,9},{25,17},{10,2},{18,10},{26,18},{... | collective-permute-start | bytes 110600 | tf_op jit(solution)/shard_map/ppermute | solution.py:492
  46.1 4.4 %copy-start = (f32[8,64,1500]{2,1,0:T(8,128)S(1)}, f32[8,64,1500]{2,1,0:T(8,128)}, u32[]{:S(2)}) copy-start(f32[8,64,1500]{2,1,0:T(8,128)} %tracer_ref.1) | copy-start | bytes 9216004

commit v7 on v6

--- a/solution.py
+++ b/solution.py
@@ -188,7 +188,7 @@
 
 def analyse_kernel(
     segments, groups, device_ref, cut_ref, places_ref, gather_ref, moment_ref,
-    u_ref, v_ref, q_ref, node_ref, ahead_ref, behind_ref, every_ref, table_ref,
+    u_ref, v_ref, q_ref, node_ref, inner_ref, outer_ref, every_ref, table_ref,
     lines_ref, high_ref, low_ref, sems,
 ):
     width = u_ref.shape[2]
@@ -196,6 +196,7 @@
     lines = levels * rows
     nodes = gather_ref.shape[0] // 2
     me = device_ref[0]
+    even = lax.rem(me, 2) == 0
 
     copies = []
     for step in range(steps):
@@ -229,11 +230,12 @@
             mine = node_ref[tile]
             turned = jnp.concatenate([mine * table_ref[0], mine * table_ref[1]], axis=1)
             out = product(moment_ref[...], stacked(turned), ((1,), (0,)))
-            at = 0
-            for ref in (ahead_ref, behind_ref):
-                ref[tile, :NEAR] = out[at : at + NEAR, :LANES]
-                ref[tile, NEAR:] = out[at : at + NEAR, LANES:]
-                at += NEAR
+            ahead, behind = out[:NEAR], out[NEAR : 2 * NEAR]
+            inner, outer = jnp.where(even, ahead, behind), jnp.where(even, behind, ahead)
+            for ref, mine in ((inner_ref, inner), (outer_ref, outer)):
+                ref[tile, :NEAR] = mine[:, :LANES]
+                ref[tile, NEAR:] = mine[:, LANES:]
+            at = 2 * NEAR
             for s in range(1, segments):
                 to = lax.rem(me + s, segments)
                 every_ref[to, tile, :FAR] = out[at : at + FAR, :LANES]
@@ -273,20 +275,22 @@
 
 
 def combine_kernel(
-    per_field, rows, device_ref, scale_ref, turn_ref, far_ref, near_ref, before_ref, after_ref,
-    every_ref, pack_ref, top_ref, bottom_ref,
+    per_field, rows, lon_ref, lat_ref, scale_ref, turn_ref, far_ref, near_ref, inner_ref, outer_ref,
+    every_ref, pack_ref, first_ref, second_ref,
 ):
     tiles, _, wide = near_ref.shape
     segments = every_ref.shape[0]
+    even, even_lat = lax.rem(lon_ref[0], 2) == 0, lax.rem(lat_ref[0], 2) == 0
     inverse = 1.0 / scale_ref[...]
     pair = LANES // rows
     for start in range(0, tiles, GROUP):
         columns = []
         for tile in range(start, start + GROUP):
-            pieces = [before_ref[tile], after_ref[tile]]
+            inner, outer = inner_ref[tile], outer_ref[tile]
+            pieces = [jnp.where(even, outer, inner), jnp.where(even, inner, outer)]
             pieces += [every_ref[e, tile] for e in range(segments)]
             columns.append(jnp.concatenate(pieces, axis=0))
-        got = product(stacked(jnp.concatenate(columns, axis=1)), far_ref[0], ((0,), (0,)))
+        got = product(stacked(jnp.concatenate(columns, axis=1)), far_ref[...], ((0,), (0,)))
         for tile in range(start, start + GROUP):
             mine = got[(tile - start) * LANES : (tile - start + 1) * LANES]
             values = near_ref[tile] + turn_ref[1] * mine[:, :wide] - turn_ref[0] * mine[:, wide:]
@@ -298,8 +302,8 @@
                 top, bottom = values[first : first + 1], values[last : last + 1]
                 if wind:
                     top, bottom = top * inverse[:, :1], bottom * inverse[:, rows - 1 :]
-                top_ref[line : line + 1] = top
-                bottom_ref[line : line + 1] = bottom
+                first_ref[line : line + 1] = jnp.where(even_lat, bottom, top)
+                second_ref[line : line + 1] = jnp.where(even_lat, top, bottom)
 
 
 def early_kernel(early, spread_ref, pack_ref, filtered_ref):
@@ -310,13 +314,13 @@
 
 
 def finish_kernel(
-    scale_ref, spread_ref, above_ref, below_ref, pack_ref, early_ref, tracer_ref, *refs
+    lat_ref, scale_ref, spread_ref, first_ref, second_ref, pack_ref, early_ref, tracer_ref, *refs
 ):
     outs = refs[:3]
     filtered_ref, edge_ref, column_ref, held_ref, load_sems, sems = refs[3:]
     levels, rows, width = tracer_ref.shape
     lanes = spread_ref.shape[1]
-    count = above_ref.shape[0]
+    count = first_ref.shape[0]
     pair = LANES // rows
     steps = levels // pair
     early = early_ref.shape[0]
@@ -337,7 +341,10 @@
         )
 
     load(0).start()
-    edges = jnp.concatenate([above_ref[...], below_ref[...]], axis=0)
+    even_lat = lax.rem(lat_ref[0], 2) == 0
+    first, second = first_ref[...], second_ref[...]
+    above, below = jnp.where(even_lat, second, first), jnp.where(even_lat, first, second)
+    edges = jnp.concatenate([above, below], axis=0)
     edge_ref[...] = spread_lines(packed(edges), spread_ref)
     here = lax.broadcasted_iota(jnp.int32, (rows, rows), 0)
     there = lax.broadcasted_iota(jnp.int32, (rows, rows), 1)
@@ -416,7 +423,8 @@
     per_field = levels // pair
     tiles = 3 * per_field
     count = 3 * levels
-    device = lax.axis_index("lon").astype(jnp.int32)[None]
+    lon, lat = lax.axis_index("lon").astype(jnp.int32), lax.axis_index("lat").astype(jnp.int32)
+    lon, lat = lon[None], lat[None]
     cut = cutoff.reshape(1, rows)
     scale = row_scale.reshape(1, rows)
 
@@ -430,7 +438,7 @@
 
     steps = 3 * groups
     extra = jax.ShapeDtypeStruct((tiles, 2 * NEAR, LANES), F32)
-    values, ahead, behind, every, table = pl.pallas_call(
+    values, inner, outer, every, table = pl.pallas_call(
         functools.partial(analyse_kernel, segments, groups),
         out_shape=(
             jax.ShapeDtypeStruct((tiles, nodes, LANES), F32),
@@ -447,16 +455,19 @@
             pltpu.VMEM((2, group * rows, width), BF),
             pltpu.SemaphoreType.DMA((steps,)),
         ],
-        compiler_params=limit(50),
+        compiler_params=limit(56),
         cost_estimate=cost(12),
         name="analyse",
-    )(device, cut, places, gather_table, moment_table, wind_u, wind_v, tracer)
-
-    def shifted(array, by):
-        return lax.ppermute(array, "lon", [(i, (i + by) % segments) for i in range(segments)])
+    )(lon, cut, places, gather_table, moment_table, wind_u, wind_v, tracer)
+
+    def swapped(array, axis, start, closed):
+        size = segments if axis == "lon" else lats
+        pairs = [(i, (i + 1) % size) for i in range(start, size if closed else size - 1, 2)]
+        return lax.ppermute(array, axis, pairs + [(b, a) for a, b in pairs])
 
     every = lax.all_to_all(every, "lon", 0, 0)
-    ahead, behind = shifted(ahead, 1), shifted(behind, -1)
+    inner, outer = swapped(inner, "lon", 0, True), swapped(outer, "lon", 1, True)
+    far_mine = lax.dynamic_index_in_dim(jnp.asarray(far_table), lon[0], 0, False)
 
     near, turn = pl.pallas_call(
         near_kernel_call,
@@ -472,24 +483,17 @@
     )(local_table, table, values)
 
     edge = jax.ShapeDtypeStruct((count, wide), F32)
-    pack, top, bottom = pl.pallas_call(
+    pack, first, second = pl.pallas_call(
         functools.partial(combine_kernel, per_field, rows),
         out_shape=(jax.ShapeDtypeStruct((tiles, LANES, 2 * wide - LANES), BF), edge, edge),
-        grid_spec=pltpu.PrefetchScalarGridSpec(
-            num_scalar_prefetch=1,
-            grid=(1,),
-            in_specs=[whole_spec()] * 2
-            + [pl.BlockSpec((1,) + far_table.shape[1:], lambda s, d: (d[0], 0, 0))]
-            + [whole_spec()] * 4,
-            out_specs=(whole_spec(),) * 3,
-        ),
+        in_specs=[smem] * 2 + [whole_spec()] * 7,
+        out_specs=(whole_spec(),) * 3,
         compiler_params=limit(24),
         cost_estimate=cost(4),
         name="combine",
-    )(device, scale, turn, far_table, near, ahead, behind, every)
-
-    above = lax.ppermute(bottom, "lat", [(i, i + 1) for i in range(lats - 1)])
-    below = lax.ppermute(top, "lat", [(i + 1, i) for i in range(lats - 1)])
+    )(lon, lat, scale, turn, far_mine, near, inner, outer, every)
+
+    first, second = swapped(first, "lat", 0, False), swapped(second, "lat", 1, False)
 
     early = per_field // 2
     filtered = pl.pallas_call(
@@ -505,7 +509,7 @@
     return pl.pallas_call(
         finish_kernel,
         out_shape=(jax.ShapeDtypeStruct((levels, rows, width), F32),) * 3,
-        in_specs=[whole_spec()] * 6 + [anywhere],
+        in_specs=[smem] + [whole_spec()] * 6 + [anywhere],
         out_specs=(anywhere,) * 3,
         scratch_shapes=[
             pltpu.VMEM((per_field - early, 3 * LANES, lanes), F32),
@@ -518,7 +522,7 @@
         compiler_params=limit(32),
         cost_estimate=cost(10),
         name="finish",
-    )(scale, spread_table, above, below, pack, filtered, tracer)
+    )(lat, scale, spread_table, first, second, pack, filtered, tracer)
 
 
 def solution(mesh):

time: 60.9 us -> 54.4 us (0.89)
  the two profiles are of different devices: /device:TPU:0 before, /device:TPU:8 now
where the time goes in v7:
time: 54.4 us; the launch traced here: 54 us
  Pallas kernels  32.1 us (59%)
  starting transfers between devices  12.4 us (23%)
  local copies, waits for them, and re-layouts  8.59 us (16%)
  between operations  0.94 us (2%)
    pallas_call x1, Pallas kernels, on_device(): pl.pallas_call(functools.partial(analyse_kernel, segments, groups), out_s...  14.4 us
    pallas_call x1, Pallas kernels, on_device(): pl.pallas_call(finish_kernel, out_shape=(jax.ShapeDtypeStruct((levels, ro...  9.84 us
    ppermute x4, starting transfers between devices, swapped(): return lax.ppermute(array, axis, pairs + [(b, a) for a, b in pairs])  8.25 us
    unnamed x20, local copies, waits for them, and re-layouts  7.37 us
    all_to_all x1, starting transfers between devices, on_device(): every = lax.all_to_all(every, 'lon', 0, 0)  4.12 us
    pallas_call x1, Pallas kernels, on_device(): pl.pallas_call(functools.partial(combine_kernel, per_field, rows), out_sh...  2.94 us
    pallas_call x1, Pallas kernels, on_device(): pl.pallas_call(functools.partial(early_kernel, early), out_shape=jax.Shap...  2.59 us
    pallas_call x1, Pallas kernels, on_device(): pl.pallas_call(near_kernel_call, out_shape=(jax.ShapeDtypeStruct((tiles,...  2.3 us
  transfers between devices with their start and end apart: 5, of which 0 were waited for; matrix products, arithmetic and copies ran while one was open for 2% of the time, Pallas kernels for 9%

profile of v7, /device:TPU:8, one launch (start us, length us, event | category | flops | bytes accessed | tf_op | source)
XLA Modules:
  0.0 54.0 jit_solution(6692337590160205817)
XLA Ops:
  0.6 0.0 copy-start.6
  0.6 14.4 %analyse.1 = (f32[12,288,128]{2,1,0:T(8,128)}, f32[12,24,128]{2,1,0:T(8,128)}, f32[12,24,128]{2,1,0:T(8,128)}, f32[8,12,8,128]{3,2,1,0:T(8,128)}, f32[4,288,128]{2,1,0:T(8,128)}) custom-call(s32[1]{0:T(128)} %bitcast.2.device_ref.lon_ref, s32[1,64]{1,0:T(1,128)} %bitcast.8, f32[2,288,1]{2,1,0:T(8,128)} %constant.26.clone.places_ref, ...), custom_call_target="tpu_custom_call" | custom-call | bytes 43200000 | tf_op jit(solution)/shard_map/analyse/pallas_call | solution.py:441
  15.1 0.0 copy-start.9
  15.1 4.1 %all-to-all-start = ((f32[8,12,8,128]{3,2,1,0:T(8,128)}), f32[8,12,8,128]{3,2,1,0:T(8,128)}, u32[]{:S(2)}, u32[]{:S(2)}) async-start(f32[8,12,8,128]{3,2,1,0:T(8,128)} %get-tuple-element.19), calls=%async_computation | async-start | bytes 786432 | tf_op jit(solution)/shard_map/all_to_all | solution.py:468
  19.2 0.4 collective-permute-start
  19.6 2.6 %collective-permute-start.1 = (f32[12,24,128]{2,1,0:T(8,128)}, f32[12,24,128]{2,1,0:T(8,128)}, u32[]{:S(2)}, u32[]{:S(2)}) collective-permute-start(f32[12,24,128]{2,1,0:T(8,128)} %get-tuple-element.18), channel_id=1, source_target_pairs={{1,2},{3,4},{5,6},{7,0},{2,1},{4,3},{6,5},{0,7},{9,10},{11,12},{13... | collective-permute-start | bytes 442376 | tf_op jit(solution)/shard_map/ppermute | solution.py:466
  22.2 1.5 %copy-done.4 = f32[12,288,128]{2,1,0:T(8,128)S(1)} copy-done((f32[12,288,128]{2,1,0:T(8,128)S(1)}, f32[12,288,128]{2,1,0:T(8,128)}, u32[]{:S(2)}) %copy-start.4) | copy-done | bytes 1769496
  23.7 1.1 %copy-done.5 = f32[4,288,128]{2,1,0:T(8,128)S(1)} copy-done((f32[4,288,128]{2,1,0:T(8,128)S(1)}, f32[4,288,128]{2,1,0:T(8,128)}, u32[]{:S(2)}) %copy-start.5) | copy-done | bytes 589848
  24.7 2.3 %near.1 = (f32[12,128,384]{2,1,0:T(8,128)S(1)}, f32[2,128,384]{2,1,0:T(8,128)S(1)}) custom-call(bf16[288,864]{1,0:T(8,128)(2,1)S(1)} %copy-done.6, f32[4,288,128]{2,1,0:T(8,128)S(1)} %copy-done.5, f32[12,288,128]{2,1,0:T(8,128)S(1)} %copy-done.4), custom_call_target="tpu_custom_call" | custom-call | bytes 21600000 | tf_op jit(solution)/shard_map/near/pallas_call | solution.py:472
  27.0 1.4 %copy-done.2 = f32[12,128,384]{2,1,0:T(8,128)} copy-done((f32[12,128,384]{2,1,0:T(8,128)}, f32[12,128,384]{2,1,0:T(8,128)S(1)}, u32[]{:S(2)}) %copy-start.2) | copy-done | bytes 2359320
  28.4 0.7 %copy-done.7 = f32[2,128,384]{2,1,0:T(8,128)} copy-done((f32[2,128,384]{2,1,0:T(8,128)}, f32[2,128,384]{2,1,0:T(8,128)S(1)}, u32[]{:S(2)}) %copy-start.7) | copy-done | bytes 393240
  29.2 1.2 %dynamic-slice_bitcast_fusion.far_ref = bf16[336,768]{1,0:T(8,128)(2,1)S(1)} fusion(bf16[8,336,768]{2,1,0:T(8,128)(2,1)} %constant.29.clone, s32[]{:T(128)S(6)} %select_n.4), kind=kLoop, calls=%fused_computation | loop fusion | bytes 1032196 | tf_op jit(solution)/shard_map/jit(dynamic_index_in_dim)/squeeze | solution.py:470
  30.4 0.0 collective-permute-done.inner_ref
  30.4 0.0 collective-permute-done.1.outer_ref
  30.5 0.0 copy-start.3
  30.5 1.7 %copy-done.3 = f32[12,128,384]{2,1,0:T(8,128)S(1)} copy-done((f32[12,128,384]{2,1,0:T(8,128)S(1)}, f32[12,128,384]{2,1,0:T(8,128)}, u32[]{:S(2)}) %copy-start.3) | copy-done | bytes 2359320
  32.1 1.0 %copy-done.8 = f32[2,128,384]{2,1,0:T(8,128)S(1)} copy-done((f32[2,128,384]{2,1,0:T(8,128)S(1)}, f32[2,128,384]{2,1,0:T(8,128)}, u32[]{:S(2)}) %copy-start.8) | copy-done | bytes 393240
  33.1 2.9 %combine.1 = (bf16[12,128,640]{2,1,0:T(8,128)(2,1)S(1)}, f32[24,384]{1,0:T(8,128)S(1)}, f32[24,384]{1,0:T(8,128)S(1)}) custom-call(s32[1]{0:T(128)} %bitcast.2.device_ref.lon_ref, s32[1]{0:T(128)} %bitcast.lat_ref, f32[1,64]{1,0:T(1,128)S(1)} %bitcast.6, f32[2,128,384]{2,1,0:T(8,128)S(1)} %copy-done.8, ...), custom_call_target="tpu_custom_call" | custom-call | bytes 14400000 | tf_op jit(solution)/shard_map/combine/pallas_call | solution.py:486
  36.1 0.2 collective-permute-start.2
  36.3 5.1 %collective-permute-start.3 = (f32[24,384]{1,0:T(8,128)S(1)}, f32[24,384]{1,0:T(8,128)S(1)}, u32[]{:S(2)}, u32[]{:S(2)}) collective-permute-start(f32[24,384]{1,0:T(8,128)S(1)} %get-tuple-element.21), channel_id=1, source_target_pairs={{8,16},{16,8},{9,17},{17,9},{10,18},{18,10},{11,19},{19,11},{12,20... | collective-permute-start | bytes 110600 | tf_op jit(solution)/shard_map/ppermute | solution.py:466
  41.4 0.0 copy-start
  41.4 2.6 %early.1.early_ref = f32[2,384,1536]{2,1,0:T(8,128)S(1)} custom-call(bf16[896,1536]{1,0:T(8,128)(2,1)S(1)} %copy-done.1, bf16[12,128,640]{2,1,0:T(8,128)(2,1)S(1)} %get-tuple-element.22.pack_ref), custom_call_target="tpu_custom_call" | custom-call | bytes 14400000 | tf_op jit(solution)/shard_map/early/pallas_call | solution.py:499
  44.0 0.0 collective-permute-done.2.first_ref
  44.0 9.8 %finish.1 = (f32[8,64,1500]{2,1,0:T(8,128)}, f32[8,64,1500]{2,1,0:T(8,128)}, f32[8,64,1500]{2,1,0:T(8,128)}) custom-call(s32[1]{0:T(128)} %bitcast.lat_ref, f32[1,64]{1,0:T(1,128)S(1)} %bitcast.7, bf16[896,1536]{1,0:T(8,128)(2,1)S(1)} %copy-done.1, f32[24,384]{1,0:T(8,128)S(1)} %collective-permute-done.2.first_ref, ...), custom_call_target="tpu_custom_call" | custom-call | bytes 36000000 | tf_op jit(solution)/shard_map/finish/pallas_call | solution.py:509
  (12 shorter events, 0.0 us)
Async XLA Ops:
  0.6 21.6 %copy-start.6 = (bf16[288,864]{1,0:T(8,128)(2,1)S(1)}, bf16[288,864]{1,0:T(8,128)(2,1)}, u32[]{:S(2)}) copy-start(bf16[288,864]{1,0:T(8,128)(2,1)} %constant.30.clone.local_ref) | copy-start | bytes 1492996
  15.1 15.3 %copy-start.9 = (f32[64]{0:T(128)S(1)}, f32[64]{0:T(128)}, u32[]{:S(2)}) copy-start(f32[64]{0:T(128)} %param.15) | copy-start | bytes 772
  15.1 15.3 %all-to-all-start = ((f32[8,12,8,128]{3,2,1,0:T(8,128)}), f32[8,12,8,128]{3,2,1,0:T(8,128)}, u32[]{:S(2)}, u32[]{:S(2)}) async-start(f32[8,12,8,128]{3,2,1,0:T(8,128)} %get-tuple-element.19), calls=%async_computation | async-start | bytes 786432 | tf_op jit(solution)/shard_map/all_to_all | solution.py:468
  19.2 11.2 %collective-permute-start = (f32[12,24,128]{2,1,0:T(8,128)}, f32[12,24,128]{2,1,0:T(8,128)S(1)}, u32[]{:S(2)}, u32[]{:S(2)}) collective-permute-start(f32[12,24,128]{2,1,0:T(8,128)} %get-tuple-element.17), channel_id=1, source_target_pairs={{0,1},{2,3},{4,5},{6,7},{1,0},{3,2},{5,4},{7,6},{8,9},{10,11},{12,... | collective-permute-start | bytes 442376 | tf_op jit(solution)/shard_map/ppermute | solution.py:466
  19.6 10.8 %collective-permute-start.1 = (f32[12,24,128]{2,1,0:T(8,128)}, f32[12,24,128]{2,1,0:T(8,128)}, u32[]{:S(2)}, u32[]{:S(2)}) collective-permute-start(f32[12,24,128]{2,1,0:T(8,128)} %get-tuple-element.18), channel_id=1, source_target_pairs={{1,2},{3,4},{5,6},{7,0},{2,1},{4,3},{6,5},{0,7},{9,10},{11,12},{13... | collective-permute-start | bytes 442376 | tf_op jit(solution)/shard_map/ppermute | solution.py:466
  22.2 1.5 %copy-start.4 = (f32[12,288,128]{2,1,0:T(8,128)S(1)}, f32[12,288,128]{2,1,0:T(8,128)}, u32[]{:S(2)}) copy-start(f32[12,288,128]{2,1,0:T(8,128)} %get-tuple-element.14.node_ref) | copy-start | bytes 5308420
  23.7 1.1 %copy-start.5 = (f32[4,288,128]{2,1,0:T(8,128)S(1)}, f32[4,288,128]{2,1,0:T(8,128)}, u32[]{:S(2)}) copy-start(f32[4,288,128]{2,1,0:T(8,128)} %get-tuple-element.13.table_ref) | copy-start | bytes 1769476
  27.0 1.4 %copy-start.2 = (f32[12,128,384]{2,1,0:T(8,128)}, f32[12,128,384]{2,1,0:T(8,128)S(1)}, u32[]{:S(2)}) copy-start(f32[12,128,384]{2,1,0:T(8,128)S(1)} %get-tuple-element.16.near_ref) | copy-start | bytes 7077892
  28.4 0.7 %copy-start.7 = (f32[2,128,384]{2,1,0:T(8,128)}, f32[2,128,384]{2,1,0:T(8,128)S(1)}, u32[]{:S(2)}) copy-start(f32[2,128,384]{2,1,0:T(8,128)S(1)} %get-tuple-element.15.turn_ref) | copy-start | bytes 1179652
  29.2 12.2 %copy-start.1 = (bf16[896,1536]{1,0:T(8,128)(2,1)S(1)}, bf16[896,1536]{1,0:T(8,128)(2,1)}, u32[]{:S(2)}) copy-start(bf16[896,1536]{1,0:T(8,128)(2,1)} %constant.31.clone.spread_ref) | copy-start | bytes 8257540
  30.5 1.7 %copy-start.3 = (f32[12,128,384]{2,1,0:T(8,128)S(1)}, f32[12,128,384]{2,1,0:T(8,128)}, u32[]{:S(2)}) copy-start(f32[12,128,384]{2,1,0:T(8,128)} %copy-done.2) | copy-start | bytes 7077892
  32.1 1.0 %copy-start.8 = (f32[2,128,384]{2,1,0:T(8,128)S(1)}, f32[2,128,384]{2,1,0:T(8,128)}, u32[]{:S(2)}) copy-start(f32[2,128,384]{2,1,0:T(8,128)} %copy-done.7) | copy-start | bytes 1179652
  36.1 7.9 %collective-permute-start.2 = (f32[24,384]{1,0:T(8,128)S(1)}, f32[24,384]{1,0:T(8,128)S(1)}, u32[]{:S(2)}, u32[]{:S(2)}) collective-permute-start(f32[24,384]{1,0:T(8,128)S(1)} %get-tuple-element.20), channel_id=1, source_target_pairs={{0,8},{16,24},{8,0},{24,16},{1,9},{17,25},{9,1},{25,17},{2,10},{18... | collective-permute-start | bytes 110600 | tf_op jit(solution)/shard_map/ppermute | solution.py:466
  36.3 7.7 %collective-permute-start.3 = (f32[24,384]{1,0:T(8,128)S(1)}, f32[24,384]{1,0:T(8,128)S(1)}, u32[]{:S(2)}, u32[]{:S(2)}) collective-permute-start(f32[24,384]{1,0:T(8,128)S(1)} %get-tuple-element.21), channel_id=1, source_target_pairs={{8,16},{16,8},{9,17},{17,9},{10,18},{18,10},{11,19},{19,11},{12,20... | collective-permute-start | bytes 110600 | tf_op jit(solution)/shard_map/ppermute | solution.py:466
  41.4 2.6 %copy-start = (f32[8,64,1500]{2,1,0:T(8,128)S(1)}, f32[8,64,1500]{2,1,0:T(8,128)}, u32[]{:S(2)}) copy-start(f32[8,64,1500]{2,1,0:T(8,128)} %tracer_ref.1) | copy-start | bytes 9216004

commit v8 on v7

--- a/solution.py
+++ b/solution.py
@@ -16,6 +16,7 @@
 FAR = 4
 EXTRA = 32
 LANES = 128
+SUB = 8
 GROUP = 4
 courant = 0.5
 BF = jnp.bfloat16
@@ -187,9 +188,9 @@
 
 
 def analyse_kernel(
-    segments, groups, device_ref, cut_ref, places_ref, gather_ref, moment_ref,
-    u_ref, v_ref, q_ref, node_ref, inner_ref, outer_ref, every_ref, table_ref,
-    lines_ref, high_ref, low_ref, sems,
+    segments, groups, device_ref, cut_ref, places_ref, moment_ref, gather_in, far_in,
+    u_ref, v_ref, q_ref, node_out, inner_ref, outer_ref, every_ref, table_out, far_out,
+    lines_ref, high_ref, low_ref, gather_ref, node_ref, table_ref, sems, node_sems,
 ):
     width = u_ref.shape[2]
     steps, levels, rows, _ = lines_ref.shape
@@ -198,17 +199,24 @@
     me = device_ref[0]
     even = lax.rem(me, 2) == 0
 
-    copies = []
+    gather_copy = pltpu.make_async_copy(gather_in, gather_ref, sems.at[steps])
+    far_copy = pltpu.make_async_copy(far_in.at[me], far_out, sems.at[steps + 1])
+    table_copy = pltpu.make_async_copy(table_ref, table_out, sems.at[steps + 2])
+    copies, node_copies = [], []
     for step in range(steps):
         ref = (u_ref, v_ref, q_ref)[step // groups]
         levels_at = pl.ds((step % groups) * levels, levels)
         copies.append(pltpu.make_async_copy(ref.at[levels_at], lines_ref.at[step], sems.at[step]))
         copies[-1].start()
+        if step == 0:
+            gather_copy.start()
+    far_copy.start()
     for side in range(2):
         cosine, sine = phases(
             lane_cut(cut_ref), places_ref[side], me.astype(F32), segments, width
         )
         table_ref[2 * side], table_ref[2 * side + 1] = cosine, sine
+    table_copy.start()
     every_ref[me] = jnp.zeros(every_ref.shape[1:], F32)
 
     def cast(step):
@@ -244,6 +252,7 @@
 
     copies[0].wait()
     cast(0)
+    gather_copy.wait()
     for step in range(steps):
         if step + 1 < steps:
             copies[step + 1].wait()
@@ -252,7 +261,14 @@
             cast(step + 1)
         if step > 0:
             moments(step - 1)
+        tiles_at = pl.ds(step * (lines // LANES), lines // LANES)
+        node_copies.append(
+            pltpu.make_async_copy(node_ref.at[tiles_at], node_out.at[tiles_at], node_sems.at[step])
+        )
+        node_copies[-1].start()
     moments(steps - 1)
+    for copy in [table_copy, far_copy] + node_copies:
+        copy.wait()
 
 
 def turned_over(values):
@@ -352,7 +368,7 @@
     column = jnp.sum(column, axis=1, keepdims=True)
     column_ref[0] = jnp.broadcast_to(column, (rows, LANES))
     column_ref[1] = 1.0 / column_ref[0]
-    row_number = lax.broadcasted_iota(jnp.int32, (rows, 1), 0)
+    row_number = lax.broadcasted_iota(jnp.int32, (SUB, 1), 0)
 
     def fill(step):
         pack = jnp.concatenate([pack_ref[f * steps + step] for f in range(3)], axis=0)
@@ -377,9 +393,12 @@
                 at = number * levels + level
                 above = edge_ref[at : at + 1]
                 below = edge_ref[count + at : count + at + 1]
-                later = jnp.where(row_number == rows - 1, below, pltpu.roll(values, rows - 1, 0))
-                earlier = jnp.where(row_number == 0, above, pltpu.roll(values, 1, 0))
-                return later - earlier
+                later, earlier = pltpu.roll(values, rows - 1, 0), pltpu.roll(values, 1, 0)
+                low, high = slice(0, SUB), slice(rows - SUB, rows)
+                first = later[low] - jnp.where(row_number == 0, above, earlier[low])
+                last = jnp.where(row_number == SUB - 1, below, later[high]) - earlier[high]
+                inside = slice(SUB, rows - SUB)
+                return jnp.concatenate([first, later[inside] - earlier[inside], last], axis=0)
 
             u, v, q = field(0), field(1), field(2)
             div = scale * (east_west(u) + north_south(v * inverse, 1))
@@ -438,7 +457,7 @@
 
     steps = 3 * groups
     extra = jax.ShapeDtypeStruct((tiles, 2 * NEAR, LANES), F32)
-    values, inner, outer, every, table = pl.pallas_call(
+    values, inner, outer, every, table, far_mine = pl.pallas_call(
         functools.partial(analyse_kernel, segments, groups),
         out_shape=(
             jax.ShapeDtypeStruct((tiles, nodes, LANES), F32),
@@ -446,19 +465,24 @@
             extra,
             jax.ShapeDtypeStruct((segments, tiles, 2 * FAR, LANES), F32),
             jax.ShapeDtypeStruct((4, nodes, LANES), F32),
+            jax.ShapeDtypeStruct(far_table.shape[1:], BF),
         ),
-        in_specs=[smem] + [whole_spec()] * 4 + [anywhere] * 3,
-        out_specs=(whole_spec(),) * 5,
+        in_specs=[smem] + [whole_spec()] * 3 + [anywhere] * 5,
+        out_specs=(anywhere,) + (whole_spec(),) * 3 + (anywhere,) * 2,
         scratch_shapes=[
             pltpu.VMEM((steps, group, rows, width), F32),
             pltpu.VMEM((2, group * rows, width), BF),
             pltpu.VMEM((2, group * rows, width), BF),
+            pltpu.VMEM(gather_table.shape, BF),
+            pltpu.VMEM((tiles, nodes, LANES), F32),
+            pltpu.VMEM((4, nodes, LANES), F32),
+            pltpu.SemaphoreType.DMA((steps + 3,)),
             pltpu.SemaphoreType.DMA((steps,)),
         ],
         compiler_params=limit(56),
         cost_estimate=cost(12),
         name="analyse",
-    )(lon, cut, places, gather_table, moment_table, wind_u, wind_v, tracer)
+    )(lon, cut, places, moment_table, gather_table, far_table, wind_u, wind_v, tracer)
 
     def swapped(array, axis, start, closed):
         size = segments if axis == "lon" else lats
@@ -467,7 +491,6 @@
 
     every = lax.all_to_all(every, "lon", 0, 0)
     inner, outer = swapped(inner, "lon", 0, True), swapped(outer, "lon", 1, True)
-    far_mine = lax.dynamic_index_in_dim(jnp.asarray(far_table), lon[0], 0, False)
 
     near, turn = pl.pallas_call(
         near_kernel_call,

time: 54.4 us -> 58.2 us (1.070)
  Pallas kernels: 32.1 us -> 36.3 us
  local copies, waits for them, and re-layouts: 8.59 us -> 7.7 us
  waiting for transfers between devices: 0.01 us -> 0.79 us
    pallas_call x1, Pallas kernels: 14.4 us -> 18.7 us  [on_device(): pl.pallas_call(functools.partial(analyse_kernel, segments, groups), out_s...]
    squeeze x1 -> x0, local copies, waits for them, and re-layouts: 1.22 us -> none  [on_device(): lax.dynamic_index_in_dim(jnp.asarray(far_table), lon[0], 0, False)]
    ppermute x4, waiting for transfers between devices: 0.01 us -> 0.79 us  [swapped(): return lax.ppermute(array, axis, pairs + [(b, a) for a, b in pairs])]
    unnamed x20 -> x18, local copies, waits for them, and re-layouts: 7.37 us -> 7.7 us
  transfers between devices with their start and end apart: 5 -> 5, of which waited for: 0 -> 1; matrix products, arithmetic and copies ran while one was open for 2% -> 0% of each run, Pallas kernels for 9% -> 8%
where the time goes in v8:
time: 58.2 us; the launch traced here: 57.8 us
  Pallas kernels  36.3 us (62%)
  starting transfers between devices  12.1 us (21%)
  local copies, waits for them, and re-layouts  7.7 us (13%)
  between operations  0.89 us (2%)
  waiting for transfers between devices  0.79 us (1%)
    pallas_call x1, Pallas kernels, on_device(): pl.pallas_call(functools.partial(analyse_kernel, segments, groups), out_s...  18.7 us
    pallas_call x1, Pallas kernels, on_device(): pl.pallas_call(finish_kernel, out_shape=(jax.ShapeDtypeStruct((levels, ro...  9.78 us
    ppermute x4, starting transfers between devices, swapped(): return lax.ppermute(array, axis, pairs + [(b, a) for a, b in pairs])  8.33 us
    unnamed x18, local copies, waits for them, and re-layouts  7.7 us
    all_to_all x1, starting transfers between devices, on_device(): every = lax.all_to_all(every, 'lon', 0, 0)  3.74 us
    pallas_call x1, Pallas kernels, on_device(): pl.pallas_call(functools.partial(combine_kernel, per_field, rows), out_sh...  2.89 us
    pallas_call x1, Pallas kernels, on_device(): pl.pallas_call(functools.partial(early_kernel, early), out_shape=jax.Shap...  2.6 us
    pallas_call x1, Pallas kernels, on_device(): pl.pallas_call(near_kernel_call, out_shape=(jax.ShapeDtypeStruct((tiles,...  2.31 us
  transfers between devices with their start and end apart: 5, of which 1 were waited for; matrix products, arithmetic and copies ran while one was open for 0% of the time, Pallas kernels for 8%

profile of v8, /device:TPU:8, one launch (start us, length us, event | category | flops | bytes accessed | tf_op | source)
XLA Modules:
  0.0 57.8 jit_solution(18416908576153403647)
XLA Ops:
  0.6 18.7 %analyse.1 = (f32[12,288,128]{2,1,0:T(8,128)}, f32[12,24,128]{2,1,0:T(8,128)}, f32[12,24,128]{2,1,0:T(8,128)}, f32[8,12,8,128]{3,2,1,0:T(8,128)}, f32[4,288,128]{2,1,0:T(8,128)}, /*index=5*/bf16[336,768]{1,0:T(8,128)(2,1)}) custom-call(s32[1]{0:T(128)} %bitcast.2.device_ref.lon_ref, s32[1,64]{1,0:T(1,128)} %bitcast.6, ...), custom_call_target="tpu_custom_call" | custom-call | bytes 43200000 | tf_op jit(solution)/shard_map/analyse/pallas_call | solution.py:460
  19.4 0.0 copy-start.8
  19.4 3.7 %all-to-all-start = ((f32[8,12,8,128]{3,2,1,0:T(8,128)}), f32[8,12,8,128]{3,2,1,0:T(8,128)S(1)}, u32[]{:S(2)}, u32[]{:S(2)}) async-start(f32[8,12,8,128]{3,2,1,0:T(8,128)} %get-tuple-element.21), calls=%async_computation | async-start | bytes 786432 | tf_op jit(solution)/shard_map/all_to_all | solution.py:492
  23.1 0.5 collective-permute-start
  23.6 2.5 %collective-permute-start.1 = (f32[12,24,128]{2,1,0:T(8,128)}, f32[12,24,128]{2,1,0:T(8,128)}, u32[]{:S(2)}, u32[]{:S(2)}) collective-permute-start(f32[12,24,128]{2,1,0:T(8,128)} %get-tuple-element.20), channel_id=1, source_target_pairs={{1,2},{3,4},{5,6},{7,0},{2,1},{4,3},{6,5},{0,7},{9,10},{11,12},{13... | collective-permute-start | bytes 442376 | tf_op jit(solution)/shard_map/ppermute | solution.py:490
  26.2 1.5 %copy-done.4 = f32[12,288,128]{2,1,0:T(8,128)S(1)} copy-done((f32[12,288,128]{2,1,0:T(8,128)S(1)}, f32[12,288,128]{2,1,0:T(8,128)}, u32[]{:S(2)}) %copy-start.4) | copy-done | bytes 1769496
  27.7 1.1 %copy-done.5 = f32[4,288,128]{2,1,0:T(8,128)S(1)} copy-done((f32[4,288,128]{2,1,0:T(8,128)S(1)}, f32[4,288,128]{2,1,0:T(8,128)}, u32[]{:S(2)}) %copy-start.5) | copy-done | bytes 589848
  28.7 1.0 %copy-done.7 = bf16[288,864]{1,0:T(8,128)(2,1)S(1)} copy-done((bf16[288,864]{1,0:T(8,128)(2,1)S(1)}, bf16[288,864]{1,0:T(8,128)(2,1)}, u32[]{:S(2)}) %copy-start.7) | copy-done | bytes 497688
  29.8 2.3 %near.1 = (f32[12,128,384]{2,1,0:T(8,128)S(1)}, f32[2,128,384]{2,1,0:T(8,128)S(1)}) custom-call(bf16[288,864]{1,0:T(8,128)(2,1)S(1)} %copy-done.7, f32[4,288,128]{2,1,0:T(8,128)S(1)} %copy-done.5, f32[12,288,128]{2,1,0:T(8,128)S(1)} %copy-done.4), custom_call_target="tpu_custom_call" | custom-call | bytes 21600000 | tf_op jit(solution)/shard_map/near/pallas_call | solution.py:495
  32.1 0.0 copy-start.2
  32.1 1.4 %copy-done.2 = f32[12,128,384]{2,1,0:T(8,128)} copy-done((f32[12,128,384]{2,1,0:T(8,128)}, f32[12,128,384]{2,1,0:T(8,128)S(1)}, u32[]{:S(2)}) %copy-start.2) | copy-done | bytes 2359320
  33.5 0.0 collective-permute-done.inner_ref
  33.5 0.8 %collective-permute-done.1.outer_ref = f32[12,24,128]{2,1,0:T(8,128)} collective-permute-done((f32[12,24,128]{2,1,0:T(8,128)}, f32[12,24,128]{2,1,0:T(8,128)}, u32[]{:S(2)}, u32[]{:S(2)}) %collective-permute-start.1) | collective-permute-done | bytes 147488 | tf_op jit(solution)/shard_map/ppermute | solution.py:490
  34.3 0.0 all-to-all-done.every_ref
  34.3 1.7 %copy-done.3 = f32[12,128,384]{2,1,0:T(8,128)S(1)} copy-done((f32[12,128,384]{2,1,0:T(8,128)S(1)}, f32[12,128,384]{2,1,0:T(8,128)}, u32[]{:S(2)}) %copy-start.3) | copy-done | bytes 2359320
  35.9 1.0 %copy-done.6 = bf16[336,768]{1,0:T(8,128)(2,1)S(1)} copy-done((bf16[336,768]{1,0:T(8,128)(2,1)S(1)}, bf16[336,768]{1,0:T(8,128)(2,1)}, u32[]{:S(2)}) %copy-start.6) | copy-done | bytes 516120
  37.0 2.9 %combine.1 = (bf16[12,128,640]{2,1,0:T(8,128)(2,1)S(1)}, f32[24,384]{1,0:T(8,128)S(1)}, f32[24,384]{1,0:T(8,128)S(1)}) custom-call(s32[1]{0:T(128)} %bitcast.2.device_ref.lon_ref, s32[1]{0:T(128)} %bitcast.lat_ref, f32[1,64]{1,0:T(1,128)S(1)} %bitcast.4, f32[2,128,384]{2,1,0:T(8,128)S(1)} %get-tuple-element.16.turn_ref, bf16[336,768]{1,0:T(8,128)(2,1)S(1)} %copy-done.6, ...), custom_call_target="tpu_custom_call" | custom-call | bytes 14400000 | tf_op jit(solution)/shard_map/combine/pallas_call | solution.py:509
  39.9 0.5 collective-permute-start.2
  40.4 4.8 %collective-permute-start.3 = (f32[24,384]{1,0:T(8,128)S(1)}, f32[24,384]{1,0:T(8,128)S(1)}, u32[]{:S(2)}, u32[]{:S(2)}) collective-permute-start(f32[24,384]{1,0:T(8,128)S(1)} %get-tuple-element.23), channel_id=1, source_target_pairs={{8,16},{16,8},{9,17},{17,9},{10,18},{18,10},{11,19},{19,11},{12,20... | collective-permute-start | bytes 110600 | tf_op jit(solution)/shard_map/ppermute | solution.py:490
  45.2 0.0 copy-start
  45.2 2.6 %early.1.early_ref = f32[2,384,1536]{2,1,0:T(8,128)S(1)} custom-call(bf16[896,1536]{1,0:T(8,128)(2,1)S(1)} %copy-done.1, bf16[12,128,640]{2,1,0:T(8,128)(2,1)S(1)} %get-tuple-element.24.pack_ref), custom_call_target="tpu_custom_call" | custom-call | bytes 14400000 | tf_op jit(solution)/shard_map/early/pallas_call | solution.py:522
  47.8 0.0 collective-permute-done.2.first_ref
  47.8 0.0 collective-permute-done.3.second_ref
  47.8 9.8 %finish.1 = (f32[8,64,1500]{2,1,0:T(8,128)}, f32[8,64,1500]{2,1,0:T(8,128)}, f32[8,64,1500]{2,1,0:T(8,128)}) custom-call(s32[1]{0:T(128)} %bitcast.lat_ref, f32[1,64]{1,0:T(1,128)S(1)} %bitcast.5, bf16[896,1536]{1,0:T(8,128)(2,1)S(1)} %copy-done.1, f32[24,384]{1,0:T(8,128)S(1)} %collective-permute-done.2.first_ref, ...), custom_call_target="tpu_custom_call" | custom-call | bytes 36000000 | tf_op jit(solution)/shard_map/finish/pallas_call | solution.py:532
  (9 shorter events, 0.0 us)
Async XLA Ops:
  19.4 14.9 %copy-start.8 = (f32[64]{0:T(128)S(1)}, f32[64]{0:T(128)}, u32[]{:S(2)}) copy-start(f32[64]{0:T(128)} %param.15) | copy-start | bytes 772
  19.4 14.9 %all-to-all-start = ((f32[8,12,8,128]{3,2,1,0:T(8,128)}), f32[8,12,8,128]{3,2,1,0:T(8,128)S(1)}, u32[]{:S(2)}, u32[]{:S(2)}) async-start(f32[8,12,8,128]{3,2,1,0:T(8,128)} %get-tuple-element.21), calls=%async_computation | async-start | bytes 786432 | tf_op jit(solution)/shard_map/all_to_all | solution.py:492
  23.1 10.3 %collective-permute-start = (f32[12,24,128]{2,1,0:T(8,128)}, f32[12,24,128]{2,1,0:T(8,128)}, u32[]{:S(2)}, u32[]{:S(2)}) collective-permute-start(f32[12,24,128]{2,1,0:T(8,128)} %get-tuple-element.19), channel_id=1, source_target_pairs={{0,1},{2,3},{4,5},{6,7},{1,0},{3,2},{5,4},{7,6},{8,9},{10,11},{12,... | collective-permute-start | bytes 442376 | tf_op jit(solution)/shard_map/ppermute | solution.py:490
  23.6 10.6 %collective-permute-start.1 = (f32[12,24,128]{2,1,0:T(8,128)}, f32[12,24,128]{2,1,0:T(8,128)}, u32[]{:S(2)}, u32[]{:S(2)}) collective-permute-start(f32[12,24,128]{2,1,0:T(8,128)} %get-tuple-element.20), channel_id=1, source_target_pairs={{1,2},{3,4},{5,6},{7,0},{2,1},{4,3},{6,5},{0,7},{9,10},{11,12},{13... | collective-permute-start | bytes 442376 | tf_op jit(solution)/shard_map/ppermute | solution.py:490
  26.2 1.5 %copy-start.4 = (f32[12,288,128]{2,1,0:T(8,128)S(1)}, f32[12,288,128]{2,1,0:T(8,128)}, u32[]{:S(2)}) copy-start(f32[12,288,128]{2,1,0:T(8,128)} %get-tuple-element.15.node_ref) | copy-start | bytes 5308420
  27.7 1.1 %copy-start.5 = (f32[4,288,128]{2,1,0:T(8,128)S(1)}, f32[4,288,128]{2,1,0:T(8,128)}, u32[]{:S(2)}) copy-start(f32[4,288,128]{2,1,0:T(8,128)} %get-tuple-element.14.table_ref) | copy-start | bytes 1769476
  28.7 1.0 %copy-start.7 = (bf16[288,864]{1,0:T(8,128)(2,1)S(1)}, bf16[288,864]{1,0:T(8,128)(2,1)}, u32[]{:S(2)}) copy-start(bf16[288,864]{1,0:T(8,128)(2,1)} %constant.24.clone.local_ref) | copy-start | bytes 1492996
  29.8 15.4 %copy-start.1 = (bf16[896,1536]{1,0:T(8,128)(2,1)S(1)}, bf16[896,1536]{1,0:T(8,128)(2,1)}, u32[]{:S(2)}) copy-start(bf16[896,1536]{1,0:T(8,128)(2,1)} %constant.25.clone.spread_ref) | copy-start | bytes 8257540
  32.1 1.4 %copy-start.2 = (f32[12,128,384]{2,1,0:T(8,128)}, f32[12,128,384]{2,1,0:T(8,128)S(1)}, u32[]{:S(2)}) copy-start(f32[12,128,384]{2,1,0:T(8,128)S(1)} %get-tuple-element.18.near_ref) | copy-start | bytes 7077892
  34.3 1.7 %copy-start.3 = (f32[12,128,384]{2,1,0:T(8,128)S(1)}, f32[12,128,384]{2,1,0:T(8,128)}, u32[]{:S(2)}) copy-start(f32[12,128,384]{2,1,0:T(8,128)} %copy-done.2) | copy-start | bytes 7077892
  35.9 1.0 %copy-start.6 = (bf16[336,768]{1,0:T(8,128)(2,1)S(1)}, bf16[336,768]{1,0:T(8,128)(2,1)}, u32[]{:S(2)}) copy-start(bf16[336,768]{1,0:T(8,128)(2,1)} %get-tuple-element.17.far_ref) | copy-start | bytes 1548292
  39.9 7.9 %collective-permute-start.2 = (f32[24,384]{1,0:T(8,128)S(1)}, f32[24,384]{1,0:T(8,128)S(1)}, u32[]{:S(2)}, u32[]{:S(2)}) collective-permute-start(f32[24,384]{1,0:T(8,128)S(1)} %get-tuple-element.22), channel_id=1, source_target_pairs={{0,8},{16,24},{8,0},{24,16},{1,9},{17,25},{9,1},{25,17},{2,10},{18... | collective-permute-start | bytes 110600 | tf_op jit(solution)/shard_map/ppermute | solution.py:490
  40.4 7.4 %collective-permute-start.3 = (f32[24,384]{1,0:T(8,128)S(1)}, f32[24,384]{1,0:T(8,128)S(1)}, u32[]{:S(2)}, u32[]{:S(2)}) collective-permute-start(f32[24,384]{1,0:T(8,128)S(1)} %get-tuple-element.23), channel_id=1, source_target_pairs={{8,16},{16,8},{9,17},{17,9},{10,18},{18,10},{11,19},{19,11},{12,20... | collective-permute-start | bytes 110600 | tf_op jit(solution)/shard_map/ppermute | solution.py:490
  45.2 2.6 %copy-start = (f32[8,64,1500]{2,1,0:T(8,128)S(1)}, f32[8,64,1500]{2,1,0:T(8,128)}, u32[]{:S(2)}) copy-start(f32[8,64,1500]{2,1,0:T(8,128)} %tracer_ref.1) | copy-start | bytes 9216004

commit v9 on v7

--- a/solution.py
+++ b/solution.py
@@ -16,6 +16,7 @@
 FAR = 4
 EXTRA = 32
 LANES = 128
+SUB = 8
 GROUP = 4
 courant = 0.5
 BF = jnp.bfloat16
@@ -275,22 +276,31 @@
 
 
 def combine_kernel(
-    per_field, rows, lon_ref, lat_ref, scale_ref, turn_ref, far_ref, near_ref, inner_ref, outer_ref,
-    every_ref, pack_ref, first_ref, second_ref,
+    per_field, rows, lon_ref, lat_ref, scale_ref, turn_ref, far_ref, inner_ref, outer_ref, every_ref,
+    near_in, pack_out, first_ref, second_ref, near_ref, pack_ref, in_sems, out_sems,
 ):
     tiles, _, wide = near_ref.shape
     segments = every_ref.shape[0]
     even, even_lat = lax.rem(lon_ref[0], 2) == 0, lax.rem(lat_ref[0], 2) == 0
     inverse = 1.0 / scale_ref[...]
     pair = LANES // rows
-    for start in range(0, tiles, GROUP):
+
+    def moved(start, source, target, sems):
+        at = pl.ds(start, GROUP)
+        return pltpu.make_async_copy(source.at[at], target.at[at], sems.at[start // GROUP])
+
+    starts = range(0, tiles, GROUP)
+    for start in starts:
+        moved(start, near_in, near_ref, in_sems).start()
+    for start in starts:
         columns = []
         for tile in range(start, start + GROUP):
             inner, outer = inner_ref[tile], outer_ref[tile]
             pieces = [jnp.where(even, outer, inner), jnp.where(even, inner, outer)]
             pieces += [every_ref[e, tile] for e in range(segments)]
             columns.append(jnp.concatenate(pieces, axis=0))
-        got = product(stacked(jnp.concatenate(columns, axis=1)), far_ref[...], ((0,), (0,)))
+        got = product(stacked(jnp.concatenate(columns, axis=1)), far_ref[0], ((0,), (0,)))
+        moved(start, near_in, near_ref, in_sems).wait()
         for tile in range(start, start + GROUP):
             mine = got[(tile - start) * LANES : (tile - start + 1) * LANES]
             values = near_ref[tile] + turn_ref[1] * mine[:, :wide] - turn_ref[0] * mine[:, wide:]
@@ -304,6 +314,9 @@
                     top, bottom = top * inverse[:, :1], bottom * inverse[:, rows - 1 :]
                 first_ref[line : line + 1] = jnp.where(even_lat, bottom, top)
                 second_ref[line : line + 1] = jnp.where(even_lat, top, bottom)
+        moved(start, pack_ref, pack_out, out_sems).start()
+    for start in starts:
+        moved(start, pack_ref, pack_out, out_sems).wait()
 
 
 def early_kernel(early, spread_ref, pack_ref, filtered_ref):
@@ -352,7 +365,7 @@
     column = jnp.sum(column, axis=1, keepdims=True)
     column_ref[0] = jnp.broadcast_to(column, (rows, LANES))
     column_ref[1] = 1.0 / column_ref[0]
-    row_number = lax.broadcasted_iota(jnp.int32, (rows, 1), 0)
+    row_number = lax.broadcasted_iota(jnp.int32, (SUB, 1), 0)
 
     def fill(step):
         pack = jnp.concatenate([pack_ref[f * steps + step] for f in range(3)], axis=0)
@@ -377,9 +390,12 @@
                 at = number * levels + level
                 above = edge_ref[at : at + 1]
                 below = edge_ref[count + at : count + at + 1]
-                later = jnp.where(row_number == rows - 1, below, pltpu.roll(values, rows - 1, 0))
-                earlier = jnp.where(row_number == 0, above, pltpu.roll(values, 1, 0))
-                return later - earlier
+                later, earlier = pltpu.roll(values, rows - 1, 0), pltpu.roll(values, 1, 0)
+                low, high = slice(0, SUB), slice(rows - SUB, rows)
+                first = later[low] - jnp.where(row_number == 0, above, earlier[low])
+                last = jnp.where(row_number == SUB - 1, below, later[high]) - earlier[high]
+                inside = slice(SUB, rows - SUB)
+                return jnp.concatenate([first, later[inside] - earlier[inside], last], axis=0)
 
             u, v, q = field(0), field(1), field(2)
             div = scale * (east_west(u) + north_south(v * inverse, 1))
@@ -467,7 +483,6 @@
 
     every = lax.all_to_all(every, "lon", 0, 0)
     inner, outer = swapped(inner, "lon", 0, True), swapped(outer, "lon", 1, True)
-    far_mine = lax.dynamic_index_in_dim(jnp.asarray(far_table), lon[0], 0, False)
 
     near, turn = pl.pallas_call(
         near_kernel_call,
@@ -477,7 +492,7 @@
         ),
         in_specs=[whole_spec()] * 3,
         out_specs=(whole_spec(),) * 2,
-        compiler_params=limit(24),
+        compiler_params=limit(56),
         cost_estimate=cost(6),
         name="near",
     )(local_table, table, values)
@@ -486,12 +501,25 @@
     pack, first, second = pl.pallas_call(
         functools.partial(combine_kernel, per_field, rows),
         out_shape=(jax.ShapeDtypeStruct((tiles, LANES, 2 * wide - LANES), BF), edge, edge),
-        in_specs=[smem] * 2 + [whole_spec()] * 7,
-        out_specs=(whole_spec(),) * 3,
-        compiler_params=limit(24),
+        grid_spec=pltpu.PrefetchScalarGridSpec(
+            num_scalar_prefetch=2,
+            grid=(1,),
+            in_specs=[whole_spec()] * 2
+            + [pl.BlockSpec((1,) + far_table.shape[1:], lambda s, d, e: (d[0], 0, 0))]
+            + [whole_spec()] * 3
+            + [anywhere],
+            out_specs=(anywhere, whole_spec(), whole_spec()),
+            scratch_shapes=[
+                pltpu.VMEM((tiles, LANES, wide), F32),
+                pltpu.VMEM((tiles, LANES, 2 * wide - LANES), BF),
+                pltpu.SemaphoreType.DMA((tiles // GROUP,)),
+                pltpu.SemaphoreType.DMA((tiles // GROUP,)),
+            ],
+        ),
+        compiler_params=limit(56),
         cost_estimate=cost(4),
         name="combine",
-    )(lon, lat, scale, turn, far_mine, near, inner, outer, every)
+    )(lon, lat, scale, turn, far_table, inner, outer, every, near)
 
     first, second = swapped(first, "lat", 0, False), swapped(second, "lat", 1, False)
 

time: 54.4 us -> 56 us (1.029)
  local copies, waits for them, and re-layouts: 8.59 us -> 2.34 us
  Pallas kernels: 32.1 us -> 37.8 us
  waiting for transfers between devices: 0.01 us -> 2.59 us
    unnamed x20 -> x16, local copies, waits for them, and re-layouts: 7.37 us -> 2.34 us
    pallas_call x1, Pallas kernels: 2.94 us -> 6.13 us  [on_device(): pl.pallas_call(functools.partial(combine_kernel, per_field, rows), out_sh...]
    pallas_call x1, Pallas kernels: 2.3 us -> 5.4 us  [on_device(): pl.pallas_call(near_kernel_call, out_shape=(jax.ShapeDtypeStruct((tiles,...]
    ppermute x4, waiting for transfers between devices: 0.01 us -> 2.58 us  [swapped(): return lax.ppermute(array, axis, pairs + [(b, a) for a, b in pairs])]
    squeeze x1 -> x0, local copies, waits for them, and re-layouts: 1.22 us -> none  [on_device(): lax.dynamic_index_in_dim(jnp.asarray(far_table), lon[0], 0, False)]
    pallas_call x1, Pallas kernels: 9.84 us -> 9.23 us  [on_device(): pl.pallas_call(finish_kernel, out_shape=(jax.ShapeDtypeStruct((levels, ro...]
  transfers between devices with their start and end apart: 5 -> 5, of which waited for: 0 -> 1; matrix products, arithmetic and copies ran while one was open for 2% -> 0% of each run, Pallas kernels for 9% -> 14%
where the time goes in v9:
time: 56 us; the launch traced here: 55.7 us
  Pallas kernels  37.8 us (67%)
  starting transfers between devices  12.1 us (22%)
  waiting for transfers between devices  2.59 us (5%)
  local copies, waits for them, and re-layouts  2.34 us (4%)
  between operations  0.89 us (2%)
    pallas_call x1, Pallas kernels, on_device(): pl.pallas_call(functools.partial(analyse_kernel, segments, groups), out_s...  14.4 us
    pallas_call x1, Pallas kernels, on_device(): pl.pallas_call(finish_kernel, out_shape=(jax.ShapeDtypeStruct((levels, ro...  9.23 us
    ppermute x4, starting transfers between devices, swapped(): return lax.ppermute(array, axis, pairs + [(b, a) for a, b in pairs])  8.33 us
    pallas_call x1, Pallas kernels, on_device(): pl.pallas_call(functools.partial(combine_kernel, per_field, rows), out_sh...  6.13 us
    pallas_call x1, Pallas kernels, on_device(): pl.pallas_call(near_kernel_call, out_shape=(jax.ShapeDtypeStruct((tiles,...  5.4 us
    all_to_all x1, starting transfers between devices, on_device(): every = lax.all_to_all(every, 'lon', 0, 0)  3.75 us
    pallas_call x1, Pallas kernels, on_device(): pl.pallas_call(functools.partial(early_kernel, early), out_shape=jax.Shap...  2.59 us
    ppermute x4, waiting for transfers between devices, swapped(): return lax.ppermute(array, axis, pairs + [(b, a) for a, b in pairs])  2.58 us
  transfers between devices with their start and end apart: 5, of which 1 were waited for; matrix products, arithmetic and copies ran while one was open for 0% of the time, Pallas kernels for 14%

profile of v9, /device:TPU:8, one launch (start us, length us, event | category | flops | bytes accessed | tf_op | source)
XLA Modules:
  0.0 55.7 jit_solution(17190554270540208084)
XLA Ops:
  0.6 14.4 %analyse.1 = (f32[12,288,128]{2,1,0:T(8,128)}, f32[12,24,128]{2,1,0:T(8,128)}, f32[12,24,128]{2,1,0:T(8,128)}, f32[8,12,8,128]{3,2,1,0:T(8,128)}, f32[4,288,128]{2,1,0:T(8,128)}) custom-call(s32[1]{0:T(128)} %bitcast.2.device_ref.lon_ref, s32[1,64]{1,0:T(1,128)} %bitcast.6, f32[2,288,1]{2,1,0:T(8,128)} %constant.20.clone.places_ref, ...), custom_call_target="tpu_custom_call" | custom-call | bytes 43200000 | tf_op jit(solution)/shard_map/analyse/pallas_call | solution.py:457
  15.0 3.7 %all-to-all-start = ((f32[8,12,8,128]{3,2,1,0:T(8,128)}), f32[8,12,8,128]{3,2,1,0:T(8,128)S(1)}, u32[]{:S(2)}, u32[]{:S(2)}) async-start(f32[8,12,8,128]{3,2,1,0:T(8,128)} %get-tuple-element.18), calls=%async_computation | async-start | bytes 786432 | tf_op jit(solution)/shard_map/all_to_all | solution.py:484
  18.8 0.5 collective-permute-start
  19.3 2.5 %collective-permute-start.1 = (f32[12,24,128]{2,1,0:T(8,128)}, f32[12,24,128]{2,1,0:T(8,128)S(1)}, u32[]{:S(2)}, u32[]{:S(2)}) collective-permute-start(f32[12,24,128]{2,1,0:T(8,128)} %get-tuple-element.17), channel_id=1, source_target_pairs={{1,2},{3,4},{5,6},{7,0},{2,1},{4,3},{6,5},{0,7},{9,10},{11,12},{13... | collective-permute-start | bytes 442376 | tf_op jit(solution)/shard_map/ppermute | solution.py:482
  21.8 5.4 %near.1 = (f32[12,128,384]{2,1,0:T(8,128)}, f32[2,128,384]{2,1,0:T(8,128)}) custom-call(bf16[288,864]{1,0:T(8,128)(2,1)} %constant.23.clone.local_ref, f32[4,288,128]{2,1,0:T(8,128)} %get-tuple-element.13.table_ref, f32[12,288,128]{2,1,0:T(8,128)} %get-tuple-element.14.node_ref), custom_call_target="tpu_custom_call" | custom-call | bytes 21600000 | tf_op jit(solution)/shard_map/near/pallas_call | solution.py:487
  27.2 0.0 collective-permute-done.inner_ref
  27.2 2.6 %collective-permute-done.1.outer_ref = f32[12,24,128]{2,1,0:T(8,128)S(1)} collective-permute-done((f32[12,24,128]{2,1,0:T(8,128)}, f32[12,24,128]{2,1,0:T(8,128)S(1)}, u32[]{:S(2)}, u32[]{:S(2)}) %collective-permute-start.1) | collective-permute-done | bytes 147488 | tf_op jit(solution)/shard_map/ppermute | solution.py:482
  29.8 0.0 all-to-all-done.every_ref
  29.8 0.0 copy-done.6
  29.8 0.6 %copy-done.7 = f32[12,24,128]{2,1,0:T(8,128)} copy-done((f32[12,24,128]{2,1,0:T(8,128)}, f32[12,24,128]{2,1,0:T(8,128)S(1)}, u32[]{:S(2)}) %copy-start.7) | copy-done | bytes 147480
  30.5 0.1 copy-done.5
  30.6 6.1 %combine.1 = (bf16[12,128,640]{2,1,0:T(8,128)(2,1)}, f32[24,384]{1,0:T(8,128)}, f32[24,384]{1,0:T(8,128)}) custom-call(s32[1]{0:T(128)} %bitcast.2.device_ref.lon_ref, s32[1]{0:T(128)} %bitcast.lat_ref, f32[1,64]{1,0:T(1,128)} %bitcast.4, f32[2,128,384]{2,1,0:T(8,128)} %get-tuple-element.15.turn_ref, bf16[8,336,768]{2,1,0:T(8,128)(2,1)} %constant.24.clone.far_ref, ...), custom_call_target="tpu_custom_call" | custom-call | bytes 14400000 | tf_op jit(solution)/shard_map/combine/pallas_call | solution.py:501
  36.7 0.5 collective-permute-start.2
  37.3 4.8 %collective-permute-start.3 = (f32[24,384]{1,0:T(8,128)}, f32[24,384]{1,0:T(8,128)S(1)}, u32[]{:S(2)}, u32[]{:S(2)}) collective-permute-start(f32[24,384]{1,0:T(8,128)} %get-tuple-element.21), channel_id=1, source_target_pairs={{8,16},{16,8},{9,17},{17,9},{10,18},{18,10},{11,19},{19,11},{12,20... | collective-permute-start | bytes 110600 | tf_op jit(solution)/shard_map/ppermute | solution.py:482
  42.0 0.0 copy-done.1
  42.1 0.0 copy-start.2
  42.1 1.5 %copy-done.2 = bf16[12,128,640]{2,1,0:T(8,128)(2,1)S(1)} copy-done((bf16[12,128,640]{2,1,0:T(8,128)(2,1)S(1)}, bf16[12,128,640]{2,1,0:T(8,128)(2,1)}, u32[]{:S(2)}) %copy-start.2) | copy-done | bytes 1966104
  43.6 2.6 %early.1.early_ref = f32[2,384,1536]{2,1,0:T(8,128)S(1)} custom-call(bf16[896,1536]{1,0:T(8,128)(2,1)S(1)} %copy-done.1, bf16[12,128,640]{2,1,0:T(8,128)(2,1)S(1)} %copy-done.2), custom_call_target="tpu_custom_call" | custom-call | bytes 14400000 | tf_op jit(solution)/shard_map/early/pallas_call | solution.py:527
  46.2 0.0 collective-permute-done.2.first_ref
  46.2 0.0 collective-permute-done.3.second_ref
  46.2 0.0 copy-done
  46.2 0.0 copy-done.3
  46.2 0.0 copy-done.4
  46.3 9.2 %finish.1 = (f32[8,64,1500]{2,1,0:T(8,128)}, f32[8,64,1500]{2,1,0:T(8,128)}, f32[8,64,1500]{2,1,0:T(8,128)}) custom-call(s32[1]{0:T(128)} %bitcast.lat_ref, f32[1,64]{1,0:T(1,128)S(1)} %bitcast.5, bf16[896,1536]{1,0:T(8,128)(2,1)S(1)} %copy-done.1, f32[24,384]{1,0:T(8,128)S(1)} %collective-permute-done.2.first_ref, ...), custom_call_target="tpu_custom_call" | custom-call | bytes 36000000 | tf_op jit(solution)/shard_map/finish/pallas_call | solution.py:537
  (7 shorter events, 0.0 us)
Async XLA Ops:
  15.0 14.8 %all-to-all-start = ((f32[8,12,8,128]{3,2,1,0:T(8,128)}), f32[8,12,8,128]{3,2,1,0:T(8,128)S(1)}, u32[]{:S(2)}, u32[]{:S(2)}) async-start(f32[8,12,8,128]{3,2,1,0:T(8,128)} %get-tuple-element.18), calls=%async_computation | async-start | bytes 786432 | tf_op jit(solution)/shard_map/all_to_all | solution.py:484
  18.8 8.4 %collective-permute-start = (f32[12,24,128]{2,1,0:T(8,128)}, f32[12,24,128]{2,1,0:T(8,128)S(1)}, u32[]{:S(2)}, u32[]{:S(2)}) collective-permute-start(f32[12,24,128]{2,1,0:T(8,128)} %get-tuple-element.16), channel_id=1, source_target_pairs={{0,1},{2,3},{4,5},{6,7},{1,0},{3,2},{5,4},{7,6},{8,9},{10,11},{12,... | collective-permute-start | bytes 442376 | tf_op jit(solution)/shard_map/ppermute | solution.py:482
  19.3 10.5 %collective-permute-start.1 = (f32[12,24,128]{2,1,0:T(8,128)}, f32[12,24,128]{2,1,0:T(8,128)S(1)}, u32[]{:S(2)}, u32[]{:S(2)}) collective-permute-start(f32[12,24,128]{2,1,0:T(8,128)} %get-tuple-element.17), channel_id=1, source_target_pairs={{1,2},{3,4},{5,6},{7,0},{2,1},{4,3},{6,5},{0,7},{9,10},{11,12},{13... | collective-permute-start | bytes 442376 | tf_op jit(solution)/shard_map/ppermute | solution.py:482
  27.2 2.6 %copy-start.6 = (f32[12,24,128]{2,1,0:T(8,128)}, f32[12,24,128]{2,1,0:T(8,128)S(1)}, u32[]{:S(2)}) copy-start(f32[12,24,128]{2,1,0:T(8,128)S(1)} %collective-permute-done.inner_ref) | copy-start | bytes 442372
  29.8 0.7 %copy-start.7 = (f32[12,24,128]{2,1,0:T(8,128)}, f32[12,24,128]{2,1,0:T(8,128)S(1)}, u32[]{:S(2)}) copy-start(f32[12,24,128]{2,1,0:T(8,128)S(1)} %collective-permute-done.1.outer_ref) | copy-start | bytes 442372
  29.8 0.8 %copy-start.5 = (f32[8,12,8,128]{3,2,1,0:T(8,128)}, f32[8,12,8,128]{3,2,1,0:T(8,128)S(1)}, u32[]{:S(2)}) copy-start(f32[8,12,8,128]{3,2,1,0:T(8,128)S(1)} %all-to-all-done.every_ref) | copy-start | bytes 1179652
  30.6 11.4 %copy-start.1 = (bf16[896,1536]{1,0:T(8,128)(2,1)S(1)}, bf16[896,1536]{1,0:T(8,128)(2,1)}, u32[]{:S(2)}) copy-start(bf16[896,1536]{1,0:T(8,128)(2,1)} %constant.25.clone.spread_ref) | copy-start | bytes 8257540
  36.7 9.5 %collective-permute-start.2 = (f32[24,384]{1,0:T(8,128)}, f32[24,384]{1,0:T(8,128)S(1)}, u32[]{:S(2)}, u32[]{:S(2)}) collective-permute-start(f32[24,384]{1,0:T(8,128)} %get-tuple-element.20), channel_id=1, source_target_pairs={{0,8},{16,24},{8,0},{24,16},{1,9},{17,25},{9,1},{25,17},{2,10},{18... | collective-permute-start | bytes 110600 | tf_op jit(solution)/shard_map/ppermute | solution.py:482
  37.3 9.0 %collective-permute-start.3 = (f32[24,384]{1,0:T(8,128)}, f32[24,384]{1,0:T(8,128)S(1)}, u32[]{:S(2)}, u32[]{:S(2)}) collective-permute-start(f32[24,384]{1,0:T(8,128)} %get-tuple-element.21), channel_id=1, source_target_pairs={{8,16},{16,8},{9,17},{17,9},{10,18},{18,10},{11,19},{19,11},{12,20... | collective-permute-start | bytes 110600 | tf_op jit(solution)/shard_map/ppermute | solution.py:482
  42.1 1.5 %copy-start.2 = (bf16[12,128,640]{2,1,0:T(8,128)(2,1)S(1)}, bf16[12,128,640]{2,1,0:T(8,128)(2,1)}, u32[]{:S(2)}) copy-start(bf16[12,128,640]{2,1,0:T(8,128)(2,1)} %get-tuple-element.22.pack_ref) | copy-start | bytes 5898244
  43.6 2.6 %copy-start = (f32[8,64,1500]{2,1,0:T(8,128)S(1)}, f32[8,64,1500]{2,1,0:T(8,128)}, u32[]{:S(2)}) copy-start(f32[8,64,1500]{2,1,0:T(8,128)} %tracer_ref.1) | copy-start | bytes 9216004
  43.6 2.6 %copy-start.3 = (bf16[12,128,640]{2,1,0:T(8,128)(2,1)S(1)}, bf16[12,128,640]{2,1,0:T(8,128)(2,1)}, u32[]{:S(2)}) copy-start(bf16[12,128,640]{2,1,0:T(8,128)(2,1)} %get-tuple-element.22.pack_ref) | copy-start | bytes 5898244
  43.6 2.6 %copy-start.4 = (f32[64]{0:T(128)S(1)}, f32[64]{0:T(128)}, u32[]{:S(2)}) copy-start(f32[64]{0:T(128)} %param.15) | copy-start | bytes 772

commit v10 on v7

--- a/solution.py
+++ b/solution.py
@@ -16,6 +16,7 @@
 FAR = 4
 EXTRA = 32
 LANES = 128
+SUB = 8
 GROUP = 4
 courant = 0.5
 BF = jnp.bfloat16
@@ -187,7 +188,7 @@
 
 
 def analyse_kernel(
-    segments, groups, device_ref, cut_ref, places_ref, gather_ref, moment_ref,
+    segments, groups, cut_ref, places_ref, gather_ref, moment_ref,
     u_ref, v_ref, q_ref, node_ref, inner_ref, outer_ref, every_ref, table_ref,
     lines_ref, high_ref, low_ref, sems,
 ):
@@ -195,7 +196,7 @@
     steps, levels, rows, _ = lines_ref.shape
     lines = levels * rows
     nodes = gather_ref.shape[0] // 2
-    me = device_ref[0]
+    me = lax.axis_index("lon")
     even = lax.rem(me, 2) == 0
 
     copies = []
@@ -260,9 +261,10 @@
     return jnp.transpose(jnp.concatenate([values, none], axis=0))
 
 
-def near_kernel_call(local_ref, table_ref, node_ref, near_ref, turn_ref):
-    turn_ref[0] = turned_over(table_ref[2])
-    turn_ref[1] = turned_over(table_ref[3])
+def near_kernel_call(local_ref, table_ref, node_ref, near_ref):
+    tiles = node_ref.shape[0]
+    near_ref[tiles] = turned_over(table_ref[2])
+    near_ref[tiles + 1] = turned_over(table_ref[3])
     for start in range(0, node_ref.shape[0], GROUP):
         columns = []
         for tile in range(start, start + GROUP):
@@ -275,12 +277,13 @@
 
 
 def combine_kernel(
-    per_field, rows, lon_ref, lat_ref, scale_ref, turn_ref, far_ref, near_ref, inner_ref, outer_ref,
+    per_field, rows, scale_ref, far_ref, near_ref, inner_ref, outer_ref,
     every_ref, pack_ref, first_ref, second_ref,
 ):
-    tiles, _, wide = near_ref.shape
-    segments = every_ref.shape[0]
-    even, even_lat = lax.rem(lon_ref[0], 2) == 0, lax.rem(lat_ref[0], 2) == 0
+    segments, tiles = every_ref.shape[:2]
+    wide = near_ref.shape[2]
+    even = lax.rem(lax.axis_index("lon"), 2) == 0
+    even_lat = lax.rem(lax.axis_index("lat"), 2) == 0
     inverse = 1.0 / scale_ref[...]
     pair = LANES // rows
     for start in range(0, tiles, GROUP):
@@ -293,7 +296,8 @@
         got = product(stacked(jnp.concatenate(columns, axis=1)), far_ref[...], ((0,), (0,)))
         for tile in range(start, start + GROUP):
             mine = got[(tile - start) * LANES : (tile - start + 1) * LANES]
-            values = near_ref[tile] + turn_ref[1] * mine[:, :wide] - turn_ref[0] * mine[:, wide:]
+            values = near_ref[tile] + near_ref[tiles + 1] * mine[:, :wide]
+            values = values - near_ref[tiles] * mine[:, wide:]
             pack_ref[tile] = packed(values)
             wind = tile < 2 * per_field
             for part in range(pair):
@@ -314,7 +318,7 @@
 
 
 def finish_kernel(
-    lat_ref, scale_ref, spread_ref, first_ref, second_ref, pack_ref, early_ref, tracer_ref, *refs
+    scale_ref, spread_ref, first_ref, second_ref, pack_ref, early_ref, tracer_ref, *refs
 ):
     outs = refs[:3]
     filtered_ref, edge_ref, column_ref, held_ref, load_sems, sems = refs[3:]
@@ -341,7 +345,7 @@
         )
 
     load(0).start()
-    even_lat = lax.rem(lat_ref[0], 2) == 0
+    even_lat = lax.rem(lax.axis_index("lat"), 2) == 0
     first, second = first_ref[...], second_ref[...]
     above, below = jnp.where(even_lat, second, first), jnp.where(even_lat, first, second)
     edges = jnp.concatenate([above, below], axis=0)
@@ -352,7 +356,7 @@
     column = jnp.sum(column, axis=1, keepdims=True)
     column_ref[0] = jnp.broadcast_to(column, (rows, LANES))
     column_ref[1] = 1.0 / column_ref[0]
-    row_number = lax.broadcasted_iota(jnp.int32, (rows, 1), 0)
+    row_number = lax.broadcasted_iota(jnp.int32, (SUB, 1), 0)
 
     def fill(step):
         pack = jnp.concatenate([pack_ref[f * steps + step] for f in range(3)], axis=0)
@@ -377,9 +381,12 @@
                 at = number * levels + level
                 above = edge_ref[at : at + 1]
                 below = edge_ref[count + at : count + at + 1]
-                later = jnp.where(row_number == rows - 1, below, pltpu.roll(values, rows - 1, 0))
-                earlier = jnp.where(row_number == 0, above, pltpu.roll(values, 1, 0))
-                return later - earlier
+                later, earlier = pltpu.roll(values, rows - 1, 0), pltpu.roll(values, 1, 0)
+                low, high = slice(0, SUB), slice(rows - SUB, rows)
+                first = later[low] - jnp.where(row_number == 0, above, earlier[low])
+                last = jnp.where(row_number == SUB - 1, below, later[high]) - earlier[high]
+                inside = slice(SUB, rows - SUB)
+                return jnp.concatenate([first, later[inside] - earlier[inside], last], axis=0)
 
             u, v, q = field(0), field(1), field(2)
             div = scale * (east_west(u) + north_south(v * inverse, 1))
@@ -423,12 +430,10 @@
     per_field = levels // pair
     tiles = 3 * per_field
     count = 3 * levels
-    lon, lat = lax.axis_index("lon").astype(jnp.int32), lax.axis_index("lat").astype(jnp.int32)
-    lon, lat = lon[None], lat[None]
+    lon = lax.axis_index("lon").astype(jnp.int32)
     cut = cutoff.reshape(1, rows)
     scale = row_scale.reshape(1, rows)
 
-    smem = pl.BlockSpec(memory_space=pltpu.SMEM)
     anywhere = pl.BlockSpec(memory_space=pl.ANY)
     def limit(mib):
         return pltpu.CompilerParams(vmem_limit_bytes=mib * 1024 * 1024)
@@ -447,7 +452,7 @@
             jax.ShapeDtypeStruct((segments, tiles, 2 * FAR, LANES), F32),
             jax.ShapeDtypeStruct((4, nodes, LANES), F32),
         ),
-        in_specs=[smem] + [whole_spec()] * 4 + [anywhere] * 3,
+        in_specs=[whole_spec()] * 4 + [anywhere] * 3,
         out_specs=(whole_spec(),) * 5,
         scratch_shapes=[
             pltpu.VMEM((steps, group, rows, width), F32),
@@ -458,7 +463,7 @@
         compiler_params=limit(56),
         cost_estimate=cost(12),
         name="analyse",
-    )(lon, cut, places, gather_table, moment_table, wind_u, wind_v, tracer)
+    )(cut, places, gather_table, moment_table, wind_u, wind_v, tracer)
 
     def swapped(array, axis, start, closed):
         size = segments if axis == "lon" else lats
@@ -467,16 +472,13 @@
 
     every = lax.all_to_all(every, "lon", 0, 0)
     inner, outer = swapped(inner, "lon", 0, True), swapped(outer, "lon", 1, True)
-    far_mine = lax.dynamic_index_in_dim(jnp.asarray(far_table), lon[0], 0, False)
-
-    near, turn = pl.pallas_call(
+    far_mine = lax.dynamic_index_in_dim(jnp.asarray(far_table), lon, 0, False)
+
+    near = pl.pallas_call(
         near_kernel_call,
-        out_shape=(
-            jax.ShapeDtypeStruct((tiles, LANES, wide), F32),
-            jax.ShapeDtypeStruct((2, LANES, wide), F32),
-        ),
+        out_shape=jax.ShapeDtypeStruct((tiles + 2, LANES, wide), F32),
         in_specs=[whole_spec()] * 3,
-        out_specs=(whole_spec(),) * 2,
+        out_specs=whole_spec(),
         compiler_params=limit(24),
         cost_estimate=cost(6),
         name="near",
@@ -486,12 +488,12 @@
     pack, first, second = pl.pallas_call(
         functools.partial(combine_kernel, per_field, rows),
         out_shape=(jax.ShapeDtypeStruct((tiles, LANES, 2 * wide - LANES), BF), edge, edge),
-        in_specs=[smem] * 2 + [whole_spec()] * 7,
+        in_specs=[whole_spec()] * 6,
         out_specs=(whole_spec(),) * 3,
         compiler_params=limit(24),
         cost_estimate=cost(4),
         name="combine",
-    )(lon, lat, scale, turn, far_mine, near, inner, outer, every)
+    )(scale, far_mine, near, inner, outer, every)
 
     first, second = swapped(first, "lat", 0, False), swapped(second, "lat", 1, False)
 
@@ -509,7 +511,7 @@
     return pl.pallas_call(
         finish_kernel,
         out_shape=(jax.ShapeDtypeStruct((levels, rows, width), F32),) * 3,
-        in_specs=[smem] + [whole_spec()] * 6 + [anywhere],
+        in_specs=[whole_spec()] * 6 + [anywhere],
         out_specs=(anywhere,) * 3,
         scratch_shapes=[
             pltpu.VMEM((per_field - early, 3 * LANES, lanes), F32),
@@ -522,7 +524,7 @@
         compiler_params=limit(32),
         cost_estimate=cost(10),
         name="finish",
-    )(lat, scale, spread_table, first, second, pack, filtered, tracer)
+    )(scale, spread_table, first, second, pack, filtered, tracer)
 
 
 def solution(mesh):

time: 54.4 us -> 53.1 us (0.976)
  local copies, waits for them, and re-layouts: 8.59 us -> 7.09 us
  waiting for transfers between devices: 0.01 us -> 0.6 us
    unnamed x20 -> x16, local copies, waits for them, and re-layouts: 7.37 us -> 5.87 us
    ppermute x4, waiting for transfers between devices: 0.01 us -> 0.59 us  [swapped(): return lax.ppermute(array, axis, pairs + [(b, a) for a, b in pairs])]
  transfers between devices with their start and end apart: 5 -> 5, of which waited for: 0 -> 1; matrix products, arithmetic and copies ran while one was open for 2% -> 2% of each run, Pallas kernels for 9% -> 9%
where the time goes in v10:
time: 53.1 us; the launch traced here: 52.8 us
  Pallas kernels  31.8 us (60%)
  starting transfers between devices  12.3 us (23%)
  local copies, waits for them, and re-layouts  7.09 us (13%)
  between operations  0.9 us (2%)
  waiting for transfers between devices  0.6 us (1%)
    pallas_call x1, Pallas kernels, on_device(): pl.pallas_call(functools.partial(analyse_kernel, segments, groups), out_s...  14.4 us
    pallas_call x1, Pallas kernels, on_device(): pl.pallas_call(finish_kernel, out_shape=(jax.ShapeDtypeStruct((levels, ro...  9.84 us
    ppermute x4, starting transfers between devices, swapped(): return lax.ppermute(array, axis, pairs + [(b, a) for a, b in pairs])  8.24 us
    unnamed x16, local copies, waits for them, and re-layouts  5.87 us
    all_to_all x1, starting transfers between devices, on_device(): every = lax.all_to_all(every, 'lon', 0, 0)  4.11 us
    pallas_call x1, Pallas kernels, on_device(): pl.pallas_call(functools.partial(combine_kernel, per_field, rows), out_sh...  2.76 us
    pallas_call x1, Pallas kernels, on_device(): pl.pallas_call(functools.partial(early_kernel, early), out_shape=jax.Shap...  2.61 us
    pallas_call x1, Pallas kernels, on_device(): pl.pallas_call(near_kernel_call, out_shape=jax.ShapeDtypeStruct((tiles +...  2.18 us
  transfers between devices with their start and end apart: 5, of which 1 were waited for; matrix products, arithmetic and copies ran while one was open for 2% of the time, Pallas kernels for 9%

profile of v10, /device:TPU:8, one launch (start us, length us, event | category | flops | bytes accessed | tf_op | source)
XLA Modules:
  0.0 52.8 jit_solution(9221085745087711347)
XLA Ops:
  0.6 0.0 copy-start.6
  0.6 14.4 %analyse.1 = (f32[12,288,128]{2,1,0:T(8,128)}, f32[12,24,128]{2,1,0:T(8,128)}, f32[12,24,128]{2,1,0:T(8,128)}, f32[8,12,8,128]{3,2,1,0:T(8,128)}, f32[4,288,128]{2,1,0:T(8,128)}) custom-call(s32[1,64]{1,0:T(1,128)} %bitcast.6, f32[2,288,1]{2,1,0:T(8,128)} %constant.22.clone.places_ref, bf16[576,1500]{1,0:T(8,128)(2,1)} %constant.23.clone.gather_ref, ...), custom_call_target="tpu_custom_call" | custom-call | bytes 43200000 | tf_op jit(solution)/shard_map/analyse/pallas_call | solution.py:446
  15.1 4.1 %all-to-all-start = ((f32[8,12,8,128]{3,2,1,0:T(8,128)}), f32[8,12,8,128]{3,2,1,0:T(8,128)}, u32[]{:S(2)}, u32[]{:S(2)}) async-start(f32[8,12,8,128]{3,2,1,0:T(8,128)} %get-tuple-element.15), calls=%async_computation | async-start | bytes 786432 | tf_op jit(solution)/shard_map/all_to_all | solution.py:473
  19.2 0.4 collective-permute-start
  19.6 2.6 %collective-permute-start.1 = (f32[12,24,128]{2,1,0:T(8,128)}, f32[12,24,128]{2,1,0:T(8,128)}, u32[]{:S(2)}, u32[]{:S(2)}) collective-permute-start(f32[12,24,128]{2,1,0:T(8,128)} %get-tuple-element.14), channel_id=1, source_target_pairs={{1,2},{3,4},{5,6},{7,0},{2,1},{4,3},{6,5},{0,7},{9,10},{11,12},{13... | collective-permute-start | bytes 442376 | tf_op jit(solution)/shard_map/ppermute | solution.py:471
  22.2 1.5 %copy-done.4 = f32[12,288,128]{2,1,0:T(8,128)S(1)} copy-done((f32[12,288,128]{2,1,0:T(8,128)S(1)}, f32[12,288,128]{2,1,0:T(8,128)}, u32[]{:S(2)}) %copy-start.4) | copy-done | bytes 1769496
  23.6 1.1 %copy-done.5 = f32[4,288,128]{2,1,0:T(8,128)S(1)} copy-done((f32[4,288,128]{2,1,0:T(8,128)S(1)}, f32[4,288,128]{2,1,0:T(8,128)}, u32[]{:S(2)}) %copy-start.5) | copy-done | bytes 589848
  24.7 2.2 %near.1.near_ref = f32[14,128,384]{2,1,0:T(8,128)S(1)} custom-call(bf16[288,864]{1,0:T(8,128)(2,1)S(1)} %copy-done.6, f32[4,288,128]{2,1,0:T(8,128)S(1)} %copy-done.5, f32[12,288,128]{2,1,0:T(8,128)S(1)} %copy-done.4), custom_call_target="tpu_custom_call" | custom-call | bytes 21600000 | tf_op jit(solution)/shard_map/near/pallas_call | solution.py:477
  26.9 0.0 copy-start.2
  26.9 1.5 %copy-done.2 = f32[14,128,384]{2,1,0:T(8,128)} copy-done((f32[14,128,384]{2,1,0:T(8,128)}, f32[14,128,384]{2,1,0:T(8,128)S(1)}, u32[]{:S(2)}) %copy-start.2) | copy-done | bytes 2752536
  28.4 1.2 %dynamic-slice_bitcast_fusion.far_ref = bf16[336,768]{1,0:T(8,128)(2,1)S(1)} fusion(bf16[8,336,768]{2,1,0:T(8,128)(2,1)} %constant.25.clone, s32[]{:T(128)S(6)} %select_n.4), kind=kLoop, calls=%fused_computation | loop fusion | bytes 1032196 | tf_op jit(solution)/shard_map/jit(dynamic_index_in_dim)/squeeze | solution.py:475
  29.6 0.0 collective-permute-done.inner_ref
  29.7 0.6 %collective-permute-done.1.outer_ref = f32[12,24,128]{2,1,0:T(8,128)} collective-permute-done((f32[12,24,128]{2,1,0:T(8,128)}, f32[12,24,128]{2,1,0:T(8,128)}, u32[]{:S(2)}, u32[]{:S(2)}) %collective-permute-start.1) | collective-permute-done | bytes 147488 | tf_op jit(solution)/shard_map/ppermute | solution.py:471
  30.2 0.0 all-to-all-done.every_ref
  30.2 1.8 %copy-done.3 = f32[14,128,384]{2,1,0:T(8,128)S(1)} copy-done((f32[14,128,384]{2,1,0:T(8,128)S(1)}, f32[14,128,384]{2,1,0:T(8,128)}, u32[]{:S(2)}) %copy-start.3) | copy-done | bytes 2752536
  32.0 2.8 %combine.1 = (bf16[12,128,640]{2,1,0:T(8,128)(2,1)S(1)}, f32[24,384]{1,0:T(8,128)S(1)}, f32[24,384]{1,0:T(8,128)S(1)}) custom-call(f32[1,64]{1,0:T(1,128)S(1)} %bitcast.4, bf16[336,768]{1,0:T(8,128)(2,1)S(1)} %dynamic-slice_bitcast_fusion.far_ref, f32[14,128,384]{2,1,0:T(8,128)S(1)} %copy-done.3, f32[12,24,128]{2,1,0:T(8,128)S(1)} %collective-permute-done.inner_ref, ...), custom_call_target="tpu_custom_call" | custom-call | bytes 14400000 | tf_op jit(solution)/shard_map/combine/pallas_call | solution.py:488
  34.8 0.2 collective-permute-start.2
  35.0 5.1 %collective-permute-start.3 = (f32[24,384]{1,0:T(8,128)S(1)}, f32[24,384]{1,0:T(8,128)S(1)}, u32[]{:S(2)}, u32[]{:S(2)}) collective-permute-start(f32[24,384]{1,0:T(8,128)S(1)} %get-tuple-element.17), channel_id=1, source_target_pairs={{8,16},{16,8},{9,17},{17,9},{10,18},{18,10},{11,19},{19,11},{12,20... | collective-permute-start | bytes 110600 | tf_op jit(solution)/shard_map/ppermute | solution.py:471
  40.1 0.0 copy-start
  40.1 2.6 %early.1.early_ref = f32[2,384,1536]{2,1,0:T(8,128)S(1)} custom-call(bf16[896,1536]{1,0:T(8,128)(2,1)S(1)} %copy-done.1, bf16[12,128,640]{2,1,0:T(8,128)(2,1)S(1)} %get-tuple-element.18.pack_ref), custom_call_target="tpu_custom_call" | custom-call | bytes 14400000 | tf_op jit(solution)/shard_map/early/pallas_call | solution.py:501
  42.7 0.0 collective-permute-done.2.first_ref
  42.7 0.0 collective-permute-done.3.second_ref
  42.7 0.0 copy-done
  42.8 9.8 %finish.1 = (f32[8,64,1500]{2,1,0:T(8,128)}, f32[8,64,1500]{2,1,0:T(8,128)}, f32[8,64,1500]{2,1,0:T(8,128)}) custom-call(f32[1,64]{1,0:T(1,128)S(1)} %bitcast.5, bf16[896,1536]{1,0:T(8,128)(2,1)S(1)} %copy-done.1, f32[24,384]{1,0:T(8,128)S(1)} %collective-permute-done.2.first_ref, f32[24,384]{1,0:T(8,128)S(1)} %collective-permute-done.3.second_ref, ...), custom_call_target="tpu_custom_call" | custom-call | bytes 36000000 | tf_op jit(solution)/shard_map/finish/pallas_call | solution.py:511
  (8 shorter events, 0.0 us)
Async XLA Ops:
  0.6 21.5 %copy-start.6 = (bf16[288,864]{1,0:T(8,128)(2,1)S(1)}, bf16[288,864]{1,0:T(8,128)(2,1)}, u32[]{:S(2)}) copy-start(bf16[288,864]{1,0:T(8,128)(2,1)} %constant.26.clone.local_ref) | copy-start | bytes 1492996
  15.1 15.2 %all-to-all-start = ((f32[8,12,8,128]{3,2,1,0:T(8,128)}), f32[8,12,8,128]{3,2,1,0:T(8,128)}, u32[]{:S(2)}, u32[]{:S(2)}) async-start(f32[8,12,8,128]{3,2,1,0:T(8,128)} %get-tuple-element.15), calls=%async_computation | async-start | bytes 786432 | tf_op jit(solution)/shard_map/all_to_all | solution.py:473
  19.2 10.4 %collective-permute-start = (f32[12,24,128]{2,1,0:T(8,128)}, f32[12,24,128]{2,1,0:T(8,128)S(1)}, u32[]{:S(2)}, u32[]{:S(2)}) collective-permute-start(f32[12,24,128]{2,1,0:T(8,128)} %get-tuple-element.13), channel_id=1, source_target_pairs={{0,1},{2,3},{4,5},{6,7},{1,0},{3,2},{5,4},{7,6},{8,9},{10,11},{12,... | collective-permute-start | bytes 442376 | tf_op jit(solution)/shard_map/ppermute | solution.py:471
  19.6 10.7 %collective-permute-start.1 = (f32[12,24,128]{2,1,0:T(8,128)}, f32[12,24,128]{2,1,0:T(8,128)}, u32[]{:S(2)}, u32[]{:S(2)}) collective-permute-start(f32[12,24,128]{2,1,0:T(8,128)} %get-tuple-element.14), channel_id=1, source_target_pairs={{1,2},{3,4},{5,6},{7,0},{2,1},{4,3},{6,5},{0,7},{9,10},{11,12},{13... | collective-permute-start | bytes 442376 | tf_op jit(solution)/shard_map/ppermute | solution.py:471
  22.2 1.5 %copy-start.4 = (f32[12,288,128]{2,1,0:T(8,128)S(1)}, f32[12,288,128]{2,1,0:T(8,128)}, u32[]{:S(2)}) copy-start(f32[12,288,128]{2,1,0:T(8,128)} %get-tuple-element.12.node_ref) | copy-start | bytes 5308420
  23.6 1.1 %copy-start.5 = (f32[4,288,128]{2,1,0:T(8,128)S(1)}, f32[4,288,128]{2,1,0:T(8,128)}, u32[]{:S(2)}) copy-start(f32[4,288,128]{2,1,0:T(8,128)} %get-tuple-element.11.table_ref) | copy-start | bytes 1769476
  24.7 5.6 %copy-start.7 = (f32[64]{0:T(128)S(1)}, f32[64]{0:T(128)}, u32[]{:S(2)}) copy-start(f32[64]{0:T(128)} %param.15) | copy-start | bytes 772
  26.9 1.5 %copy-start.2 = (f32[14,128,384]{2,1,0:T(8,128)}, f32[14,128,384]{2,1,0:T(8,128)S(1)}, u32[]{:S(2)}) copy-start(f32[14,128,384]{2,1,0:T(8,128)S(1)} %near.1.near_ref) | copy-start | bytes 8257540
  28.4 11.7 %copy-start.1 = (bf16[896,1536]{1,0:T(8,128)(2,1)S(1)}, bf16[896,1536]{1,0:T(8,128)(2,1)}, u32[]{:S(2)}) copy-start(bf16[896,1536]{1,0:T(8,128)(2,1)} %constant.27.clone.spread_ref) | copy-start | bytes 8257540
  30.2 1.8 %copy-start.3 = (f32[14,128,384]{2,1,0:T(8,128)S(1)}, f32[14,128,384]{2,1,0:T(8,128)}, u32[]{:S(2)}) copy-start(f32[14,128,384]{2,1,0:T(8,128)} %copy-done.2) | copy-start | bytes 8257540
  34.8 7.9 %collective-permute-start.2 = (f32[24,384]{1,0:T(8,128)S(1)}, f32[24,384]{1,0:T(8,128)S(1)}, u32[]{:S(2)}, u32[]{:S(2)}) collective-permute-start(f32[24,384]{1,0:T(8,128)S(1)} %get-tuple-element.16), channel_id=1, source_target_pairs={{0,8},{16,24},{8,0},{24,16},{1,9},{17,25},{9,1},{25,17},{2,10},{18... | collective-permute-start | bytes 110600 | tf_op jit(solution)/shard_map/ppermute | solution.py:471
  35.0 7.7 %collective-permute-start.3 = (f32[24,384]{1,0:T(8,128)S(1)}, f32[24,384]{1,0:T(8,128)S(1)}, u32[]{:S(2)}, u32[]{:S(2)}) collective-permute-start(f32[24,384]{1,0:T(8,128)S(1)} %get-tuple-element.17), channel_id=1, source_target_pairs={{8,16},{16,8},{9,17},{17,9},{10,18},{18,10},{11,19},{19,11},{12,20... | collective-permute-start | bytes 110600 | tf_op jit(solution)/shard_map/ppermute | solution.py:471
  40.1 2.6 %copy-start = (f32[8,64,1500]{2,1,0:T(8,128)S(1)}, f32[8,64,1500]{2,1,0:T(8,128)}, u32[]{:S(2)}) copy-start(f32[8,64,1500]{2,1,0:T(8,128)} %tracer_ref.1) | copy-start | bytes 9216004

commit v11 on v10

--- a/solution.py
+++ b/solution.py
@@ -102,7 +102,8 @@
     local_table = np.concatenate([high, low, high], 1)
     blocks = []
     for d in range(segments):
-        pieces = [far[d - (d - s) % segments] @ basis[-s].T for s in (1, segments - 1)]
+        order = (segments - 1, 1) if d % 2 == 0 else (1, segments - 1)
+        pieces = [far[d - (d - s) % segments] @ basis[-s].T for s in order]
         for e in range(segments):
             if e == d:
                 pieces.append(np.zeros((nodes, FAR)))
@@ -261,10 +262,12 @@
     return jnp.transpose(jnp.concatenate([values, none], axis=0))
 
 
-def near_kernel_call(local_ref, table_ref, node_ref, near_ref):
+def near_kernel_call(local_ref, table_ref, node_ref, far_ref, near_ref):
+    del far_ref
     tiles = node_ref.shape[0]
-    near_ref[tiles] = turned_over(table_ref[2])
-    near_ref[tiles + 1] = turned_over(table_ref[3])
+    half = LANES // 2
+    near_ref[tiles, :half] = turned_over(table_ref[2])[:half]
+    near_ref[tiles, half:] = turned_over(table_ref[3])[:half]
     for start in range(0, node_ref.shape[0], GROUP):
         columns = []
         for tile in range(start, start + GROUP):
@@ -282,22 +285,21 @@
 ):
     segments, tiles = every_ref.shape[:2]
     wide = near_ref.shape[2]
-    even = lax.rem(lax.axis_index("lon"), 2) == 0
     even_lat = lax.rem(lax.axis_index("lat"), 2) == 0
     inverse = 1.0 / scale_ref[...]
     pair = LANES // rows
+    cosine = jnp.concatenate([near_ref[tiles, :rows]] * pair, axis=0)
+    sine = jnp.concatenate([near_ref[tiles, LANES // 2 : LANES // 2 + rows]] * pair, axis=0)
     for start in range(0, tiles, GROUP):
         columns = []
         for tile in range(start, start + GROUP):
-            inner, outer = inner_ref[tile], outer_ref[tile]
-            pieces = [jnp.where(even, outer, inner), jnp.where(even, inner, outer)]
+            pieces = [inner_ref[tile], outer_ref[tile]]
             pieces += [every_ref[e, tile] for e in range(segments)]
             columns.append(jnp.concatenate(pieces, axis=0))
         got = product(stacked(jnp.concatenate(columns, axis=1)), far_ref[...], ((0,), (0,)))
         for tile in range(start, start + GROUP):
             mine = got[(tile - start) * LANES : (tile - start + 1) * LANES]
-            values = near_ref[tile] + near_ref[tiles + 1] * mine[:, :wide]
-            values = values - near_ref[tiles] * mine[:, wide:]
+            values = near_ref[tile] + sine * mine[:, :wide] - cosine * mine[:, wide:]
             pack_ref[tile] = packed(values)
             wind = tile < 2 * per_field
             for part in range(pair):
@@ -476,13 +478,13 @@
 
     near = pl.pallas_call(
         near_kernel_call,
-        out_shape=jax.ShapeDtypeStruct((tiles + 2, LANES, wide), F32),
-        in_specs=[whole_spec()] * 3,
+        out_shape=jax.ShapeDtypeStruct((tiles + 1, LANES, wide), F32),
+        in_specs=[whole_spec()] * 4,
         out_specs=whole_spec(),
         compiler_params=limit(24),
         cost_estimate=cost(6),
         name="near",
-    )(local_table, table, values)
+    )(local_table, table, values, far_mine)
 
     edge = jax.ShapeDtypeStruct((count, wide), F32)
     pack, first, second = pl.pallas_call(

time: 53.1 us -> 53.3 us (level)
  no operation moved by 1% of the time
where the time goes in v11:
time: 53.3 us; the launch traced here: 52.9 us
  Pallas kernels  32 us (60%)
  starting transfers between devices  12.3 us (23%)
  local copies, waits for them, and re-layouts  6.85 us (13%)
  between operations  0.91 us (2%)
  waiting for transfers between devices  0.8 us (2%)
    pallas_call x1, Pallas kernels, on_device(): pl.pallas_call(functools.partial(analyse_kernel, segments, groups), out_s...  14.4 us
    pallas_call x1, Pallas kernels, on_device(): pl.pallas_call(finish_kernel, out_shape=(jax.ShapeDtypeStruct((levels, ro...  9.84 us
    ppermute x4, starting transfers between devices, swapped(): return lax.ppermute(array, axis, pairs + [(b, a) for a, b in pairs])  8.24 us
    unnamed x16, local copies, waits for them, and re-layouts  5.78 us
    all_to_all x1, starting transfers between devices, on_device(): every = lax.all_to_all(every, 'lon', 0, 0)  4.11 us
    pallas_call x1, Pallas kernels, on_device(): pl.pallas_call(functools.partial(combine_kernel, per_field, rows), out_sh...  2.88 us
    pallas_call x1, Pallas kernels, on_device(): pl.pallas_call(functools.partial(early_kernel, early), out_shape=jax.Shap...  2.61 us
    pallas_call x1, Pallas kernels, on_device(): pl.pallas_call(near_kernel_call, out_shape=jax.ShapeDtypeStruct((tiles +...  2.18 us
  transfers between devices with their start and end apart: 5, of which 1 were waited for; matrix products, arithmetic and copies ran while one was open for 2% of the time, Pallas kernels for 9%

profile of v11, /device:TPU:8, one launch (start us, length us, event | category | flops | bytes accessed | tf_op | source)
XLA Modules:
  0.0 52.9 jit_solution(12516514872100701222)
XLA Ops:
  0.6 0.0 copy-start.6
  0.6 14.4 %analyse.1 = (f32[12,288,128]{2,1,0:T(8,128)}, f32[12,24,128]{2,1,0:T(8,128)}, f32[12,24,128]{2,1,0:T(8,128)}, f32[8,12,8,128]{3,2,1,0:T(8,128)}, f32[4,288,128]{2,1,0:T(8,128)}) custom-call(s32[1,64]{1,0:T(1,128)} %bitcast.6, f32[2,288,1]{2,1,0:T(8,128)} %constant.22.clone.places_ref, bf16[576,1500]{1,0:T(8,128)(2,1)} %constant.23.clone.gather_ref, ...), custom_call_target="tpu_custom_call" | custom-call | bytes 43200000 | tf_op jit(solution)/shard_map/analyse/pallas_call | solution.py:448
  15.1 4.1 %all-to-all-start = ((f32[8,12,8,128]{3,2,1,0:T(8,128)}), f32[8,12,8,128]{3,2,1,0:T(8,128)}, u32[]{:S(2)}, u32[]{:S(2)}) async-start(f32[8,12,8,128]{3,2,1,0:T(8,128)} %get-tuple-element.15), calls=%async_computation | async-start | bytes 786432 | tf_op jit(solution)/shard_map/all_to_all | solution.py:475
  19.2 0.4 collective-permute-start
  19.6 2.6 %collective-permute-start.1 = (f32[12,24,128]{2,1,0:T(8,128)}, f32[12,24,128]{2,1,0:T(8,128)}, u32[]{:S(2)}, u32[]{:S(2)}) collective-permute-start(f32[12,24,128]{2,1,0:T(8,128)} %get-tuple-element.14), channel_id=1, source_target_pairs={{1,2},{3,4},{5,6},{7,0},{2,1},{4,3},{6,5},{0,7},{9,10},{11,12},{13... | collective-permute-start | bytes 442376 | tf_op jit(solution)/shard_map/ppermute | solution.py:473
  22.1 1.1 %dynamic-slice_bitcast_fusion.far_ref = bf16[336,768]{1,0:T(8,128)(2,1)S(1)} fusion(bf16[8,336,768]{2,1,0:T(8,128)(2,1)} %constant.25.clone, s32[]{:T(128)S(6)} %select_n.4), kind=kLoop, calls=%fused_computation | loop fusion | bytes 1032196 | tf_op jit(solution)/shard_map/jit(dynamic_index_in_dim)/squeeze | solution.py:477
  23.2 0.0 copy-start.7
  23.2 0.0 copy-start.4
  23.3 1.5 %copy-done.4 = f32[12,288,128]{2,1,0:T(8,128)S(1)} copy-done((f32[12,288,128]{2,1,0:T(8,128)S(1)}, f32[12,288,128]{2,1,0:T(8,128)}, u32[]{:S(2)}) %copy-start.4) | copy-done | bytes 1769496
  24.7 1.1 %copy-done.5 = f32[4,288,128]{2,1,0:T(8,128)S(1)} copy-done((f32[4,288,128]{2,1,0:T(8,128)S(1)}, f32[4,288,128]{2,1,0:T(8,128)}, u32[]{:S(2)}) %copy-start.5) | copy-done | bytes 589848
  25.8 2.2 %near.1.near_ref = f32[13,128,384]{2,1,0:T(8,128)S(1)} custom-call(bf16[288,864]{1,0:T(8,128)(2,1)S(1)} %copy-done.6, f32[4,288,128]{2,1,0:T(8,128)S(1)} %copy-done.5, f32[12,288,128]{2,1,0:T(8,128)S(1)} %copy-done.4, bf16[336,768]{1,0:T(8,128)(2,1)S(1)} %dynamic-slice_bitcast_fusion.far_ref), custom_call_target="tpu_custom_call" | custom-call | bytes 21600000 | tf_op jit(solution)/shard_map/near/pallas_call | solution.py:479
  28.0 1.5 %copy-done.2 = f32[13,128,384]{2,1,0:T(8,128)} copy-done((f32[13,128,384]{2,1,0:T(8,128)}, f32[13,128,384]{2,1,0:T(8,128)S(1)}, u32[]{:S(2)}) %copy-start.2) | copy-done | bytes 2555928
  29.4 0.0 collective-permute-done.inner_ref
  29.5 0.8 %collective-permute-done.1.outer_ref = f32[12,24,128]{2,1,0:T(8,128)} collective-permute-done((f32[12,24,128]{2,1,0:T(8,128)}, f32[12,24,128]{2,1,0:T(8,128)}, u32[]{:S(2)}, u32[]{:S(2)}) %collective-permute-start.1) | collective-permute-done | bytes 147488 | tf_op jit(solution)/shard_map/ppermute | solution.py:473
  30.2 0.0 all-to-all-done.every_ref
  30.2 1.8 %copy-done.3 = f32[13,128,384]{2,1,0:T(8,128)S(1)} copy-done((f32[13,128,384]{2,1,0:T(8,128)S(1)}, f32[13,128,384]{2,1,0:T(8,128)}, u32[]{:S(2)}) %copy-start.3) | copy-done | bytes 2555928
  32.0 2.9 %combine.1 = (bf16[12,128,640]{2,1,0:T(8,128)(2,1)S(1)}, f32[24,384]{1,0:T(8,128)S(1)}, f32[24,384]{1,0:T(8,128)S(1)}) custom-call(f32[1,64]{1,0:T(1,128)S(1)} %bitcast.4, bf16[336,768]{1,0:T(8,128)(2,1)S(1)} %dynamic-slice_bitcast_fusion.far_ref, f32[13,128,384]{2,1,0:T(8,128)S(1)} %copy-done.3, f32[12,24,128]{2,1,0:T(8,128)S(1)} %collective-permute-done.inner_ref, ...), custom_call_target="tpu_custom_call" | custom-call | bytes 14400000 | tf_op jit(solution)/shard_map/combine/pallas_call | solution.py:490
  34.9 0.2 collective-permute-start.2
  35.1 5.1 %collective-permute-start.3 = (f32[24,384]{1,0:T(8,128)S(1)}, f32[24,384]{1,0:T(8,128)S(1)}, u32[]{:S(2)}, u32[]{:S(2)}) collective-permute-start(f32[24,384]{1,0:T(8,128)S(1)} %get-tuple-element.17), channel_id=1, source_target_pairs={{8,16},{16,8},{9,17},{17,9},{10,18},{18,10},{11,19},{19,11},{12,20... | collective-permute-start | bytes 110600 | tf_op jit(solution)/shard_map/ppermute | solution.py:473
  40.2 0.0 copy-start
  40.2 2.6 %early.1.early_ref = f32[2,384,1536]{2,1,0:T(8,128)S(1)} custom-call(bf16[896,1536]{1,0:T(8,128)(2,1)S(1)} %copy-done.1, bf16[12,128,640]{2,1,0:T(8,128)(2,1)S(1)} %get-tuple-element.18.pack_ref), custom_call_target="tpu_custom_call" | custom-call | bytes 14400000 | tf_op jit(solution)/shard_map/early/pallas_call | solution.py:503
  42.8 0.0 collective-permute-done.2.first_ref
  42.8 0.0 collective-permute-done.3.second_ref
  42.9 9.8 %finish.1 = (f32[8,64,1500]{2,1,0:T(8,128)}, f32[8,64,1500]{2,1,0:T(8,128)}, f32[8,64,1500]{2,1,0:T(8,128)}) custom-call(f32[1,64]{1,0:T(1,128)S(1)} %bitcast.5, bf16[896,1536]{1,0:T(8,128)(2,1)S(1)} %copy-done.1, f32[24,384]{1,0:T(8,128)S(1)} %collective-permute-done.2.first_ref, f32[24,384]{1,0:T(8,128)S(1)} %collective-permute-done.3.second_ref, ...), custom_call_target="tpu_custom_call" | custom-call | bytes 36000000 | tf_op jit(solution)/shard_map/finish/pallas_call | solution.py:513
  (8 shorter events, 0.0 us)
Async XLA Ops:
  0.6 22.6 %copy-start.6 = (bf16[288,864]{1,0:T(8,128)(2,1)S(1)}, bf16[288,864]{1,0:T(8,128)(2,1)}, u32[]{:S(2)}) copy-start(bf16[288,864]{1,0:T(8,128)(2,1)} %constant.26.clone.local_ref) | copy-start | bytes 1492996
  15.1 15.2 %all-to-all-start = ((f32[8,12,8,128]{3,2,1,0:T(8,128)}), f32[8,12,8,128]{3,2,1,0:T(8,128)}, u32[]{:S(2)}, u32[]{:S(2)}) async-start(f32[8,12,8,128]{3,2,1,0:T(8,128)} %get-tuple-element.15), calls=%async_computation | async-start | bytes 786432 | tf_op jit(solution)/shard_map/all_to_all | solution.py:475
  19.2 10.2 %collective-permute-start = (f32[12,24,128]{2,1,0:T(8,128)}, f32[12,24,128]{2,1,0:T(8,128)S(1)}, u32[]{:S(2)}, u32[]{:S(2)}) collective-permute-start(f32[12,24,128]{2,1,0:T(8,128)} %get-tuple-element.13), channel_id=1, source_target_pairs={{0,1},{2,3},{4,5},{6,7},{1,0},{3,2},{5,4},{7,6},{8,9},{10,11},{12,... | collective-permute-start | bytes 442376 | tf_op jit(solution)/shard_map/ppermute | solution.py:473
  19.6 10.7 %collective-permute-start.1 = (f32[12,24,128]{2,1,0:T(8,128)}, f32[12,24,128]{2,1,0:T(8,128)}, u32[]{:S(2)}, u32[]{:S(2)}) collective-permute-start(f32[12,24,128]{2,1,0:T(8,128)} %get-tuple-element.14), channel_id=1, source_target_pairs={{1,2},{3,4},{5,6},{7,0},{2,1},{4,3},{6,5},{0,7},{9,10},{11,12},{13... | collective-permute-start | bytes 442376 | tf_op jit(solution)/shard_map/ppermute | solution.py:473
  23.2 7.0 %copy-start.7 = (f32[64]{0:T(128)S(1)}, f32[64]{0:T(128)}, u32[]{:S(2)}) copy-start(f32[64]{0:T(128)} %param.15) | copy-start | bytes 772
  23.2 1.5 %copy-start.4 = (f32[12,288,128]{2,1,0:T(8,128)S(1)}, f32[12,288,128]{2,1,0:T(8,128)}, u32[]{:S(2)}) copy-start(f32[12,288,128]{2,1,0:T(8,128)} %get-tuple-element.12.node_ref) | copy-start | bytes 5308420
  24.7 1.1 %copy-start.5 = (f32[4,288,128]{2,1,0:T(8,128)S(1)}, f32[4,288,128]{2,1,0:T(8,128)}, u32[]{:S(2)}) copy-start(f32[4,288,128]{2,1,0:T(8,128)} %get-tuple-element.11.table_ref) | copy-start | bytes 1769476
  28.0 1.5 %copy-start.2 = (f32[13,128,384]{2,1,0:T(8,128)}, f32[13,128,384]{2,1,0:T(8,128)S(1)}, u32[]{:S(2)}) copy-start(f32[13,128,384]{2,1,0:T(8,128)S(1)} %near.1.near_ref) | copy-start | bytes 7667716
  29.4 10.7 %copy-start.1 = (bf16[896,1536]{1,0:T(8,128)(2,1)S(1)}, bf16[896,1536]{1,0:T(8,128)(2,1)}, u32[]{:S(2)}) copy-start(bf16[896,1536]{1,0:T(8,128)(2,1)} %constant.27.clone.spread_ref) | copy-start | bytes 8257540
  30.2 1.8 %copy-start.3 = (f32[13,128,384]{2,1,0:T(8,128)S(1)}, f32[13,128,384]{2,1,0:T(8,128)}, u32[]{:S(2)}) copy-start(f32[13,128,384]{2,1,0:T(8,128)} %copy-done.2) | copy-start | bytes 7667716
  34.9 7.9 %collective-permute-start.2 = (f32[24,384]{1,0:T(8,128)S(1)}, f32[24,384]{1,0:T(8,128)S(1)}, u32[]{:S(2)}, u32[]{:S(2)}) collective-permute-start(f32[24,384]{1,0:T(8,128)S(1)} %get-tuple-element.16), channel_id=1, source_target_pairs={{0,8},{16,24},{8,0},{24,16},{1,9},{17,25},{9,1},{25,17},{2,10},{18... | collective-permute-start | bytes 110600 | tf_op jit(solution)/shard_map/ppermute | solution.py:473
  35.1 7.7 %collective-permute-start.3 = (f32[24,384]{1,0:T(8,128)S(1)}, f32[24,384]{1,0:T(8,128)S(1)}, u32[]{:S(2)}, u32[]{:S(2)}) collective-permute-start(f32[24,384]{1,0:T(8,128)S(1)} %get-tuple-element.17), channel_id=1, source_target_pairs={{8,16},{16,8},{9,17},{17,9},{10,18},{18,10},{11,19},{19,11},{12,20... | collective-permute-start | bytes 110600 | tf_op jit(solution)/shard_map/ppermute | solution.py:473
  40.2 2.6 %copy-start = (f32[8,64,1500]{2,1,0:T(8,128)S(1)}, f32[8,64,1500]{2,1,0:T(8,128)}, u32[]{:S(2)}) copy-start(f32[8,64,1500]{2,1,0:T(8,128)} %tracer_ref.1) | copy-start | bytes 9216004
